TPU v7x, 256 devices: a whole 4x4x8 slice. The times are simulated.
256 devices in a mesh: size: 4 (over x_hi, core), gz: 64 (over z, y, x_lo).
Axes of the slice: x: 4 (x_hi: 2, x_lo: 2; x = x_hi * 2 + x_lo), y: 4, z: 8, core: 2. Of those that a mesh axis runs over, the one named last changes fastest.
Arguments:
- concentration: float32 [8, 256, 128, 128], P('size', 'gz'), may hold values from 0 to 2
- deposit: float32 [8, 256, 128, 128], P('size', 'gz'), may hold values from 0 to 1
- velocity: float32 [256, 128, 128], P('gz'), may hold values from 0.2 to 1
- pore_label: int32 [256, 128, 128], P('gz'), may hold values from 0 to 3
- diffusivity: float32 [8], P('size'), may hold values from 0.15 to 0.5
- attach_rate: float32 [8], P('size'), may hold values from 0.4 to 4
- volume: float32 [8], P('size'), may hold values from 0.05 to 0.3
- conc_cotangent: float32 [8, 256, 128, 128], P('size', 'gz'), may hold values from -6 to 6
- deposit_cotangent: float32 [8, 256, 128, 128], P('size', 'gz'), may hold values from -6 to 6
Outputs:
- conc_adjoint: float32 [8, 256, 128, 128], P('size', 'gz')
- deposit_adjoint: float32 [8, 256, 128, 128], P('size', 'gz')
All inputs are finite; a program needn't handle non-finite values.
Results may differ from a plain program's by a relative error of at most 0.0001.
Values sent between devices are 32-bit elements; how exact they have to be, the bound alone decides.
No kernel may reach another device: no remote copies, remote signals or barrier semaphores. Data moves between devices by JAX's collectives and lax.ppermute only.
A program may use at most 64 MiB of HBM per device.

v0:
```python
import jax
import jax.numpy as jnp
from jax import lax
from jax.sharding import PartitionSpec as P

CLOGGING = 1.0
TIME_STEP = 0.25
SURFACE_EFF = (0.1, 0.6, 1.2, 2.0)
MIXING = ((0.0, 1.0), (0.75, 0.25), (1.0 / 3.0, 2.0 / 3.0))


def with_halo(array, sides, width):
    for axis, dim in sides:
        peers, length = (lax.axis_size(axis), array.shape[dim])
        up = [(i, (i + 1) % peers) for i in range(peers - 1)]
        down = [(j, i) for i, j in up]
        last = lax.slice_in_dim(array, length - width, length, axis=dim)
        initial = lax.slice_in_dim(array, 0, width, axis=dim)
        before = lax.ppermute(last, axis, up)
        after = lax.ppermute(initial, axis, down)
        array = jnp.concatenate([before, array, after], axis=dim)
    return array


def efficiency(labels):
    result = jnp.zeros(labels.shape, jnp.float32)
    for label_value in range(4):
        result = result + SURFACE_EFF[label_value] * (labels == label_value).astype(jnp.float32)
    return result


def lateral(extended):
    middle = extended[:, 1:-1]
    padded = jnp.pad(middle, ((0, 0), (0, 0), (1, 1), (1, 1)))
    return (
        extended[:, 2:]
        + extended[:, :-2]
        + padded[:, :, 2:, 1:-1]
        + padded[:, :, :-2, 1:-1]
        + padded[:, :, 1:-1, 2:]
        + padded[:, :, 1:-1, :-2]
        - 6.0 * middle
    )


def shards(
    concentration,
    deposit,
    velocity,
    pore_label,
    diffusivity,
    attach_rate,
    volume,
    conc_cotangent,
    deposit_cotangent,
):
    classes_here = concentration.shape[0]
    coeff_dif = diffusivity[:, None, None, None]
    coeff_rate = attach_rate[:, None, None, None]
    coeff_vol = volume[:, None, None, None]
    collector = efficiency(pore_label)

    def blocking(dep_state):
        partial_sum = jnp.sum(coeff_vol * dep_state, axis=0)
        return jnp.exp(-CLOGGING * lax.psum(partial_sum, "size"))

    def forward_rates(extended, blocked, collect, flow_now):
        middle = extended[:, 1:-1]
        reaction = coeff_rate * collect * blocked * middle
        rate_conc = (
            coeff_dif * lateral(extended) - flow_now * (middle - extended[:, :-2]) - reaction
        )
        return (rate_conc, reaction)

    stacked = jnp.concatenate([concentration, velocity[None]], axis=0)
    first_ext = with_halo(stacked, (("gz", 1),), 1)
    flow_here = first_ext[classes_here, 1:-1]
    flow_above = first_ext[classes_here, 2:]
    blocked_zero = blocking(deposit)
    rate_conc, reaction = forward_rates(
        first_ext[:classes_here], blocked_zero, collector, flow_here
    )
    conc_one = concentration + TIME_STEP * rate_conc
    dep_one = deposit + TIME_STEP * reaction
    blocked_one = blocking(dep_one)
    conc_one_ext = with_halo(conc_one, (("gz", 1),), 1)
    rate_conc, reaction = forward_rates(conc_one_ext, blocked_one, collector, flow_here)
    conc_two = 0.75 * concentration + 0.25 * (conc_one + TIME_STEP * rate_conc)
    dep_two = 0.75 * deposit + 0.25 * (dep_one + TIME_STEP * reaction)
    blocked_two = blocking(dep_two)
    conc_states = (concentration, conc_one, conc_two)
    blocks = (blocked_zero, blocked_one, blocked_two)
    adj_conc = conc_cotangent
    adj_dep = deposit_cotangent
    total_conc = jnp.zeros(concentration.shape, jnp.float32)
    total_dep = jnp.zeros(deposit.shape, jnp.float32)
    for segment_index in (2, 1, 0):
        weight_old, weight_new = MIXING[segment_index]
        push_conc = weight_new * TIME_STEP * adj_conc
        push_ext = with_halo(push_conc, (("gz", 1),), 1)
        uptake = coeff_rate * collector * blocks[segment_index]
        weight = weight_new * TIME_STEP * adj_dep - push_conc
        back_conc = (
            coeff_dif * lateral(push_ext)
            - flow_here * push_conc
            + flow_above * push_ext[:, 2:]
            + uptake * weight
        )
        theta_part = -CLOGGING * jnp.sum(weight * (uptake * conc_states[segment_index]), axis=0)
        theta_grad = lax.psum(theta_part, "size")
        back_conc, back_dep = (back_conc, coeff_vol * theta_grad[None])
        total_conc = total_conc + weight_old * adj_conc
        total_dep = total_dep + weight_old * adj_dep
        adj_conc = weight_new * adj_conc + back_conc
        adj_dep = weight_new * adj_dep + back_dep
    return (total_conc + adj_conc, total_dep + adj_dep)


def solution(mesh):
    in_specs = (
        P("size", "gz", None, None),
        P("size", "gz", None, None),
        P("gz", None, None),
        P("gz", None, None),
        P("size"),
        P("size"),
        P("size"),
        P("size", "gz", None, None),
        P("size", "gz", None, None),
    )
    out_specs = (P("size", "gz", None, None), P("size", "gz", None, None))
    return jax.shard_map(shards, mesh=mesh, in_specs=in_specs, out_specs=out_specs, check_vma=False)
```

profile of v0, /device:TPU:129, one launch (start us, length us, event | category | flops | bytes accessed | tf_op | source)
XLA Modules:
  0.0 331.4 jit_solution(14072504348396859562)
XLA Ops:
  7.2 0.0 all-reduce.12.cloned.1.call-start
  7.2 1.9 multiply_reduce_fusion.4
  9.1 0.0 all-reduce.12.cloned.1.call-update
  9.2 0.0 copy-start
  9.2 0.0 copy-start.3
  9.2 0.0 all-reduce.14.cloned.1.call-start
  9.2 0.1 select_add_fusion
  9.3 49.5 %all-reduce.12.cloned.1.call-done = f32[4,128,128]{2,1,0:T(8,128)} async-done(((f32[4,128,128]{2,1,0:T(8,128)}), f32[4,128,128]{2,1,0:T(8,128)}) %all-reduce.12.cloned.1.call-update) | async-done | bytes 262160 | tf_op jit(solution)/shard_map/psum | solution.py:65
  58.9 1.0 multiply_exponential_fusion.2
  59.9 0.0 copy-start.2
  59.9 0.9 multiply_reduce_fusion.3
  60.8 0.0 all-reduce.14.cloned.1.call-update
  60.9 0.0 all-reduce.16.cloned.1.call-start
  61.0 0.0 copy-start.15
  61.0 4.3 %collective-permute-start.2 = (f32[3,1,128,128]{3,2,1,0:T(8,128)S(1)}, f32[3,1,128,128]{3,2,1,0:T(8,128)S(1)}, u32[]{:S(2)}, u32[]{:S(2)}) collective-permute-start(f32[3,1,128,128]{3,2,1,0:T(8,128)S(1)} %get-tuple-element.8), channel_id=1, source_target_pairs={{1,0},{2,1},{3,2},{4,3},{5,4},{6,5},{7,6},{8,7},{9,8},{10,9},{11,1... | collective-permute-start | bytes 589832 | tf_op jit(solution)/shard_map/ppermute | solution.py:20
  65.3 1.9 collective-permute-start.3
  67.2 41.6 %all-reduce.14.cloned.1.call-done = f32[4,128,128]{2,1,0:T(8,128)} async-done(((f32[4,128,128]{2,1,0:T(8,128)}), f32[4,128,128]{2,1,0:T(8,128)}) %all-reduce.14.cloned.1.call-update) | async-done | bytes 262160 | tf_op jit(solution)/shard_map/psum | solution.py:65
  108.8 1.0 multiply_exponential_fusion.1
  109.8 0.0 collective-permute-done.2
  109.8 0.0 collective-permute-done.3
  109.8 1.3 multiply_reduce_fusion.2
  111.1 0.0 all-reduce.16.cloned.1.call-update
  111.2 0.0 all-reduce.18.cloned.1.call-start
  111.2 0.0 copy-start.1
  111.2 0.0 copy-start.4
  111.2 0.7 fusion.77
  111.9 4.3 %collective-permute-start.6 = (f32[2,1,128,128]{3,2,1,0:T(8,128)}, f32[2,1,128,128]{3,2,1,0:T(8,128)S(1)}, u32[]{:S(2)}, u32[]{:S(2)}) collective-permute-start(f32[2,1,128,128]{3,2,1,0:T(8,128)} %get-tuple-element.18), channel_id=1, source_target_pairs={{1,0},{2,1},{3,2},{4,3},{5,4},{6,5},{7,6},{8,7},{9,8},{10,9},{11,1... | collective-permute-start | bytes 393224 | tf_op jit(solution)/shard_map/ppermute | solution.py:20
  116.2 1.9 collective-permute-start.7
  118.1 40.6 %all-reduce.16.cloned.1.call-done = f32[4,128,128]{2,1,0:T(8,128)} async-done(((f32[4,128,128]{2,1,0:T(8,128)}), f32[4,128,128]{2,1,0:T(8,128)}) %all-reduce.16.cloned.1.call-update) | async-done | bytes 262160 | tf_op jit(solution)/shard_map/psum | solution.py:65
  158.7 1.0 multiply_exponential_fusion
  159.8 0.0 collective-permute-done.6
  159.8 2.4 broadcast_multiply_fusion.2
  162.2 0.7 broadcast_multiply_fusion.7
  162.9 0.0 all-reduce.18.cloned.1.call-update
  162.9 0.0 all-reduce.20.cloned.1.call-start
  163.0 1.0 fusion.76
  164.0 4.3 %collective-permute-start = (f32[2,1,128,128]{3,2,1,0:T(8,128)S(1)}, f32[2,1,128,128]{3,2,1,0:T(8,128)S(1)}, u32[]{:S(2)}, u32[]{:S(2)}) collective-permute-start(f32[2,1,128,128]{3,2,1,0:T(8,128)S(1)} %get-tuple-element.14), channel_id=1, source_target_pairs={{1,0},{2,1},{3,2},{4,3},{5,4},{6,5},{7,6},{8,7},{9,8},{10,9},{11,1... | collective-permute-start | bytes 393224 | tf_op jit(solution)/shard_map/ppermute | solution.py:20
  168.3 2.1 collective-permute-start.1
  170.3 0.9 broadcast_multiply_fusion.3
  171.3 0.7 maximum_bitcast_fusion
  172.0 7.2 %collective-permute-done.1 = f32[2,1,128,128]{3,2,1,0:T(8,128)} collective-permute-done((f32[2,1,128,128]{3,2,1,0:T(8,128)S(1)}, f32[2,1,128,128]{3,2,1,0:T(8,128)}, u32[]{:S(2)}, u32[]{:S(2)}) %collective-permute-start.1) | collective-permute-done | bytes 131104 | tf_op jit(solution)/shard_map/ppermute | solution.py:19
  179.2 31.2 %all-reduce.18.cloned.1.call-done = f32[4,128,128]{2,1,0:T(8,128)} async-done(((f32[4,128,128]{2,1,0:T(8,128)}), f32[4,128,128]{2,1,0:T(8,128)}) %all-reduce.18.cloned.1.call-update) | async-done | bytes 262160 | tf_op jit(solution)/shard_map/psum | solution.py:110
  210.5 3.8 %multiply_reduce_fusion.1 = (f32[4,128,128]{2,1,0:T(8,128)S(1)}, f32[2,4,128,128]{3,2,1,0:T(8,128)S(1)}) fusion(f32[2,4,128,128]{3,2,1,0:T(8,128)S(1)} %copy-done.1, f32[2,4,128,128]{3,2,1,0:T(8,128)S(1)} %get-tuple-element.7, f32[4,128,128]{2,1,0:T(8,128)} %all-reduce.18.cloned.1.call-done, f32[4,128,128]{2,1,0:T(8,128)S(1)} %multiply_exponential_fusion.1, ...), kind=kLoop, calls=%fused_computation.110 | loop fusion | flops 3997696 | bytes 4718616 | tf_op jit(solution)/shard_map/reduce_sum | solution.py:109
  214.3 0.7 broadcast_multiply_fusion.6
  215.0 0.0 all-reduce.20.cloned.1.call-update
  215.0 0.0 all-reduce.22.cloned.1.call-start
  215.1 0.0 copy-start.7
  215.2 4.3 %collective-permute-start.4 = (f32[2,1,128,128]{3,2,1,0:T(8,128)S(1)}, f32[2,1,128,128]{3,2,1,0:T(8,128)S(1)}, u32[]{:S(2)}, u32[]{:S(2)}) collective-permute-start(f32[2,1,128,128]{3,2,1,0:T(8,128)S(1)} %get-tuple-element.12), channel_id=1, source_target_pairs={{1,0},{2,1},{3,2},{4,3},{5,4},{6,5},{7,6},{8,7},{9,8},{10,9},{11,1... | collective-permute-start | bytes 393224 | tf_op jit(solution)/shard_map/ppermute | solution.py:20
  219.4 1.9 collective-permute-start.5
  221.4 0.8 collective-permute-done.4
  222.2 8.1 %collective-permute-done.5 = f32[2,1,128,128]{3,2,1,0:T(8,128)} collective-permute-done((f32[2,1,128,128]{3,2,1,0:T(8,128)S(1)}, f32[2,1,128,128]{3,2,1,0:T(8,128)}, u32[]{:S(2)}, u32[]{:S(2)}) %collective-permute-start.5) | collective-permute-done | bytes 131104 | tf_op jit(solution)/shard_map/ppermute | solution.py:19
  230.3 31.2 %all-reduce.20.cloned.1.call-done = f32[4,128,128]{2,1,0:T(8,128)} async-done(((f32[4,128,128]{2,1,0:T(8,128)}), f32[4,128,128]{2,1,0:T(8,128)}) %all-reduce.20.cloned.1.call-update) | async-done | bytes 262160 | tf_op jit(solution)/shard_map/psum | solution.py:110
  261.5 3.8 %multiply_reduce_fusion = (f32[4,128,128]{2,1,0:T(8,128)S(1)}, f32[2,4,128,128]{3,2,1,0:T(8,128)S(1)}) fusion(f32[2,4,128,128]{3,2,1,0:T(8,128)S(1)} %copy-done.1, f32[2,4,128,128]{3,2,1,0:T(8,128)S(1)} %copy-done, f32[4,128,128]{2,1,0:T(8,128)} %all-reduce.20.cloned.1.call-done, f32[4,128,128]{2,1,0:T(8,128)} %all-reduce.18.cloned.1.call-done, ...), kind=kLoop, calls=%fused_computation.107 | loop fusion | flops 4521984 | bytes 4980760 | tf_op jit(solution)/shard_map/reduce_sum | solution.py:109
  265.3 0.8 broadcast_multiply_fusion.1
  266.2 1.7 fusion.74
  267.8 4.4 %collective-permute-start.8 = (f32[2,1,128,128]{3,2,1,0:T(8,128)}, f32[2,1,128,128]{3,2,1,0:T(8,128)S(1)}, u32[]{:S(2)}, u32[]{:S(2)}) collective-permute-start(f32[2,1,128,128]{3,2,1,0:T(8,128)} %get-tuple-element.10), channel_id=1, source_target_pairs={{1,0},{2,1},{3,2},{4,3},{5,4},{6,5},{7,6},{8,7},{9,8},{10,9},{11,1... | collective-permute-start | bytes 393224 | tf_op jit(solution)/shard_map/ppermute | solution.py:20
  272.2 1.9 collective-permute-start.9
  274.2 0.7 broadcast_multiply_fusion.5
  274.9 0.0 all-reduce.22.cloned.1.call-update
  274.9 0.4 collective-permute-done.8
  275.3 8.0 %collective-permute-done.9 = f32[2,1,128,128]{3,2,1,0:T(8,128)} collective-permute-done((f32[2,1,128,128]{3,2,1,0:T(8,128)}, f32[2,1,128,128]{3,2,1,0:T(8,128)}, u32[]{:S(2)}, u32[]{:S(2)}) %collective-permute-start.9) | collective-permute-done | bytes 131104 | tf_op jit(solution)/shard_map/ppermute | solution.py:19
  283.3 4.4 %fusion.14 = f32[2,4,128,128]{3,2,1,0:T(8,128)} fusion(f32[2,4,128,128]{3,2,1,0:T(8,128)S(1)} %get-tuple-element.3, f32[2,4,128,128]{3,2,1,0:T(8,128)} %broadcast_multiply_fusion.1, f32[2,1,128,128]{3,2,1,0:T(8,128)} %collective-permute-done.9, f32[2,1,128,128]{3,2,1,0:T(8,128)S(1)} %collective-permute-done.8, f32[2,4,128,128]{3,2,1,0:T(8,128)S(1)} %get-tuple-element.5, ...), kind=kLoop, calls=%fused_computation.37 | loop fusion | flops 4325376 | bytes 4980760 | tf_op jit(solution)/shard_map/add | solution.py:116
  287.7 34.8 %all-reduce.22.cloned.1.call-done = f32[4,128,128]{2,1,0:T(8,128)} async-done(((f32[4,128,128]{2,1,0:T(8,128)}), f32[4,128,128]{2,1,0:T(8,128)}) %all-reduce.22.cloned.1.call-update) | async-done | bytes 262160 | tf_op jit(solution)/shard_map/psum | solution.py:110
  322.5 2.0 add_add_fusion
  (30 shorter events, 0.1 us)
Async XLA Ops:
  7.2 2.1 copy-start.12
  7.2 51.7 %all-reduce.12.cloned.1.call-start = ((), (), s32[]{:S(2)}) async-start(), calls=%async_computation | async-start | bytes 524288 | tf_op jit(solution)/shard_map/psum | solution.py:65
  9.1 50.8 %copy-start.13 = (f32[2]{0:T(128)S(1)}, f32[2]{0:T(128)}, u32[]{:S(2)}) copy-start(f32[2]{0:T(128)} %param.15) | copy-start | bytes 28
  9.1 50.8 %copy-start.14 = (f32[2]{0:T(128)S(1)}, f32[2]{0:T(128)}, u32[]{:S(2)}) copy-start(f32[2]{0:T(128)} %param.14) | copy-start | bytes 28
  9.2 50.7 %copy-start = (f32[2,4,128,128]{3,2,1,0:T(8,128)S(1)}, f32[2,4,128,128]{3,2,1,0:T(8,128)}, u32[]{:S(2)}) copy-start(f32[2,4,128,128]{3,2,1,0:T(8,128)} %param.9) | copy-start | bytes 1572868
  9.2 50.7 %copy-start.3 = (f32[2,4,128,128]{3,2,1,0:T(8,128)S(1)}, f32[2,4,128,128]{3,2,1,0:T(8,128)}, u32[]{:S(2)}) copy-start(f32[2,4,128,128]{3,2,1,0:T(8,128)} %param.10) | copy-start | bytes 1572868
  9.2 99.6 %all-reduce.14.cloned.1.call-start = ((), (), s32[]{:S(2)}) async-start(), calls=%async_computation.1 | async-start | bytes 524288 | tf_op jit(solution)/shard_map/psum | solution.py:65
  59.9 1.0 copy-start.2
  60.9 97.9 %all-reduce.16.cloned.1.call-start = ((), (), s32[]{:S(2)}) async-start(), calls=%async_computation.2 | async-start | bytes 524288 | tf_op jit(solution)/shard_map/psum | solution.py:65
  61.0 48.8 %copy-start.15 = (f32[2]{0:T(128)S(1)}, f32[2]{0:T(128)}, u32[]{:S(2)}) copy-start(f32[2]{0:T(128)} %param.13) | copy-start | bytes 28
  61.0 48.8 %collective-permute-start.2 = (f32[3,1,128,128]{3,2,1,0:T(8,128)S(1)}, f32[3,1,128,128]{3,2,1,0:T(8,128)S(1)}, u32[]{:S(2)}, u32[]{:S(2)}) collective-permute-start(f32[3,1,128,128]{3,2,1,0:T(8,128)S(1)} %get-tuple-element.8), channel_id=1, source_target_pairs={{1,0},{2,1},{3,2},{4,3},{5,4},{6,5},{7,6},{8,7},{9,8},{10,9},{11,1... | collective-permute-start | bytes 589832 | tf_op jit(solution)/shard_map/ppermute | solution.py:20
  65.3 44.5 %collective-permute-start.3 = (f32[3,1,128,128]{3,2,1,0:T(8,128)S(1)}, f32[3,1,128,128]{3,2,1,0:T(8,128)S(1)}, u32[]{:S(2)}, u32[]{:S(2)}) collective-permute-start(f32[3,1,128,128]{3,2,1,0:T(8,128)S(1)} %get-tuple-element.9), channel_id=1, source_target_pairs={{0,1},{1,2},{2,3},{3,4},{4,5},{5,6},{6,7},{7,8},{8,9},{9,10},{10,1... | collective-permute-start | bytes 589832 | tf_op jit(solution)/shard_map/ppermute | solution.py:19
  109.8 1.4 copy-start.10
  111.2 99.3 %all-reduce.18.cloned.1.call-start = ((), (), s32[]{:S(2)}) async-start(), calls=%async_computation.3 | async-start | bytes 524288 | tf_op jit(solution)/shard_map/psum | solution.py:110
  111.2 48.6 %copy-start.1 = (f32[2,4,128,128]{3,2,1,0:T(8,128)S(1)}, f32[2,4,128,128]{3,2,1,0:T(8,128)}, u32[]{:S(2)}) copy-start(f32[2,4,128,128]{3,2,1,0:T(8,128)} %param.17) | copy-start | bytes 1572868
  111.2 48.6 %copy-start.4 = (f32[2,4,128,128]{3,2,1,0:T(8,128)S(1)}, f32[2,4,128,128]{3,2,1,0:T(8,128)}, u32[]{:S(2)}) copy-start(f32[2,4,128,128]{3,2,1,0:T(8,128)} %param.16) | copy-start | bytes 1572868
  111.9 47.8 %collective-permute-start.6 = (f32[2,1,128,128]{3,2,1,0:T(8,128)}, f32[2,1,128,128]{3,2,1,0:T(8,128)S(1)}, u32[]{:S(2)}, u32[]{:S(2)}) collective-permute-start(f32[2,1,128,128]{3,2,1,0:T(8,128)} %get-tuple-element.18), channel_id=1, source_target_pairs={{1,0},{2,1},{3,2},{4,3},{5,4},{6,5},{7,6},{8,7},{9,8},{10,9},{11,1... | collective-permute-start | bytes 393224 | tf_op jit(solution)/shard_map/ppermute | solution.py:20
  116.2 43.6 %collective-permute-start.7 = (f32[2,1,128,128]{3,2,1,0:T(8,128)}, f32[2,1,128,128]{3,2,1,0:T(8,128)}, u32[]{:S(2)}, u32[]{:S(2)}) collective-permute-start(f32[2,1,128,128]{3,2,1,0:T(8,128)} %get-tuple-element.19), channel_id=1, source_target_pairs={{0,1},{1,2},{2,3},{3,4},{4,5},{5,6},{6,7},{7,8},{8,9},{9,10},{10,1... | collective-permute-start | bytes 393224 | tf_op jit(solution)/shard_map/ppermute | solution.py:19
  159.7 2.4 copy-start.8
  162.9 98.6 %all-reduce.20.cloned.1.call-start = ((), (), s32[]{:S(2)}) async-start(), calls=%async_computation.4 | async-start | bytes 524288 | tf_op jit(solution)/shard_map/psum | solution.py:110
  164.0 8.0 %collective-permute-start = (f32[2,1,128,128]{3,2,1,0:T(8,128)S(1)}, f32[2,1,128,128]{3,2,1,0:T(8,128)S(1)}, u32[]{:S(2)}, u32[]{:S(2)}) collective-permute-start(f32[2,1,128,128]{3,2,1,0:T(8,128)S(1)} %get-tuple-element.14), channel_id=1, source_target_pairs={{1,0},{2,1},{3,2},{4,3},{5,4},{6,5},{7,6},{8,7},{9,8},{10,9},{11,1... | collective-permute-start | bytes 393224 | tf_op jit(solution)/shard_map/ppermute | solution.py:20
  168.3 3.0 copy-start.11
  168.3 11.0 %collective-permute-start.1 = (f32[2,1,128,128]{3,2,1,0:T(8,128)S(1)}, f32[2,1,128,128]{3,2,1,0:T(8,128)}, u32[]{:S(2)}, u32[]{:S(2)}) collective-permute-start(f32[2,1,128,128]{3,2,1,0:T(8,128)S(1)} %get-tuple-element.15), channel_id=1, source_target_pairs={{0,1},{1,2},{2,3},{3,4},{4,5},{5,6},{6,7},{7,8},{8,9},{9,10},{10,1... | collective-permute-start | bytes 393224 | tf_op jit(solution)/shard_map/ppermute | solution.py:19
  215.0 107.5 %all-reduce.22.cloned.1.call-start = ((), (), s32[]{:S(2)}) async-start(), calls=%async_computation.5 | async-start | bytes 524288 | tf_op jit(solution)/shard_map/psum | solution.py:110
  215.1 46.4 %copy-start.7 = (f32[2,4,128,128]{3,2,1,0:T(8,128)}, f32[2,4,128,128]{3,2,1,0:T(8,128)S(1)}, u32[]{:S(2)}) copy-start(f32[2,4,128,128]{3,2,1,0:T(8,128)S(1)} %broadcast_multiply_fusion) | copy-start | bytes 1572868
  215.2 7.0 %collective-permute-start.4 = (f32[2,1,128,128]{3,2,1,0:T(8,128)S(1)}, f32[2,1,128,128]{3,2,1,0:T(8,128)S(1)}, u32[]{:S(2)}, u32[]{:S(2)}) collective-permute-start(f32[2,1,128,128]{3,2,1,0:T(8,128)S(1)} %get-tuple-element.12), channel_id=1, source_target_pairs={{1,0},{2,1},{3,2},{4,3},{5,4},{6,5},{7,6},{8,7},{9,8},{10,9},{11,1... | collective-permute-start | bytes 393224 | tf_op jit(solution)/shard_map/ppermute | solution.py:20
  219.4 10.8 %collective-permute-start.5 = (f32[2,1,128,128]{3,2,1,0:T(8,128)S(1)}, f32[2,1,128,128]{3,2,1,0:T(8,128)}, u32[]{:S(2)}, u32[]{:S(2)}) collective-permute-start(f32[2,1,128,128]{3,2,1,0:T(8,128)S(1)} %get-tuple-element.13), channel_id=1, source_target_pairs={{0,1},{1,2},{2,3},{3,4},{4,5},{5,6},{6,7},{7,8},{8,9},{9,10},{10,1... | collective-permute-start | bytes 393224 | tf_op jit(solution)/shard_map/ppermute | solution.py:19
  267.8 15.5 %copy-start.5 = (f32[4,128,128]{2,1,0:T(8,128)S(1)}, f32[4,128,128]{2,1,0:T(8,128)}, u32[]{:S(2)}) copy-start(f32[4,128,128]{2,1,0:T(8,128)} %maximum_bitcast_fusion) | copy-start | bytes 786436
  267.8 15.5 %copy-start.6 = (f32[4,128,128]{2,1,0:T(8,128)S(1)}, f32[4,128,128]{2,1,0:T(8,128)}, u32[]{:S(2)}) copy-start(f32[4,128,128]{2,1,0:T(8,128)} %all-reduce.18.cloned.1.call-done) | copy-start | bytes 786436
  267.8 15.5 %copy-start.9 = (f32[4,128,128]{2,1,0:T(8,128)S(1)}, f32[4,128,128]{2,1,0:T(8,128)}, u32[]{:S(2)}) copy-start(f32[4,128,128]{2,1,0:T(8,128)} %all-reduce.20.cloned.1.call-done) | copy-start | bytes 786436
  267.8 7.4 %collective-permute-start.8 = (f32[2,1,128,128]{3,2,1,0:T(8,128)}, f32[2,1,128,128]{3,2,1,0:T(8,128)S(1)}, u32[]{:S(2)}, u32[]{:S(2)}) collective-permute-start(f32[2,1,128,128]{3,2,1,0:T(8,128)} %get-tuple-element.10), channel_id=1, source_target_pairs={{1,0},{2,1},{3,2},{4,3},{5,4},{6,5},{7,6},{8,7},{9,8},{10,9},{11,1... | collective-permute-start | bytes 393224 | tf_op jit(solution)/shard_map/ppermute | solution.py:20
  272.2 11.0 %collective-permute-start.9 = (f32[2,1,128,128]{3,2,1,0:T(8,128)}, f32[2,1,128,128]{3,2,1,0:T(8,128)}, u32[]{:S(2)}, u32[]{:S(2)}) collective-permute-start(f32[2,1,128,128]{3,2,1,0:T(8,128)} %get-tuple-element.11), channel_id=1, source_target_pairs={{0,1},{1,2},{2,3},{3,4},{4,5},{5,6},{6,7},{7,8},{8,9},{9,10},{10,1... | collective-permute-start | bytes 393224 | tf_op jit(solution)/shard_map/ppermute | solution.py:19
Sparse Core Ops, SparseCore 0:
  11.2 47.6 all-reduce.11
  62.3 46.4 all-reduce.13
  112.0 46.7 all-reduce.15
  163.0 47.3 all-reduce.17
  215.1 46.3 all-reduce.19
  275.0 47.4 all-reduce.21
where the time goes:
time: 334 us; the launch traced here: 331 us
  waiting for transfers between devices  254 us (76%)
  starting transfers between devices  31.5 us (9%)
  other arithmetic  28.3 us (8%)
  between operations  14.4 us (4%)
  local copies, waits for them, and re-layouts  3.47 us (1%)
    psum x3, waiting for transfers between devices, blocking(): return jnp.exp(-CLOGGING * lax.psum(partial_sum, 'size'))  132 us
    psum x3, waiting for transfers between devices, shards(): theta_grad = lax.psum(theta_part, 'size')  97.3 us
    ppermute x5, waiting for transfers between devices, with_halo(): before = lax.ppermute(last, axis, up)  23.4 us
    ppermute x5, starting transfers between devices, with_halo(): after = lax.ppermute(initial, axis, down)  21.5 us
    ppermute x5, starting transfers between devices, with_halo(): before = lax.ppermute(last, axis, up)  9.74 us
    reduce_sum x2, other arithmetic, shards(): jnp.sum(weight * (uptake * conc_states[segment_index]), axis=0)  7.57 us
  transfers between devices with their start and end apart: 16, of which 11 were waited for; matrix products, arithmetic and copies ran while one was open for 3% of the time, Pallas kernels for 0%

commit v1 on v0

v1 whole, which is shorter than its diff:
```python
import functools

import jax
import jax.numpy as jnp
from jax import lax
from jax.experimental import pallas as pl
from jax.experimental.pallas import tpu as pltpu
from jax.sharding import PartitionSpec as P

H = 0.25
SURFACE_EFF = (0.1, 0.6, 1.2, 2.0)
N = 128
F32 = jnp.float32


def lateral(x):
    row = lax.broadcasted_iota(jnp.int32, x.shape, 0)
    col = lax.broadcasted_iota(jnp.int32, x.shape, 1)
    up = jnp.where(row > 0, pltpu.roll(x, 1, 0), 0.0)
    down = jnp.where(row < N - 1, pltpu.roll(x, N - 1, 0), 0.0)
    left = jnp.where(col > 0, pltpu.roll(x, 1, 1), 0.0)
    right = jnp.where(col < N - 1, pltpu.roll(x, N - 1, 1), 0.0)
    return (up + down) + (left + right) - 6.0 * x


def efficiency(label):
    out = jnp.zeros(label.shape, F32)
    for k in range(4):
        out = jnp.where(label == k, SURFACE_EFF[k], out)
    return out


class Coef:
    def __init__(self, ref):
        self.dif = [ref[c : c + 1, :] for c in range(4)]
        self.rate = [ref[4 + c : 5 + c, :] for c in range(4)]
        self.vol = [ref[8 + c : 9 + c, :] for c in range(4)]


def send_state(core_ref, dif, rate, vol, dep, conc, msg):
    other = 1 - core_ref[0]
    for l in range(2):
        msg[l] = vol[0] * dep[0, 2 * other + l] + vol[1] * dep[1, 2 * other + l]
    for c in range(2):
        for l in range(2):
            msg[2 + 3 * c + l] = conc[c, 2 * other + l]
        msg[4 + 3 * c] = conc[c, 2 - other]
    for k, ref in enumerate((dif, rate, vol)):
        for c in range(2):
            msg[8, 2 * k + c : 2 * k + c + 1, :] = jnp.full((1, N), ref[c], F32)


def send_cot(core_ref, p, q, msg):
    other = 1 - core_ref[0]
    for c in range(2):
        for l in range(2):
            msg[3 * c + l] = p[c, 2 * other + l]
            msg[6 + 2 * c + l] = q[c, 2 * other + l]
        msg[3 * c + 2] = p[c, 2 - other]


def sums_zero(core_ref, dif, rate, vol, dep, conc, got, pk1, ho, c0, coef, u4, uin):
    core = core_ref[0]
    for k, ref in enumerate((dif, rate, vol)):
        for c in range(2):
            coef[4 * k + c : 4 * k + c + 1, :] = jnp.full((1, N), ref[c], F32)
            coef[4 * k + 2 + c : 4 * k + 3 + c, :] = got[8, 2 * k + c : 2 * k + c + 1, :]
    co = Coef(coef)
    for l in range(2):
        pk1[l] = got[l] + vol[0] * dep[0, 2 * core + l] + vol[1] * dep[1, 2 * core + l]
        total = jnp.zeros((N, N), F32)
        square = jnp.zeros((N, N), F32)
        for c in range(4):
            u = conc[c, 2 * core + l] if c < 2 else got[2 + 3 * (c - 2) + l]
            u4[c, l] = u
            term = (co.vol[c] * co.rate[c]) * u
            total = total + term
            square = square + co.rate[c] * term
        pk1[2 + l] = total
        c0[l] = square
    for c in range(4):
        uin[c] = conc[c, 2 - core] if c < 2 else got[4 + 3 * (c - 2)]
        ho[(c + 2) % 4] = u4[c, core]


def advect(co, u4, vel, core, c, l):
    u = u4[c, l]
    out = co.dif[c] * lateral(u) - vel[2 * core + l] * u
    if l == 0:
        return out + co.dif[c] * u4[c, 1]
    return out + (co.dif[c] + vel[2 * core + 1]) * u4[c, 0]


def back(co, x4, vel, core, c, l):
    x = x4[c, l]
    out = co.dif[c] * lateral(x) - vel[2 * core + l] * x
    if l == 0:
        return out + (co.dif[c] + vel[2 * core + 1]) * x4[c, 1]
    return out + co.dif[c] * x4[c, 0]


def facing(co, vel, core):
    low = vel[2 * core]
    out_part = jnp.where(core == 0, low, 0.0)
    in_part = jnp.where(core == 1, low, 0.0)
    return (
        [co.dif[c] + out_part for c in range(4)],
        [co.dif[c] + in_part for c in range(4)],
    )


def step_base(core_ref, coef, u4, uin, vel, a4):
    core = core_ref[0]
    co = Coef(coef)
    _, fin = facing(co, vel, core)
    for c in range(4):
        for l in range(2):
            a4[c, l] = u4[c, l] + H * advect(co, u4, vel, core, c, l)
        a4[c, 1 - core] = a4[c, 1 - core] + H * (fin[c] * uin[c])


def cot_base(core_ref, coef, p, q, got, vel, p4, q4, base, ho):
    core = core_ref[0]
    co = Coef(coef)
    fout, _ = facing(co, vel, core)
    inner = 2 - core
    above = jnp.where(core == 0, vel[inner], 0.0)
    for c in range(4):
        for l in range(2):
            p4[c, l] = p[c, 2 * core + l] if c < 2 else got[3 * (c - 2) + l]
            q4[c, l] = q[c, 2 * core + l] if c < 2 else got[6 + 2 * (c - 2) + l]
        for l in range(2):
            base[c, l] = back(co, p4, vel, core, c, l)
        pin = p[c, inner] if c < 2 else got[3 * (c - 2) + 2]
        base[c, 1 - core] = base[c, 1 - core] + (co.dif[c] + above) * pin
        ho[(c + 2) % 4] = fout[c] * p4[c, core]


def sums_one(core_ref, coef, base, hout, vel, c0, a4, pk2):
    core = core_ref[0]
    co = Coef(coef)
    fout, _ = facing(co, vel, core)
    for l in range(2):
        for c in range(4):
            a4[c, l] = base[c, l]
    for c in range(4):
        a4[c, core] = a4[c, core] + H * (fout[c] * hout[c])
    for l in range(2):
        total = jnp.zeros((N, N), F32)
        for c in range(4):
            total = total + (co.vol[c] * co.rate[c]) * a4[c, l]
        pk2[l] = total
        pk2[2 + l] = c0[l]


def state_one(core_ref, coef, pk1, got, label, a4, u4, u1, ho, hi, k01, th, asum):
    core = core_ref[0]
    co = Coef(coef)
    for l in range(2):
        coll = efficiency(label[2 * core + l])
        theta = pk1[l] + got[l]
        a0 = pk1[2 + l] + got[2 + l]
        k0 = coll * jnp.exp(-theta)
        theta1 = theta + H * (k0 * a0)
        k01[l] = k0
        k01[2 + l] = coll * jnp.exp(-theta1)
        k01[4 + l] = coll
        th[l] = theta
        th[2 + l] = theta1
        asum[l] = a0
        for c in range(4):
            u1[c, l] = a4[c, l] - (H * k0) * (co.rate[c] * u4[c, l])
    for c in range(4):
        ho[(c + 2) % 4] = u1[c, core]
        hi[(c + 2) % 4] = u1[c, 1 - core]


def cot_two(core_ref, coef, pk2, got, k01, th, p4, q4, base, hout, vel, u1, l2, ho, hi, s1, kk, asum):
    core = core_ref[0]
    co = Coef(coef)
    fout, fin = facing(co, vel, core)
    for l in range(2):
        g0 = pk2[l] + got[l]
        c0 = pk2[2 + l] + got[2 + l]
        a1 = g0 - (H * k01[l]) * c0
        theta2 = 0.75 * th[l] + 0.25 * (th[2 + l] + H * (k01[2 + l] * a1))
        k2 = k01[4 + l] * jnp.exp(-theta2)
        asum[l] = a1
        asum[2 + l] = c0
        kk[l] = k2
        for c in range(4):
            p = p4[c, l]
            l2[c, l] = (2.0 / 3.0) * p + (2.0 / 3.0 * H) * (
                base[c, l] + (co.rate[c] * k2) * (q4[c, l] - p)
            )
    for c in range(4):
        l2[c, core] = l2[c, core] + (2.0 / 3.0 * H) * hout[c]
        ho[(c + 2) % 4] = fout[c] * l2[c, core]
        hi[(c + 2) % 4] = fin[c] * l2[c, 1 - core]
    for l in range(2):
        total = jnp.zeros((N, N), F32)
        for c in range(4):
            total = total + ((2.0 / 3.0) * q4[c, l] - l2[c, l]) * (co.rate[c] * u1[c, l])
        s1[l] = total


def sums_two(core_ref, coef, u4, u1, hout, hin, k01, vel, p4, q4, s1, pk3, tmp):
    core = core_ref[0]
    co = Coef(coef)
    fout, fin = facing(co, vel, core)
    for c in range(4):
        for l in range(2):
            tmp[c, l] = advect(co, u1, vel, core, c, l)
        tmp[c, core] = tmp[c, core] + fout[c] * hout[c]
        tmp[c, 1 - core] = tmp[c, 1 - core] + fin[c] * hin[c]
    for l in range(2):
        total = jnp.zeros((N, N), F32)
        for c in range(4):
            u = u1[c, l]
            rate = tmp[c, l] - (co.rate[c] * k01[2 + l]) * u
            u2 = 0.75 * u4[c, l] + 0.25 * (u + H * rate)
            total = total + (q4[c, l] - p4[c, l]) * (co.rate[c] * u2)
        pk3[l] = total
        pk3[2 + l] = s1[l]


def sums_three(core_ref, coef, l2, hout, hin, k01, vel, q4, u4, l1, s0):
    core = core_ref[0]
    co = Coef(coef)
    for c in range(4):
        for l in range(2):
            l1[c, l] = back(co, l2, vel, core, c, l)
        l1[c, core] = l1[c, core] + hout[c]
        l1[c, 1 - core] = l1[c, 1 - core] + hin[c]
    for l in range(2):
        total = jnp.zeros((N, N), F32)
        for c in range(4):
            x = l2[c, l]
            w = (2.0 / 3.0) * q4[c, l] - x
            y = 0.25 * x + (0.25 * H) * (l1[c, l] + (co.rate[c] * k01[2 + l]) * w)
            l1[c, l] = y
            total = total + (q4[c, l] * (1.0 / 6.0) - y) * (co.rate[c] * u4[c, l])
        s0[l] = total


def cot_one(core_ref, coef, pk3, got, k01, kk, asum, l1k, vel, l1, ho, hi, tt):
    core = core_ref[0]
    co = Coef(coef)
    fout, fin = facing(co, vel, core)
    for l in range(2):
        t2 = (-2.0 / 3.0 * H) * kk[l] * (pk3[l] + got[l])
        s1 = pk3[2 + l] + got[2 + l]
        t1 = (-0.25 * H) * k01[2 + l] * (s1 + t2 * asum[l])
        tt[l] = t2
        tt[2 + l] = t1
        push = (0.25 * H) * (k01[2 + l] * t2)
        for c in range(4):
            l1[c, l] = l1k[c, l] + (co.rate[c] * co.vol[c]) * push
    for c in range(4):
        ho[(c + 2) % 4] = fout[c] * l1[c, core]
        hi[(c + 2) % 4] = fin[c] * l1[c, 1 - core]


def total_push(core_ref, s0, got, k01, tt, a0, asum, tsum):
    for l in range(2):
        t2 = tt[l]
        t1 = tt[2 + l]
        s = s0[l] + got[l]
        mixed = s + (0.25 * t2 + t1) * a0[l] - (0.25 * H) * (k01[2 + l] * t2) * asum[2 + l]
        tsum[l] = t2 + t1 - H * (k01[l] * mixed)


def finish(core_ref, coef, p4, q4, l2, l1, hout, hin, k01, tt, vel, own, other):
    core = core_ref[0]
    co = Coef(coef)
    for c in range(4):
        dst = own if c < 2 else other
        for l in range(2):
            x = l1[c, l]
            l1s = q4[c, l] * (1.0 / 6.0) + co.vol[c] * (0.25 * tt[l] + tt[2 + l])
            rest = back(co, l1, vel, core, c, l) + (co.rate[c] * k01[l]) * (l1s - x)
            dst[c % 2, l] = (1.0 / 3.0) * p4[c, l] + 0.75 * l2[c, l] + x + H * rest
        dst[c % 2, core] = dst[c % 2, core] + H * hout[c]
        dst[c % 2, 1 - core] = dst[c % 2, 1 - core] + H * hin[c]


def assemble(core_ref, vol, own, other, tsum, tother, q, conc, dep):
    core = core_ref[0]
    for l in range(2):
        mine = 2 * core + l
        theirs = 2 * (1 - core) + l
        for c in range(2):
            conc[c, mine] = own[c, l]
            conc[c, theirs] = other[c, l]
            dep[c, mine] = q[c, mine] + vol[c] * tsum[l]
            dep[c, theirs] = q[c, theirs] + vol[c] * tother[l]


def call(body, outs, scalars, arrays, scratch=()):
    smem = pl.BlockSpec(memory_space=pltpu.SMEM)
    vmem = pl.BlockSpec(memory_space=pltpu.VMEM)
    size = sum(4 * a.size for a in arrays)
    return pl.pallas_call(
        body,
        out_shape=[jax.ShapeDtypeStruct(s, F32) for s in outs],
        in_specs=[smem] * len(scalars) + [vmem] * len(arrays),
        out_specs=[vmem] * len(outs),
        scratch_shapes=[pltpu.VMEM(s, F32) for s in scratch],
        compiler_params=pltpu.CompilerParams(vmem_limit_bytes=16 * 1024 * 1024),
        cost_estimate=pl.CostEstimate(flops=4 * size, bytes_accessed=size, transcendentals=0),
        name=body.__name__,
    )(*scalars, *arrays)


def shards(peers, conc, dep, velocity, label, dif, rate, vol, p, q):
    core = (lax.axis_index("size") % 2).astype(jnp.int32)[None]
    swap = [(0, 1), (1, 0), (2, 3), (3, 2)]
    far = [(0, 2), (2, 0), (1, 3), (3, 1)]
    face = []
    for g in range(peers - 1):
        for chip in (0, 2):
            a, b = (chip + 1) * peers + g, chip * peers + g + 1
            face += [(a, b), (b, a)]
    inner = lambda x: lax.ppermute(x, "size", swap)
    across = lambda x: lax.ppermute(x, "size", far)
    outer = lambda x: lax.ppermute(x, ("size", "gz"), face)
    field, four, pair, eight = (2, N, N), (4, N, N), (2, 2, N, N), (4, 2, N, N)

    (msg0,) = call(send_state, [(9, N, N)], (core, dif, rate, vol), (dep, conc))
    got0 = inner(msg0)
    (msg1,) = call(send_cot, [(10, N, N)], (core,), (p, q))
    got1 = inner(msg1)
    pk1, ho, c0, coef, u4, uin = call(
        sums_zero, [four, four, field, (16, N), eight, four], (core, dif, rate, vol), (dep, conc, got0)
    )
    gpk1 = across(pk1)
    hu0 = outer(ho)
    (abase,) = call(step_base, [eight], (core,), (coef, u4, uin, velocity))
    p4, q4, pbase, hop = call(
        cot_base, [eight, eight, eight, four], (core,), (coef, p, q, got1, velocity)
    )
    hp = outer(hop)
    a4, pk2 = call(sums_one, [eight, four], (core,), (coef, abase, hu0, velocity, c0))
    gpk2 = across(pk2)
    u1, ho1, hi1, k01, th, a0 = call(
        state_one,
        [eight, four, four, (6, N, N), four, field],
        (core,),
        (coef, pk1, gpk1, label, a4, u4),
    )
    hu1, iu1 = outer(ho1), inner(hi1)
    l2, ho2, hi2, s1, kk, asum = call(
        cot_two,
        [eight, four, four, field, field, four],
        (core,),
        (coef, pk2, gpk2, k01, th, p4, q4, pbase, hp, velocity, u1),
    )
    hl2, il2 = outer(ho2), inner(hi2)
    (pk3,) = call(
        sums_two,
        [four],
        (core,),
        (coef, u4, u1, hu1, iu1, k01, velocity, p4, q4, s1),
        scratch=[eight],
    )
    gpk3 = across(pk3)
    l1k, s0 = call(
        sums_three, [eight, field], (core,), (coef, l2, hl2, il2, k01, velocity, q4, u4)
    )
    gs0 = across(s0)
    l1, ho3, hi3, tt = call(
        cot_one, [eight, four, four, four], (core,), (coef, pk3, gpk3, k01, kk, asum, l1k, velocity)
    )
    hl1, il1 = outer(ho3), inner(hi3)
    (tsum,) = call(total_push, [field], (core,), (s0, gs0, k01, tt, a0, asum))
    tother = inner(tsum)
    own, other = call(
        finish, [pair, pair], (core,), (coef, p4, q4, l2, l1, hl1, il1, k01, tt, velocity)
    )
    theirs = inner(other)
    return tuple(
        call(assemble, [(2, 4, N, N), (2, 4, N, N)], (core, vol), (own, theirs, tsum, tother, q))
    )


def solution(mesh):
    state = P("size", "gz", None, None)
    flow = P("gz", None, None)
    in_specs = (state, state, flow, flow, P("size"), P("size"), P("size"), state, state)
    body = functools.partial(shards, mesh.shape["gz"])
    return jax.shard_map(
        body, mesh=mesh, in_specs=in_specs, out_specs=(state, state), check_vma=False
    )
```

time: 334 us -> 73.2 us (0.22)
  waiting for transfers between devices: 254 us -> 32.3 us
  other arithmetic: 28.3 us -> 0 us
  between operations: 14.4 us -> 0.85 us
  Pallas kernels: 0 us -> 7.05 us
    psum x6 -> x0, waiting for transfers between devices: 229 us -> none  [the longest x3 132 us: blocking(): return jnp.exp(-CLOGGING * lax.psum(partial_sum, 'size'))]
    reduce_sum x5 -> x0, other arithmetic: 11.7 us -> none  [the longest x2 7.57 us: shards(): jnp.sum(weight * (uptake * conc_states[segment_index]), axis=0)]
    ppermute x10 -> x16, waiting for transfers between devices: 24.5 us -> 32.3 us  [the longest x4 20.4 us: shards(): across = lambda x: lax.ppermute(x, 'size', far)]
    mul x8 -> x0, other arithmetic: 7.07 us -> none  [the longest x3 3.25 us: shards(): push_conc = weight_new * TIME_STEP * adj_conc]
    pallas_call x0 -> x14, Pallas kernels: none -> 7.05 us  [call(): pl.pallas_call(body, out_shape=[jax.ShapeDtypeStruct(s, F32) for s in out...]
    add x3 -> x0, other arithmetic: 6.55 us -> none  [the longest x2 6.45 us: shards(): return (total_conc + adj_conc, total_dep + adj_dep)]
    slice x4 -> x0, local copies, waits for them, and re-layouts: 3.39 us -> none  [with_halo(): initial = lax.slice_in_dim(array, 0, width, axis=dim)]
    ppermute x10 -> x16, starting transfers between devices: 31.3 us -> 29.9 us  [the longest x5 12.7 us: shards(): outer = lambda x: lax.ppermute(x, ('size', 'gz'), face)]
  transfers between devices with their start and end apart: 16 -> 16, of which waited for: 11 -> 9; matrix products, arithmetic and copies ran while one was open for 3% -> 0% of each run, Pallas kernels for 0% -> 6%
where the time goes in v1:
time: 73.2 us; the launch traced here: 72.9 us
  waiting for transfers between devices  32.3 us (44%)
  starting transfers between devices  29.9 us (41%)
  Pallas kernels  7.05 us (10%)
  local copies, waits for them, and re-layouts  2.77 us (4%)
  between operations  0.85 us (1%)
    ppermute x4, waiting for transfers between devices, shards(): across = lambda x: lax.ppermute(x, 'size', far)  20.4 us
    ppermute x5, starting transfers between devices, shards(): outer = lambda x: lax.ppermute(x, ('size', 'gz'), face)  12.7 us
    ppermute x4, starting transfers between devices, shards(): across = lambda x: lax.ppermute(x, 'size', far)  10.5 us
    ppermute x5, waiting for transfers between devices, shards(): outer = lambda x: lax.ppermute(x, ('size', 'gz'), face)  9.59 us
    pallas_call x14, Pallas kernels, call(): pl.pallas_call(body, out_shape=[jax.ShapeDtypeStruct(s, F32) for s in out...  7.05 us
    ppermute x7, starting transfers between devices, shards(): inner = lambda x: lax.ppermute(x, 'size', swap)  6.72 us
    unnamed x20, local copies, waits for them, and re-layouts  2.77 us
    ppermute x7, waiting for transfers between devices, shards(): inner = lambda x: lax.ppermute(x, 'size', swap)  2.34 us
  transfers between devices with their start and end apart: 16, of which 9 were waited for; matrix products, arithmetic and copies ran while one was open for 0% of the time, Pallas kernels for 6%

profile of v1, /device:TPU:129, one launch (start us, length us, event | category | flops | bytes accessed | tf_op | source)
XLA Modules:
  0.0 72.9 jit_solution(609950805889234711)
XLA Ops:
  0.6 0.0 copy-start.7
  0.7 0.0 copy-start.8
  0.7 0.0 copy-start.9
  0.7 0.6 copy-done.7
  1.3 0.0 copy-done.8
  1.3 0.0 copy-done.9
  1.3 0.0 copy-start.3
  1.3 1.0 %copy-done.3 = f32[2,4,128,128]{3,2,1,0:T(8,128)S(1)} copy-done((f32[2,4,128,128]{3,2,1,0:T(8,128)S(1)}, f32[2,4,128,128]{3,2,1,0:T(8,128)}, u32[]{:S(2)}) %copy-start.3) | copy-done | bytes 524312
  2.4 0.0 copy-start.4
  2.4 1.0 %copy-done.4 = f32[2,4,128,128]{3,2,1,0:T(8,128)S(1)} copy-done((f32[2,4,128,128]{3,2,1,0:T(8,128)S(1)}, f32[2,4,128,128]{3,2,1,0:T(8,128)}, u32[]{:S(2)}) %copy-start.4) | copy-done | bytes 524312
  3.4 0.0 copy-start.1
  3.4 0.0 copy-start.2
  3.4 0.6 send_state.1
  4.0 0.0 copy-start.5
  4.0 0.8 %collective-permute-start = (f32[9,128,128]{2,1,0:T(8,128)S(1)}, f32[9,128,128]{2,1,0:T(8,128)S(1)}, u32[]{:S(2)}, u32[]{:S(2)}) collective-permute-start(f32[9,128,128]{2,1,0:T(8,128)S(1)} %send_state.1), channel_id=1, source_target_pairs={{0,64},{64,0},{128,192},{192,128},{1,65},{65,1},{129,193},{193,129... | collective-permute-start | bytes 1769480 | tf_op jit(solution)/shard_map/ppermute | solution.py:324
  4.8 0.0 copy-done.1
  4.8 0.0 copy-done.2
  4.9 0.0 copy-start
  4.9 0.6 collective-permute-start.1
  5.4 1.0 %collective-permute-done.got = f32[9,128,128]{2,1,0:T(8,128)S(1)} collective-permute-done((f32[9,128,128]{2,1,0:T(8,128)S(1)}, f32[9,128,128]{2,1,0:T(8,128)S(1)}, u32[]{:S(2)}, u32[]{:S(2)}) %collective-permute-start) | collective-permute-done | bytes 589856 | tf_op jit(solution)/shard_map/ppermute | solution.py:324
  6.4 0.0 copy-done.5
  6.4 0.7 sums_zero.1
  7.1 3.4 %collective-permute-start.2 = (f32[4,128,128]{2,1,0:T(8,128)S(1)}, f32[4,128,128]{2,1,0:T(8,128)S(1)}, u32[]{:S(2)}, u32[]{:S(2)}) collective-permute-start(f32[4,128,128]{2,1,0:T(8,128)S(1)} %get-tuple-element.39), channel_id=1, source_target_pairs={{64,1},{1,64},{192,129},{129,192},{65,2},{2,65},{193,130},{130,193... | collective-permute-start | bytes 786440 | tf_op jit(solution)/shard_map/ppermute | solution.py:326
  10.5 2.5 %collective-permute-start.4 = (f32[4,128,128]{2,1,0:T(8,128)S(1)}, f32[4,128,128]{2,1,0:T(8,128)S(1)}, u32[]{:S(2)}, u32[]{:S(2)}) collective-permute-start(f32[4,128,128]{2,1,0:T(8,128)S(1)} %get-tuple-element.42.pk1), channel_id=1, source_target_pairs={{0,128},{128,0},{64,192},{192,64},{1,129},{129,1},{65,193},{193,65... | collective-permute-start | bytes 786440 | tf_op jit(solution)/shard_map/ppermute | solution.py:325
  13.1 0.0 copy-done
  13.1 0.4 step_base.1.base
  13.5 0.0 collective-permute-done.1.got
  13.5 0.5 cot_base.1
  14.0 2.2 %collective-permute-start.5 = (f32[4,128,128]{2,1,0:T(8,128)S(1)}, f32[4,128,128]{2,1,0:T(8,128)S(1)}, u32[]{:S(2)}, u32[]{:S(2)}) collective-permute-start(f32[4,128,128]{2,1,0:T(8,128)S(1)} %get-tuple-element.47), channel_id=1, source_target_pairs={{64,1},{1,64},{192,129},{129,192},{65,2},{2,65},{193,130},{130,193... | collective-permute-start | bytes 786440 | tf_op jit(solution)/shard_map/ppermute | solution.py:326
  16.2 1.1 %collective-permute-done.2.hout = f32[4,128,128]{2,1,0:T(8,128)S(1)} collective-permute-done((f32[4,128,128]{2,1,0:T(8,128)S(1)}, f32[4,128,128]{2,1,0:T(8,128)S(1)}, u32[]{:S(2)}, u32[]{:S(2)}) %collective-permute-start.2) | collective-permute-done | bytes 262176 | tf_op jit(solution)/shard_map/ppermute | solution.py:326
  17.3 0.1 sums_one.1
  17.4 2.8 %collective-permute-start.3 = (f32[4,128,128]{2,1,0:T(8,128)S(1)}, f32[4,128,128]{2,1,0:T(8,128)S(1)}, u32[]{:S(2)}, u32[]{:S(2)}) collective-permute-start(f32[4,128,128]{2,1,0:T(8,128)S(1)} %get-tuple-element.41.pk2), channel_id=1, source_target_pairs={{0,128},{128,0},{64,192},{192,64},{1,129},{129,1},{65,193},{193,65... | collective-permute-start | bytes 786440 | tf_op jit(solution)/shard_map/ppermute | solution.py:325
  20.2 7.5 %collective-permute-done.4.got = f32[4,128,128]{2,1,0:T(8,128)S(1)} collective-permute-done((f32[4,128,128]{2,1,0:T(8,128)S(1)}, f32[4,128,128]{2,1,0:T(8,128)S(1)}, u32[]{:S(2)}, u32[]{:S(2)}) %collective-permute-start.4) | collective-permute-done | bytes 262176 | tf_op jit(solution)/shard_map/ppermute | solution.py:325
  27.8 0.0 copy-done.6
  27.8 0.2 state_one.1
  28.0 1.9 %collective-permute-start.6 = (f32[4,128,128]{2,1,0:T(8,128)S(1)}, f32[4,128,128]{2,1,0:T(8,128)S(1)}, u32[]{:S(2)}, u32[]{:S(2)}) collective-permute-start(f32[4,128,128]{2,1,0:T(8,128)S(1)} %get-tuple-element.50), channel_id=1, source_target_pairs={{64,1},{1,64},{192,129},{129,192},{65,2},{2,65},{193,130},{130,193... | collective-permute-start | bytes 786440 | tf_op jit(solution)/shard_map/ppermute | solution.py:326
  29.9 1.4 %collective-permute-start.7 = (f32[4,128,128]{2,1,0:T(8,128)S(1)}, f32[4,128,128]{2,1,0:T(8,128)S(1)}, u32[]{:S(2)}, u32[]{:S(2)}) collective-permute-start(f32[4,128,128]{2,1,0:T(8,128)S(1)} %get-tuple-element.51), channel_id=1, source_target_pairs={{0,64},{64,0},{128,192},{192,128},{1,65},{65,1},{129,193},{193,129... | collective-permute-start | bytes 786440 | tf_op jit(solution)/shard_map/ppermute | solution.py:324
  31.4 0.0 collective-permute-done.5.hout
  31.4 8.1 %collective-permute-done.3.got = f32[4,128,128]{2,1,0:T(8,128)S(1)} collective-permute-done((f32[4,128,128]{2,1,0:T(8,128)S(1)}, f32[4,128,128]{2,1,0:T(8,128)S(1)}, u32[]{:S(2)}, u32[]{:S(2)}) %collective-permute-start.3) | collective-permute-done | bytes 262176 | tf_op jit(solution)/shard_map/ppermute | solution.py:325
  39.5 0.4 cot_two.1
  39.9 1.9 %collective-permute-start.9 = (f32[4,128,128]{2,1,0:T(8,128)S(1)}, f32[4,128,128]{2,1,0:T(8,128)S(1)}, u32[]{:S(2)}, u32[]{:S(2)}) collective-permute-start(f32[4,128,128]{2,1,0:T(8,128)S(1)} %get-tuple-element.55), channel_id=1, source_target_pairs={{64,1},{1,64},{192,129},{129,192},{65,2},{2,65},{193,130},{130,193... | collective-permute-start | bytes 786440 | tf_op jit(solution)/shard_map/ppermute | solution.py:326
  41.9 0.1 collective-permute-start.10
  42.0 0.0 collective-permute-done.6.hout
  42.0 0.0 collective-permute-done.7.hin
  42.0 0.8 %sums_two.1.pk3 = f32[4,128,128]{2,1,0:T(8,128)S(1)} custom-call(s32[1]{0:T(128)} %bitcast.core_ref, f32[16,128]{1,0:T(8,128)S(1)} %get-tuple-element.34.coef, f32[4,2,128,128]{3,2,1,0:T(8,128)S(1)} %get-tuple-element.37.u4, f32[4,2,128,128]{3,2,1,0:T(8,128)S(1)} %get-tuple-element.48.u1, f32[4,128,128]{2,1,0:T(8,128)S(1)} %collective-permute-done.6.hout, ...), custom_call_target="tpu_custom_call" | custom-call | flops 13664256 | bytes 3416064 | tf_op jit(solution)/shard_map/sums_two/pallas_call | solution.py:303
  42.7 2.5 %collective-permute-start.8 = (f32[4,128,128]{2,1,0:T(8,128)S(1)}, f32[4,128,128]{2,1,0:T(8,128)S(1)}, u32[]{:S(2)}, u32[]{:S(2)}) collective-permute-start(f32[4,128,128]{2,1,0:T(8,128)S(1)} %sums_two.1.pk3), channel_id=1, source_target_pairs={{0,128},{128,0},{64,192},{192,64},{1,129},{129,1},{65,193},{193,65... | collective-permute-start | bytes 786440 | tf_op jit(solution)/shard_map/ppermute | solution.py:325
  45.2 5.6 %collective-permute-done.9.hout = f32[4,128,128]{2,1,0:T(8,128)S(1)} collective-permute-done((f32[4,128,128]{2,1,0:T(8,128)S(1)}, f32[4,128,128]{2,1,0:T(8,128)S(1)}, u32[]{:S(2)}, u32[]{:S(2)}) %collective-permute-start.9) | collective-permute-done | bytes 262176 | tf_op jit(solution)/shard_map/ppermute | solution.py:326
  50.8 0.0 collective-permute-done.10.hin
  50.8 0.8 %sums_three.1 = (f32[4,2,128,128]{3,2,1,0:T(8,128)S(1)}, f32[2,128,128]{2,1,0:T(8,128)S(1)}) custom-call(s32[1]{0:T(128)} %bitcast.core_ref, f32[16,128]{1,0:T(8,128)S(1)} %get-tuple-element.34.coef, f32[4,2,128,128]{3,2,1,0:T(8,128)S(1)} %get-tuple-element.49.l2, f32[4,128,128]{2,1,0:T(8,128)S(1)} %collective-permute-done.9.hout, ...), custom_call_target="tpu_custom_call" | custom-call | flops 11042816 | bytes 2760704 | tf_op jit(solution)/shard_map/sums_three/pallas_call | solution.py:303
  51.5 1.8 %collective-permute-done.8.got = f32[4,128,128]{2,1,0:T(8,128)S(1)} collective-permute-done((f32[4,128,128]{2,1,0:T(8,128)S(1)}, f32[4,128,128]{2,1,0:T(8,128)S(1)}, u32[]{:S(2)}, u32[]{:S(2)}) %collective-permute-start.8) | collective-permute-done | bytes 262176 | tf_op jit(solution)/shard_map/ppermute | solution.py:325
  53.4 0.2 cot_one.1
  53.6 3.3 %collective-permute-start.11 = (f32[4,128,128]{2,1,0:T(8,128)S(1)}, f32[4,128,128]{2,1,0:T(8,128)S(1)}, u32[]{:S(2)}, u32[]{:S(2)}) collective-permute-start(f32[4,128,128]{2,1,0:T(8,128)S(1)} %get-tuple-element.59), channel_id=1, source_target_pairs={{64,1},{1,64},{192,129},{129,192},{65,2},{2,65},{193,130},{130,193... | collective-permute-start | bytes 786440 | tf_op jit(solution)/shard_map/ppermute | solution.py:326
  56.9 1.1 %collective-permute-start.12 = (f32[4,128,128]{2,1,0:T(8,128)S(1)}, f32[4,128,128]{2,1,0:T(8,128)S(1)}, u32[]{:S(2)}, u32[]{:S(2)}) collective-permute-start(f32[4,128,128]{2,1,0:T(8,128)S(1)} %get-tuple-element.60), channel_id=1, source_target_pairs={{0,64},{64,0},{128,192},{192,128},{1,65},{65,1},{129,193},{193,129... | collective-permute-start | bytes 786440 | tf_op jit(solution)/shard_map/ppermute | solution.py:324
  57.9 2.7 %collective-permute-start.14 = (f32[2,128,128]{2,1,0:T(8,128)S(1)}, f32[2,128,128]{2,1,0:T(8,128)S(1)}, u32[]{:S(2)}, u32[]{:S(2)}) collective-permute-start(f32[2,128,128]{2,1,0:T(8,128)S(1)} %get-tuple-element.64.s0), channel_id=1, source_target_pairs={{0,128},{128,0},{64,192},{192,64},{1,129},{129,1},{65,193},{193,65... | collective-permute-start | bytes 393224 | tf_op jit(solution)/shard_map/ppermute | solution.py:325
  60.6 2.9 %collective-permute-done.11.hout = f32[4,128,128]{2,1,0:T(8,128)S(1)} collective-permute-done((f32[4,128,128]{2,1,0:T(8,128)S(1)}, f32[4,128,128]{2,1,0:T(8,128)S(1)}, u32[]{:S(2)}, u32[]{:S(2)}) %collective-permute-start.11) | collective-permute-done | bytes 262176 | tf_op jit(solution)/shard_map/ppermute | solution.py:326
  63.5 0.0 collective-permute-done.12.hin
  63.5 0.6 finish.1
  64.2 2.7 %collective-permute-start.13 = (f32[2,2,128,128]{3,2,1,0:T(8,128)S(1)}, f32[2,2,128,128]{3,2,1,0:T(8,128)S(1)}, u32[]{:S(2)}, u32[]{:S(2)}) collective-permute-start(f32[2,2,128,128]{3,2,1,0:T(8,128)S(1)} %get-tuple-element.63), channel_id=1, source_target_pairs={{0,64},{64,0},{128,192},{192,128},{1,65},{65,1},{129,193},{193,129... | collective-permute-start | bytes 786440 | tf_op jit(solution)/shard_map/ppermute | solution.py:324
  66.9 2.9 %collective-permute-done.14.got = f32[2,128,128]{2,1,0:T(8,128)S(1)} collective-permute-done((f32[2,128,128]{2,1,0:T(8,128)S(1)}, f32[2,128,128]{2,1,0:T(8,128)S(1)}, u32[]{:S(2)}, u32[]{:S(2)}) %collective-permute-start.14) | collective-permute-done | bytes 131104 | tf_op jit(solution)/shard_map/ppermute | solution.py:325
  69.8 0.1 total_push.1.tsum
  69.8 0.1 collective-permute-start.15
  69.9 1.3 %collective-permute-done.15.tother = f32[2,128,128]{2,1,0:T(8,128)S(1)} collective-permute-done((f32[2,128,128]{2,1,0:T(8,128)S(1)}, f32[2,128,128]{2,1,0:T(8,128)S(1)}, u32[]{:S(2)}, u32[]{:S(2)}) %collective-permute-start.15) | collective-permute-done | bytes 131104 | tf_op jit(solution)/shard_map/ppermute | solution.py:324
  71.3 0.0 collective-permute-done.13.other
  71.3 1.6 %assemble.1 = (f32[2,4,128,128]{3,2,1,0:T(8,128)}, f32[2,4,128,128]{3,2,1,0:T(8,128)}) custom-call(s32[1]{0:T(128)} %bitcast.core_ref, f32[2]{0:T(128)S(1)} %copy-done.7, f32[2,2,128,128]{3,2,1,0:T(8,128)S(1)} %get-tuple-element.62.own, f32[2,2,128,128]{3,2,1,0:T(8,128)S(1)} %collective-permute-done.13.other, f32[2,128,128]{2,1,0:T(8,128)S(1)} %total_push.1.tsum, ...), custom_call_target="tpu_custom_call" | custom-call | flops 5242880 | bytes 1310720 | tf_op jit(solution)/shard_map/assemble/pallas_call | solution.py:303
  (2 shorter events, 0.0 us)
Async XLA Ops:
  0.6 0.7 copy-start.7
  0.7 0.7 copy-start.8
  0.7 0.7 copy-start.9
  1.3 1.0 %copy-start.3 = (f32[2,4,128,128]{3,2,1,0:T(8,128)S(1)}, f32[2,4,128,128]{3,2,1,0:T(8,128)}, u32[]{:S(2)}) copy-start(f32[2,4,128,128]{3,2,1,0:T(8,128)} %dep.3) | copy-start | bytes 1572868
  2.4 1.0 %copy-start.4 = (f32[2,4,128,128]{3,2,1,0:T(8,128)S(1)}, f32[2,4,128,128]{3,2,1,0:T(8,128)}, u32[]{:S(2)}) copy-start(f32[2,4,128,128]{3,2,1,0:T(8,128)} %conc.3) | copy-start | bytes 1572868
  3.4 1.4 %copy-start.1 = (f32[2,4,128,128]{3,2,1,0:T(8,128)S(1)}, f32[2,4,128,128]{3,2,1,0:T(8,128)}, u32[]{:S(2)}) copy-start(f32[2,4,128,128]{3,2,1,0:T(8,128)} %q.5) | copy-start | bytes 1572868
  3.4 1.4 %copy-start.2 = (f32[2,4,128,128]{3,2,1,0:T(8,128)S(1)}, f32[2,4,128,128]{3,2,1,0:T(8,128)}, u32[]{:S(2)}) copy-start(f32[2,4,128,128]{3,2,1,0:T(8,128)} %p.3) | copy-start | bytes 1572868
  4.0 2.4 %copy-start.5 = (f32[2,4,128,128]{3,2,1,0:T(8,128)S(1)}, f32[2,4,128,128]{3,2,1,0:T(8,128)}, u32[]{:S(2)}) copy-start(f32[2,4,128,128]{3,2,1,0:T(8,128)} %conc.3) | copy-start | bytes 1572868
  4.0 2.4 %collective-permute-start = (f32[9,128,128]{2,1,0:T(8,128)S(1)}, f32[9,128,128]{2,1,0:T(8,128)S(1)}, u32[]{:S(2)}, u32[]{:S(2)}) collective-permute-start(f32[9,128,128]{2,1,0:T(8,128)S(1)} %send_state.1), channel_id=1, source_target_pairs={{0,64},{64,0},{128,192},{192,128},{1,65},{65,1},{129,193},{193,129... | collective-permute-start | bytes 1769480 | tf_op jit(solution)/shard_map/ppermute | solution.py:324
  4.9 8.2 %copy-start = (f32[4,128,128]{2,1,0:T(8,128)S(1)}, f32[4,128,128]{2,1,0:T(8,128)}, u32[]{:S(2)}) copy-start(f32[4,128,128]{2,1,0:T(8,128)} %vel.15) | copy-start | bytes 786436
  4.9 8.6 %collective-permute-start.1 = (f32[10,128,128]{2,1,0:T(8,128)S(1)}, f32[10,128,128]{2,1,0:T(8,128)S(1)}, u32[]{:S(2)}, u32[]{:S(2)}) collective-permute-start(f32[10,128,128]{2,1,0:T(8,128)S(1)} %send_cot.1), channel_id=1, source_target_pairs={{0,64},{64,0},{128,192},{192,128},{1,65},{65,1},{129,193},{193,129... | collective-permute-start | bytes 1966088 | tf_op jit(solution)/shard_map/ppermute | solution.py:324
  7.1 10.1 %collective-permute-start.2 = (f32[4,128,128]{2,1,0:T(8,128)S(1)}, f32[4,128,128]{2,1,0:T(8,128)S(1)}, u32[]{:S(2)}, u32[]{:S(2)}) collective-permute-start(f32[4,128,128]{2,1,0:T(8,128)S(1)} %get-tuple-element.39), channel_id=1, source_target_pairs={{64,1},{1,64},{192,129},{129,192},{65,2},{2,65},{193,130},{130,193... | collective-permute-start | bytes 786440 | tf_op jit(solution)/shard_map/ppermute | solution.py:326
  10.5 17.2 %collective-permute-start.4 = (f32[4,128,128]{2,1,0:T(8,128)S(1)}, f32[4,128,128]{2,1,0:T(8,128)S(1)}, u32[]{:S(2)}, u32[]{:S(2)}) collective-permute-start(f32[4,128,128]{2,1,0:T(8,128)S(1)} %get-tuple-element.42.pk1), channel_id=1, source_target_pairs={{0,128},{128,0},{64,192},{192,64},{1,129},{129,1},{65,193},{193,65... | collective-permute-start | bytes 786440 | tf_op jit(solution)/shard_map/ppermute | solution.py:325
  14.0 17.3 %collective-permute-start.5 = (f32[4,128,128]{2,1,0:T(8,128)S(1)}, f32[4,128,128]{2,1,0:T(8,128)S(1)}, u32[]{:S(2)}, u32[]{:S(2)}) collective-permute-start(f32[4,128,128]{2,1,0:T(8,128)S(1)} %get-tuple-element.47), channel_id=1, source_target_pairs={{64,1},{1,64},{192,129},{129,192},{65,2},{2,65},{193,130},{130,193... | collective-permute-start | bytes 786440 | tf_op jit(solution)/shard_map/ppermute | solution.py:326
  17.3 10.5 %copy-start.6 = (s32[4,128,128]{2,1,0:T(8,128)S(1)}, s32[4,128,128]{2,1,0:T(8,128)}, u32[]{:S(2)}) copy-start(s32[4,128,128]{2,1,0:T(8,128)} %label.1) | copy-start | bytes 786436
  17.4 22.1 %collective-permute-start.3 = (f32[4,128,128]{2,1,0:T(8,128)S(1)}, f32[4,128,128]{2,1,0:T(8,128)S(1)}, u32[]{:S(2)}, u32[]{:S(2)}) collective-permute-start(f32[4,128,128]{2,1,0:T(8,128)S(1)} %get-tuple-element.41.pk2), channel_id=1, source_target_pairs={{0,128},{128,0},{64,192},{192,64},{1,129},{129,1},{65,193},{193,65... | collective-permute-start | bytes 786440 | tf_op jit(solution)/shard_map/ppermute | solution.py:325
  28.0 14.0 %collective-permute-start.6 = (f32[4,128,128]{2,1,0:T(8,128)S(1)}, f32[4,128,128]{2,1,0:T(8,128)S(1)}, u32[]{:S(2)}, u32[]{:S(2)}) collective-permute-start(f32[4,128,128]{2,1,0:T(8,128)S(1)} %get-tuple-element.50), channel_id=1, source_target_pairs={{64,1},{1,64},{192,129},{129,192},{65,2},{2,65},{193,130},{130,193... | collective-permute-start | bytes 786440 | tf_op jit(solution)/shard_map/ppermute | solution.py:326
  29.9 12.0 %collective-permute-start.7 = (f32[4,128,128]{2,1,0:T(8,128)S(1)}, f32[4,128,128]{2,1,0:T(8,128)S(1)}, u32[]{:S(2)}, u32[]{:S(2)}) collective-permute-start(f32[4,128,128]{2,1,0:T(8,128)S(1)} %get-tuple-element.51), channel_id=1, source_target_pairs={{0,64},{64,0},{128,192},{192,128},{1,65},{65,1},{129,193},{193,129... | collective-permute-start | bytes 786440 | tf_op jit(solution)/shard_map/ppermute | solution.py:324
  39.9 10.9 %collective-permute-start.9 = (f32[4,128,128]{2,1,0:T(8,128)S(1)}, f32[4,128,128]{2,1,0:T(8,128)S(1)}, u32[]{:S(2)}, u32[]{:S(2)}) collective-permute-start(f32[4,128,128]{2,1,0:T(8,128)S(1)} %get-tuple-element.55), channel_id=1, source_target_pairs={{64,1},{1,64},{192,129},{129,192},{65,2},{2,65},{193,130},{130,193... | collective-permute-start | bytes 786440 | tf_op jit(solution)/shard_map/ppermute | solution.py:326
  41.9 8.9 %collective-permute-start.10 = (f32[4,128,128]{2,1,0:T(8,128)S(1)}, f32[4,128,128]{2,1,0:T(8,128)S(1)}, u32[]{:S(2)}, u32[]{:S(2)}) collective-permute-start(f32[4,128,128]{2,1,0:T(8,128)S(1)} %get-tuple-element.56), channel_id=1, source_target_pairs={{0,64},{64,0},{128,192},{192,128},{1,65},{65,1},{129,193},{193,129... | collective-permute-start | bytes 786440 | tf_op jit(solution)/shard_map/ppermute | solution.py:324
  42.7 10.6 %collective-permute-start.8 = (f32[4,128,128]{2,1,0:T(8,128)S(1)}, f32[4,128,128]{2,1,0:T(8,128)S(1)}, u32[]{:S(2)}, u32[]{:S(2)}) collective-permute-start(f32[4,128,128]{2,1,0:T(8,128)S(1)} %sums_two.1.pk3), channel_id=1, source_target_pairs={{0,128},{128,0},{64,192},{192,64},{1,129},{129,1},{65,193},{193,65... | collective-permute-start | bytes 786440 | tf_op jit(solution)/shard_map/ppermute | solution.py:325
  53.6 9.9 %collective-permute-start.11 = (f32[4,128,128]{2,1,0:T(8,128)S(1)}, f32[4,128,128]{2,1,0:T(8,128)S(1)}, u32[]{:S(2)}, u32[]{:S(2)}) collective-permute-start(f32[4,128,128]{2,1,0:T(8,128)S(1)} %get-tuple-element.59), channel_id=1, source_target_pairs={{64,1},{1,64},{192,129},{129,192},{65,2},{2,65},{193,130},{130,193... | collective-permute-start | bytes 786440 | tf_op jit(solution)/shard_map/ppermute | solution.py:326
  56.9 6.6 %collective-permute-start.12 = (f32[4,128,128]{2,1,0:T(8,128)S(1)}, f32[4,128,128]{2,1,0:T(8,128)S(1)}, u32[]{:S(2)}, u32[]{:S(2)}) collective-permute-start(f32[4,128,128]{2,1,0:T(8,128)S(1)} %get-tuple-element.60), channel_id=1, source_target_pairs={{0,64},{64,0},{128,192},{192,128},{1,65},{65,1},{129,193},{193,129... | collective-permute-start | bytes 786440 | tf_op jit(solution)/shard_map/ppermute | solution.py:324
  57.9 11.8 %collective-permute-start.14 = (f32[2,128,128]{2,1,0:T(8,128)S(1)}, f32[2,128,128]{2,1,0:T(8,128)S(1)}, u32[]{:S(2)}, u32[]{:S(2)}) collective-permute-start(f32[2,128,128]{2,1,0:T(8,128)S(1)} %get-tuple-element.64.s0), channel_id=1, source_target_pairs={{0,128},{128,0},{64,192},{192,64},{1,129},{129,1},{65,193},{193,65... | collective-permute-start | bytes 393224 | tf_op jit(solution)/shard_map/ppermute | solution.py:325
  64.2 7.1 %collective-permute-start.13 = (f32[2,2,128,128]{3,2,1,0:T(8,128)S(1)}, f32[2,2,128,128]{3,2,1,0:T(8,128)S(1)}, u32[]{:S(2)}, u32[]{:S(2)}) collective-permute-start(f32[2,2,128,128]{3,2,1,0:T(8,128)S(1)} %get-tuple-element.63), channel_id=1, source_target_pairs={{0,64},{64,0},{128,192},{192,128},{1,65},{65,1},{129,193},{193,129... | collective-permute-start | bytes 786440 | tf_op jit(solution)/shard_map/ppermute | solution.py:324
  69.8 1.4 %collective-permute-start.15 = (f32[2,128,128]{2,1,0:T(8,128)S(1)}, f32[2,128,128]{2,1,0:T(8,128)S(1)}, u32[]{:S(2)}, u32[]{:S(2)}) collective-permute-start(f32[2,128,128]{2,1,0:T(8,128)S(1)} %total_push.1.tsum), channel_id=1, source_target_pairs={{0,64},{64,0},{128,192},{192,128},{1,65},{65,1},{129,193},{193,129... | collective-permute-start | bytes 393224 | tf_op jit(solution)/shard_map/ppermute | solution.py:324

commit v2 on v1

v2 whole, which is shorter than its diff:
```python
import functools

import jax
import jax.numpy as jnp
from jax import lax
from jax.experimental import pallas as pl
from jax.experimental.pallas import tpu as pltpu
from jax.sharding import PartitionSpec as P

H = 0.25
SURFACE_EFF = (0.1, 0.6, 1.2, 2.0)
N = 128
WORK = {
    "send_state": 0.0,
    "send_cot": 0.01,
    "sums_zero": 0.01,
    "sums_one": 0.01,
    "step_base": 0.01,
    "cot_base": 0.01,
    "state_one": 0.01,
    "state_two": 0.01,
    "sums_two": 0.01,
    "cot_two": 0.01,
    "cot_one_base": 0.01,
    "cot_one": 0.01,
    "sums_three": 0.01,
    "finish_base": 0.01,
    "finish": 0.01,
    "write_dep": 0.01,
    "write_conc": 0.01,
    "total_push": 0.01,
}
F32 = jnp.float32


def lateral(x):
    row = lax.broadcasted_iota(jnp.int32, x.shape, 0)
    col = lax.broadcasted_iota(jnp.int32, x.shape, 1)
    up = jnp.where(row > 0, pltpu.roll(x, 1, 0), 0.0)
    down = jnp.where(row < N - 1, pltpu.roll(x, N - 1, 0), 0.0)
    left = jnp.where(col > 0, pltpu.roll(x, 1, 1), 0.0)
    right = jnp.where(col < N - 1, pltpu.roll(x, N - 1, 1), 0.0)
    return (up + down) + (left + right) - 6.0 * x


def efficiency(label):
    out = jnp.zeros(label.shape, F32)
    for k in range(4):
        out = jnp.where(label == k, SURFACE_EFF[k], out)
    return out


class Coef:
    def __init__(self, ref):
        self.dif = [ref[c : c + 1, :] for c in range(4)]
        self.rate = [ref[4 + c : 5 + c, :] for c in range(4)]
        self.vol = [ref[8 + c : 9 + c, :] for c in range(4)]


def send_state(core_ref, dif, rate, vol, dep, conc, msg, mine, theta, rows):
    core = core_ref[0]
    other = 1 - core
    for l in range(2):
        msg[l] = vol[0] * dep[0, 2 * other + l] + vol[1] * dep[1, 2 * other + l]
        theta[l] = vol[0] * dep[0, 2 * core + l] + vol[1] * dep[1, 2 * core + l]
    for c in range(2):
        for l in range(2):
            msg[2 + 3 * c + l] = conc[c, 2 * other + l]
            mine[3 * c + l] = conc[c, 2 * core + l]
        msg[4 + 3 * c] = conc[c, 2 - other]
        mine[3 * c + 2] = conc[c, 2 - core]
    for k, ref in enumerate((dif, rate, vol)):
        for c in range(2):
            row = jnp.full((1, N), ref[c], F32)
            msg[8, 2 * k + c : 2 * k + c + 1, :] = row
            rows[2 * k + c : 2 * k + c + 1, :] = row


def send_cot(core_ref, p, q, msg):
    other = 1 - core_ref[0]
    for c in range(2):
        for l in range(2):
            msg[3 * c + l] = p[c, 2 * other + l]
            msg[6 + 2 * c + l] = q[c, 2 * other + l]
        msg[3 * c + 2] = p[c, 2 - other]


def sums_zero(core_ref, rows, theta, mine, got, pk1, ho, c0, coef, u4, uin):
    core = core_ref[0]
    for k in range(3):
        coef[4 * k : 4 * k + 2, :] = rows[2 * k : 2 * k + 2, :]
        coef[4 * k + 2 : 4 * k + 4, :] = got[8, 2 * k : 2 * k + 2, :]
    co = Coef(coef)
    for l in range(2):
        pk1[l] = got[l] + theta[l]
        total = jnp.zeros((N, N), F32)
        square = jnp.zeros((N, N), F32)
        for c in range(4):
            u = mine[3 * c + l] if c < 2 else got[2 + 3 * (c - 2) + l]
            u4[c, l] = u
            term = (co.vol[c] * co.rate[c]) * u
            total = total + term
            square = square + co.rate[c] * term
        pk1[2 + l] = total
        c0[l] = square
    for c in range(4):
        uin[c] = mine[3 * c + 2] if c < 2 else got[4 + 3 * (c - 2)]
        ho[(c + 2) % 4] = u4[c, core]


def advect(co, u4, vel, core, c, l):
    u = u4[c, l]
    out = co.dif[c] * lateral(u) - vel[2 * core + l] * u
    if l == 0:
        return out + co.dif[c] * u4[c, 1]
    return out + (co.dif[c] + vel[2 * core + 1]) * u4[c, 0]


def back(co, x4, vel, core, c, l):
    x = x4[c, l]
    out = co.dif[c] * lateral(x) - vel[2 * core + l] * x
    if l == 0:
        return out + (co.dif[c] + vel[2 * core + 1]) * x4[c, 1]
    return out + co.dif[c] * x4[c, 0]


def facing(co, vel, core):
    low = vel[2 * core]
    out_part = jnp.where(core == 0, low, 0.0)
    in_part = jnp.where(core == 1, low, 0.0)
    return (
        [co.dif[c] + out_part for c in range(4)],
        [co.dif[c] + in_part for c in range(4)],
    )


def step_base(core_ref, coef, u4, uin, vel, a4):
    core = core_ref[0]
    co = Coef(coef)
    _, fin = facing(co, vel, core)
    for c in range(4):
        for l in range(2):
            a4[c, l] = u4[c, l] + H * advect(co, u4, vel, core, c, l)
        a4[c, 1 - core] = a4[c, 1 - core] + H * (fin[c] * uin[c])


def cot_base(core_ref, coef, p, q, got, vel, p4, q4, base, ho):
    core = core_ref[0]
    co = Coef(coef)
    fout, _ = facing(co, vel, core)
    above = jnp.where(core == 0, vel[2 - core], 0.0)
    for c in range(4):
        for l in range(2):
            p4[c, l] = p[c, 2 * core + l] if c < 2 else got[3 * (c - 2) + l]
            q4[c, l] = q[c, 2 * core + l] if c < 2 else got[6 + 2 * (c - 2) + l]
        ho[(c + 2) % 4] = fout[c] * p4[c, core]
        for l in range(2):
            base[c, l] = back(co, p4, vel, core, c, l)
        pin = p[c, 2 - core] if c < 2 else got[3 * (c - 2) + 2]
        base[c, 1 - core] = base[c, 1 - core] + (co.dif[c] + above) * pin


def sums_one(core_ref, coef, base, hout, vel, c0, a4, pk2):
    core = core_ref[0]
    co = Coef(coef)
    fout, _ = facing(co, vel, core)
    for l in range(2):
        for c in range(4):
            a4[c, l] = base[c, l]
    for c in range(4):
        a4[c, core] = a4[c, core] + H * (fout[c] * hout[c])
    for l in range(2):
        total = jnp.zeros((N, N), F32)
        for c in range(4):
            total = total + (co.vol[c] * co.rate[c]) * a4[c, l]
        pk2[l] = total
        pk2[2 + l] = c0[l]


def state_one(core_ref, coef, pk1, got, label, a4, u4, u1, ho, hi, k01, th, a0s):
    core = core_ref[0]
    co = Coef(coef)
    for l in range(2):
        coll = efficiency(label[2 * core + l])
        theta = pk1[l] + got[l]
        a0 = pk1[2 + l] + got[2 + l]
        k0 = coll * jnp.exp(-theta)
        theta1 = theta + H * (k0 * a0)
        k01[l] = k0
        k01[2 + l] = coll * jnp.exp(-theta1)
        k01[4 + l] = coll
        th[l] = theta
        th[2 + l] = theta1
        a0s[l] = a0
        for c in range(4):
            u1[c, l] = a4[c, l] - (H * k0) * (co.rate[c] * u4[c, l])
    for c in range(4):
        ho[(c + 2) % 4] = u1[c, core]
        hi[(c + 2) % 4] = u1[c, 1 - core]


def state_two(core_ref, coef, u4, u1, hin, k01, vel, p4, q4, part, wout):
    core = core_ref[0]
    co = Coef(coef)
    fout, fin = facing(co, vel, core)
    for l in range(2):
        total = jnp.zeros((N, N), F32)
        for c in range(4):
            u = u1[c, l]
            rate = advect(co, u1, vel, core, c, l) - (co.rate[c] * k01[2 + l]) * u
            u2 = 0.75 * u4[c, l] + 0.25 * (u + H * rate)
            total = total + (co.rate[c] * (q4[c, l] - p4[c, l])) * u2
        part[l] = total
    edge = part[1 - core]
    for c in range(4):
        scaled = (0.25 * H) * co.rate[c]
        wout[c] = scaled * ((q4[c, core] - p4[c, core]) * fout[c])
        edge = edge + scaled * ((q4[c, 1 - core] - p4[c, 1 - core]) * (fin[c] * hin[c]))
    part[1 - core] = edge


def sums_two(core_ref, part, wout, hout, pk3):
    core = core_ref[0]
    edge = part[core]
    for c in range(4):
        edge = edge + wout[c] * hout[c]
    pk3[1 - core] = part[1 - core]
    pk3[core] = edge


def cot_two(core_ref, coef, pk2, got, k01, th, a0, p4, q4, base, hout, vel, l2, ho, hi, k2s, sums):
    core = core_ref[0]
    co = Coef(coef)
    fout, fin = facing(co, vel, core)
    for l in range(2):
        c0 = pk2[2 + l] + got[2 + l]
        a1 = (pk2[l] + got[l]) - (H * k01[l]) * c0
        theta2 = 0.75 * th[l] + 0.25 * (th[2 + l] + H * (k01[2 + l] * a1))
        k2 = k01[4 + l] * jnp.exp(-theta2)
        k2s[l] = k2
        sums[l] = a0[l]
        sums[2 + l] = a1
        sums[4 + l] = c0
        for c in range(4):
            p = p4[c, l]
            l2[c, l] = (2.0 / 3.0) * p + (2.0 / 3.0 * H) * (
                base[c, l] + (co.rate[c] * k2) * (q4[c, l] - p)
            )
    for c in range(4):
        l2[c, core] = l2[c, core] + (2.0 / 3.0 * H) * hout[c]
        ho[(c + 2) % 4] = fout[c] * l2[c, core]
        hi[(c + 2) % 4] = fin[c] * l2[c, 1 - core]


def cot_one_base(core_ref, coef, l2, hin, k01, vel, q4, u1, u4, l1, part):
    core = core_ref[0]
    co = Coef(coef)
    for c in range(4):
        for l in range(2):
            x = l2[c, l]
            w = (2.0 / 3.0) * q4[c, l] - x
            rest = back(co, l2, vel, core, c, l) + (co.rate[c] * k01[2 + l]) * w
            l1[c, l] = 0.25 * x + (0.25 * H) * rest
        l1[c, 1 - core] = l1[c, 1 - core] + (0.25 * H) * hin[c]
    for l in range(2):
        first = jnp.zeros((N, N), F32)
        zero = jnp.zeros((N, N), F32)
        for c in range(4):
            q = q4[c, l]
            first = first + (co.rate[c] * ((2.0 / 3.0) * q - l2[c, l])) * u1[c, l]
            zero = zero + (co.rate[c] * ((1.0 / 6.0) * q - l1[c, l])) * u4[c, l]
        part[l] = first
        part[2 + l] = zero


def cot_one(core_ref, coef, pk3, got, k01, k2s, sums, l1k, vel, l1, ho, hi, t2s):
    core = core_ref[0]
    co = Coef(coef)
    fout, fin = facing(co, vel, core)
    for l in range(2):
        t2 = (-2.0 / 3.0 * H) * k2s[l] * (pk3[l] + got[l])
        push = (0.25 * H) * (k01[2 + l] * t2)
        t2s[l] = t2
        t2s[2 + l] = sums[l]
        t2s[4 + l] = sums[2 + l]
        t2s[6 + l] = push * sums[4 + l]
        for c in range(4):
            l1[c, l] = l1k[c, l] + (co.rate[c] * co.vol[c]) * push
    for c in range(4):
        ho[(c + 2) % 4] = fout[c] * l1[c, core]
        hi[(c + 2) % 4] = fin[c] * l1[c, 1 - core]


def sums_three(core_ref, coef, base, part, hout, u4, l1, pk4):
    core = core_ref[0]
    co = Coef(coef)
    edge = part[2 + core]
    for c in range(4):
        more = (0.25 * H) * hout[c]
        l1[c, 1 - core] = base[c, 1 - core]
        l1[c, core] = base[c, core] + more
        edge = edge - (co.rate[c] * more) * u4[c, core]
    for l in range(2):
        pk4[l] = part[l]
    pk4[3 - core] = part[3 - core]
    pk4[2 + core] = edge


def total_push(core_ref, pk4, got, k01, t2s, tsum, mixed):
    for l in range(2):
        t2 = t2s[l]
        t1 = (-0.25 * H) * k01[2 + l] * ((pk4[l] + got[l]) + t2 * t2s[4 + l])
        both = 0.25 * t2 + t1
        zero = (pk4[2 + l] + got[2 + l]) + both * t2s[2 + l] - t2s[6 + l]
        tsum[l] = t2 + t1 - H * (k01[l] * zero)
        mixed[l] = both


def finish_base(core_ref, coef, p4, q4, l2, l1, hin, k01, mixed, vel, out):
    core = core_ref[0]
    co = Coef(coef)
    for l in range(2):
        for c in range(4):
            x = l1[c, l]
            l1s = q4[c, l] * (1.0 / 6.0) + co.vol[c] * mixed[l]
            rest = back(co, l1, vel, core, c, l) + (co.rate[c] * k01[l]) * (l1s - x)
            out[c, l] = (1.0 / 3.0) * p4[c, l] + 0.75 * l2[c, l] + x + H * rest
    for c in range(4):
        out[c, 1 - core] = out[c, 1 - core] + H * hin[c]


def finish(core_ref, base, hout, after, own, msg):
    core = core_ref[0]
    for c in range(4):
        dst = own if c < 2 else msg
        k = 2 * (c % 2)
        dst[k + 1 - core] = base[c, 1 - core]
        dst[k + core] = base[c, core] + H * hout[c]


def write_dep(core_ref, coef, tsum, got, q, dep, buf, sem):
    core = core_ref[0]
    vol = Coef(coef).vol
    copies = []
    for c in range(2):
        for k, (src, half) in enumerate(((tsum, core), (got, 1 - core))):
            for l in range(2):
                buf[c, 2 * half + l] = q[c, 2 * half + l] + vol[c] * src[l]
            there = pl.ds(2 * half, 2)
            copies.append(pltpu.make_async_copy(buf.at[c, there], dep.at[c, there], sem.at[2 * c + k]))
            copies[-1].start()
    for copy in copies:
        copy.wait()


def write_conc(core_ref, own, got, conc, sem):
    core = core_ref[0]
    copies = []
    for c in range(2):
        for k, (src, half) in enumerate(((own, core), (got, 1 - core))):
            copies.append(
                pltpu.make_async_copy(
                    src.at[pl.ds(2 * c, 2)], conc.at[c, pl.ds(2 * half, 2)], sem.at[2 * c + k]
                )
            )
            copies[-1].start()
    for copy in copies:
        copy.wait()


def call(body, outs, scalars, arrays, scratch=(), sems=0, hbm_out=False, size=None):
    smem = pl.BlockSpec(memory_space=pltpu.SMEM)
    vmem = pl.BlockSpec(memory_space=pltpu.VMEM)
    hbm = pl.BlockSpec(memory_space=pltpu.HBM)
    scratch_shapes = [pltpu.VMEM(s, F32) for s in scratch]
    if sems:
        scratch_shapes.append(pltpu.SemaphoreType.DMA((sems,)))
    if size is None:
        size = sum(4 * a.size for a in arrays)
    return pl.pallas_call(
        body,
        out_shape=[jax.ShapeDtypeStruct(s, F32) for s in outs],
        in_specs=[smem] * len(scalars) + [vmem] * len(arrays),
        out_specs=[hbm if hbm_out else vmem] * len(outs),
        scratch_shapes=scratch_shapes,
        compiler_params=pltpu.CompilerParams(vmem_limit_bytes=16 * 1024 * 1024),
        cost_estimate=pl.CostEstimate(
            flops=int(WORK[body.__name__] * 1e9), bytes_accessed=size, transcendentals=0
        ),
        name=body.__name__,
    )(*scalars, *arrays)


def shards(peers, conc, dep, velocity, label, dif, rate, vol, p, q):
    core = (lax.axis_index("size") % 2).astype(jnp.int32)[None]
    swap = [(0, 1), (1, 0), (2, 3), (3, 2)]
    far = [(0, 2), (2, 0), (1, 3), (3, 1)]
    face = []
    for g in range(peers - 1):
        for chip in (0, 2):
            a, b = (chip + 1) * peers + g, chip * peers + g + 1
            face += [(a, b), (b, a)]
    inner = lambda x: lax.ppermute(x, "size", swap)
    across = lambda x: lax.ppermute(x, "size", far)
    outer = lambda x: lax.ppermute(x, ("size", "gz"), face)
    layers = lambda n: (n, N, N)
    eight = (4, 2, N, N)

    msg0, mine, theta, rows = call(
        send_state,
        [layers(9), layers(6), layers(2), (8, N)],
        (core, dif, rate, vol),
        (dep, conc),
        size=0,
    )
    got0 = inner(msg0)
    (msg1,) = call(send_cot, [layers(10)], (core,), (p, q))
    got1 = inner(msg1)
    pk1, ho0, c0, coef, u4, uin = call(
        sums_zero,
        [layers(4), layers(4), layers(2), (16, N), eight, layers(4)],
        (core,),
        (rows, theta, mine, got0),
    )
    gpk1 = across(pk1)
    hu0 = outer(ho0)
    (abase,) = call(step_base, [eight], (core,), (coef, u4, uin, velocity))
    p4, q4, pbase, hop = call(
        cot_base, [eight, eight, eight, layers(4)], (core,), (coef, p, q, got1, velocity)
    )
    hp = outer(hop)
    a4, pk2 = call(sums_one, [eight, layers(4)], (core,), (coef, abase, hu0, velocity, c0))
    gpk2 = across(pk2)
    u1, ho1, hi1, k01, th, a0 = call(
        state_one,
        [eight, layers(4), layers(4), layers(6), layers(4), layers(2)],
        (core,),
        (coef, pk1, gpk1, label, a4, u4),
    )
    iu1 = inner(hi1)
    hu1 = outer(ho1)
    part2, wout = call(
        state_two, [layers(2), layers(4)], (core,), (coef, u4, u1, iu1, k01, velocity, p4, q4)
    )
    l2, ho2, hi2, k2s, sums = call(
        cot_two,
        [eight, layers(4), layers(4), layers(2), layers(6)],
        (core,),
        (coef, pk2, gpk2, k01, th, a0, p4, q4, pbase, hp, velocity),
    )
    il2 = inner(hi2)
    hl2 = outer(ho2)
    (pk3,) = call(sums_two, [layers(2)], (core,), (part2, wout, hu1))
    gpk3 = across(pk3)
    l1base, part1 = call(
        cot_one_base, [eight, layers(4)], (core,), (coef, l2, il2, k01, velocity, q4, u1, u4)
    )
    l1k, pk4 = call(sums_three, [eight, layers(4)], (core,), (coef, l1base, part1, hl2, u4))
    gpk4 = across(pk4)
    l1, ho3, hi3, t2s = call(
        cot_one,
        [eight, layers(4), layers(4), layers(8)],
        (core,),
        (coef, pk3, gpk3, k01, k2s, sums, l1k, velocity),
    )
    il1 = inner(hi3)
    hl1 = outer(ho3)
    tsum, mixed = call(
        total_push, [layers(2), layers(2)], (core,), (pk4, gpk4, k01, t2s)
    )
    tother = inner(tsum)
    (base,) = call(
        finish_base, [eight], (core,), (coef, p4, q4, l2, l1, il1, k01, mixed, velocity)
    )
    own, msg = call(finish, [layers(4), layers(4)], (core,), (base, hl1, tother))
    theirs = inner(msg)
    state = (2, 4, N, N)
    (dep_out,) = call(
        write_dep, [state], (core,), (coef, tsum, tother, q), [state], 4, hbm_out=True
    )
    (conc_out,) = call(write_conc, [state], (core,), (own, theirs), (), 4, hbm_out=True)
    return conc_out, dep_out


def solution(mesh):
    state = P("size", "gz", None, None)
    flow = P("gz", None, None)
    in_specs = (state, state, flow, flow, P("size"), P("size"), P("size"), state, state)
    body = functools.partial(shards, mesh.shape["gz"])
    return jax.shard_map(
        body, mesh=mesh, in_specs=in_specs, out_specs=(state, state), check_vma=False
    )
```

time: 73.2 us -> 69.2 us (0.945)
  the two profiles are of different devices: /device:TPU:129 before, /device:TPU:97 now
where the time goes in v2:
time: 69.2 us; the launch traced here: 68.8 us
  starting transfers between devices  38 us (55%)
  waiting for transfers between devices  20.7 us (30%)
  Pallas kernels  6.58 us (10%)
  local copies, waits for them, and re-layouts  2.76 us (4%)
  between operations  0.86 us (1%)
    ppermute x7, starting transfers between devices, shards(): inner = lambda x: lax.ppermute(x, 'size', swap)  16.7 us
    ppermute x5, starting transfers between devices, shards(): outer = lambda x: lax.ppermute(x, ('size', 'gz'), face)  12.5 us
    ppermute x4, waiting for transfers between devices, shards(): across = lambda x: lax.ppermute(x, 'size', far)  11.6 us
    ppermute x4, starting transfers between devices, shards(): across = lambda x: lax.ppermute(x, 'size', far)  8.77 us
    ppermute x5, waiting for transfers between devices, shards(): outer = lambda x: lax.ppermute(x, ('size', 'gz'), face)  7.68 us
    pallas_call x18, Pallas kernels, call(): pl.pallas_call(body, out_shape=[jax.ShapeDtypeStruct(s, F32) for s in out...  6.58 us
    unnamed x18, local copies, waits for them, and re-layouts  2.76 us
  transfers between devices with their start and end apart: 16, of which 8 were waited for; matrix products, arithmetic and copies ran while one was open for 0% of the time, Pallas kernels for 7%

profile of v2, /device:TPU:97, one launch (start us, length us, event | category | flops | bytes accessed | tf_op | source)
XLA Modules:
  0.0 68.8 jit_solution(7746682797327313667)
XLA Ops:
  0.6 0.0 copy-start.6
  0.7 0.0 copy-start.7
  0.7 0.0 copy-start.8
  0.7 0.6 copy-done.6
  1.3 0.0 copy-done.7
  1.3 0.0 copy-done.8
  1.3 0.0 copy-start.3
  1.3 1.0 %copy-done.3 = f32[2,4,128,128]{3,2,1,0:T(8,128)S(1)} copy-done((f32[2,4,128,128]{3,2,1,0:T(8,128)S(1)}, f32[2,4,128,128]{3,2,1,0:T(8,128)}, u32[]{:S(2)}) %copy-start.3) | copy-done | bytes 524312
  2.4 0.0 copy-start.4
  2.4 1.0 %copy-done.4 = f32[2,4,128,128]{3,2,1,0:T(8,128)S(1)} copy-done((f32[2,4,128,128]{3,2,1,0:T(8,128)S(1)}, f32[2,4,128,128]{3,2,1,0:T(8,128)}, u32[]{:S(2)}) %copy-start.4) | copy-done | bytes 524312
  3.4 0.0 copy-start.1
  3.4 0.0 copy-start.2
  3.4 0.6 send_state.1
  4.1 0.8 %collective-permute-start = (f32[9,128,128]{2,1,0:T(8,128)S(1)}, f32[9,128,128]{2,1,0:T(8,128)S(1)}, u32[]{:S(2)}, u32[]{:S(2)}) collective-permute-start(f32[9,128,128]{2,1,0:T(8,128)S(1)} %get-tuple-element.46), channel_id=1, source_target_pairs={{0,64},{64,0},{128,192},{192,128},{1,65},{65,1},{129,193},{193,129... | collective-permute-start | bytes 1769480 | tf_op jit(solution)/shard_map/ppermute | solution.py:403
  4.8 0.0 copy-done.1
  4.8 0.0 copy-done.2
  4.9 0.5 collective-permute-start.1
  5.4 1.0 %collective-permute-done.got = f32[9,128,128]{2,1,0:T(8,128)S(1)} collective-permute-done((f32[9,128,128]{2,1,0:T(8,128)S(1)}, f32[9,128,128]{2,1,0:T(8,128)S(1)}, u32[]{:S(2)}, u32[]{:S(2)}) %collective-permute-start) | collective-permute-done | bytes 589856 | tf_op jit(solution)/shard_map/ppermute | solution.py:403
  6.5 0.1 sums_zero.1
  6.6 3.4 %collective-permute-start.2 = (f32[4,128,128]{2,1,0:T(8,128)S(1)}, f32[4,128,128]{2,1,0:T(8,128)S(1)}, u32[]{:S(2)}, u32[]{:S(2)}) collective-permute-start(f32[4,128,128]{2,1,0:T(8,128)S(1)} %get-tuple-element.52), channel_id=1, source_target_pairs={{64,1},{1,64},{192,129},{129,192},{65,2},{2,65},{193,130},{130,193... | collective-permute-start | bytes 786440 | tf_op jit(solution)/shard_map/ppermute | solution.py:405
  10.0 2.5 %collective-permute-start.4 = (f32[4,128,128]{2,1,0:T(8,128)S(1)}, f32[4,128,128]{2,1,0:T(8,128)S(1)}, u32[]{:S(2)}, u32[]{:S(2)}) collective-permute-start(f32[4,128,128]{2,1,0:T(8,128)S(1)} %get-tuple-element.55.pk1), channel_id=1, source_target_pairs={{0,128},{128,0},{64,192},{192,64},{1,129},{129,1},{65,193},{193,65... | collective-permute-start | bytes 786440 | tf_op jit(solution)/shard_map/ppermute | solution.py:404
  12.5 0.0 copy-done
  12.5 0.4 step_base.1.base
  13.0 0.0 collective-permute-done.1.got
  13.0 0.5 cot_base.1
  13.5 2.2 %collective-permute-start.5 = (f32[4,128,128]{2,1,0:T(8,128)S(1)}, f32[4,128,128]{2,1,0:T(8,128)S(1)}, u32[]{:S(2)}, u32[]{:S(2)}) collective-permute-start(f32[4,128,128]{2,1,0:T(8,128)S(1)} %get-tuple-element.61), channel_id=1, source_target_pairs={{64,1},{1,64},{192,129},{129,192},{65,2},{2,65},{193,130},{130,193... | collective-permute-start | bytes 786440 | tf_op jit(solution)/shard_map/ppermute | solution.py:405
  15.6 1.1 %collective-permute-done.2.hout = f32[4,128,128]{2,1,0:T(8,128)S(1)} collective-permute-done((f32[4,128,128]{2,1,0:T(8,128)S(1)}, f32[4,128,128]{2,1,0:T(8,128)S(1)}, u32[]{:S(2)}, u32[]{:S(2)}) %collective-permute-start.2) | collective-permute-done | bytes 262176 | tf_op jit(solution)/shard_map/ppermute | solution.py:405
  16.7 0.1 sums_one.1
  16.9 2.8 %collective-permute-start.3 = (f32[4,128,128]{2,1,0:T(8,128)S(1)}, f32[4,128,128]{2,1,0:T(8,128)S(1)}, u32[]{:S(2)}, u32[]{:S(2)}) collective-permute-start(f32[4,128,128]{2,1,0:T(8,128)S(1)} %get-tuple-element.54.pk2), channel_id=1, source_target_pairs={{0,128},{128,0},{64,192},{192,64},{1,129},{129,1},{65,193},{193,65... | collective-permute-start | bytes 786440 | tf_op jit(solution)/shard_map/ppermute | solution.py:404
  19.7 4.7 %collective-permute-done.4.got = f32[4,128,128]{2,1,0:T(8,128)S(1)} collective-permute-done((f32[4,128,128]{2,1,0:T(8,128)S(1)}, f32[4,128,128]{2,1,0:T(8,128)S(1)}, u32[]{:S(2)}, u32[]{:S(2)}) %collective-permute-start.4) | collective-permute-done | bytes 262176 | tf_op jit(solution)/shard_map/ppermute | solution.py:404
  24.4 0.0 copy-done.5
  24.4 0.2 state_one.1
  24.6 2.7 %collective-permute-start.6 = (f32[4,128,128]{2,1,0:T(8,128)S(1)}, f32[4,128,128]{2,1,0:T(8,128)S(1)}, u32[]{:S(2)}, u32[]{:S(2)}) collective-permute-start(f32[4,128,128]{2,1,0:T(8,128)S(1)} %get-tuple-element.64), channel_id=1, source_target_pairs={{0,64},{64,0},{128,192},{192,128},{1,65},{65,1},{129,193},{193,129... | collective-permute-start | bytes 786440 | tf_op jit(solution)/shard_map/ppermute | solution.py:403
  27.3 1.9 %collective-permute-start.7 = (f32[4,128,128]{2,1,0:T(8,128)S(1)}, f32[4,128,128]{2,1,0:T(8,128)S(1)}, u32[]{:S(2)}, u32[]{:S(2)}) collective-permute-start(f32[4,128,128]{2,1,0:T(8,128)S(1)} %get-tuple-element.67), channel_id=1, source_target_pairs={{64,1},{1,64},{192,129},{129,192},{65,2},{2,65},{193,130},{130,193... | collective-permute-start | bytes 786440 | tf_op jit(solution)/shard_map/ppermute | solution.py:405
  29.2 0.0 collective-permute-done.5.hout
  29.2 6.6 %collective-permute-done.3.got = f32[4,128,128]{2,1,0:T(8,128)S(1)} collective-permute-done((f32[4,128,128]{2,1,0:T(8,128)S(1)}, f32[4,128,128]{2,1,0:T(8,128)S(1)}, u32[]{:S(2)}, u32[]{:S(2)}) %collective-permute-start.3) | collective-permute-done | bytes 262176 | tf_op jit(solution)/shard_map/ppermute | solution.py:404
  35.8 0.4 cot_two.1
  36.2 0.1 collective-permute-start.9
  36.3 3.2 %collective-permute-start.10 = (f32[4,128,128]{2,1,0:T(8,128)S(1)}, f32[4,128,128]{2,1,0:T(8,128)S(1)}, u32[]{:S(2)}, u32[]{:S(2)}) collective-permute-start(f32[4,128,128]{2,1,0:T(8,128)S(1)} %get-tuple-element.73), channel_id=1, source_target_pairs={{64,1},{1,64},{192,129},{129,192},{65,2},{2,65},{193,130},{130,193... | collective-permute-start | bytes 786440 | tf_op jit(solution)/shard_map/ppermute | solution.py:405
  39.5 0.0 collective-permute-done.6.hin
  39.5 0.7 state_two.1
  40.2 0.0 collective-permute-done.7.hout
  40.3 1.5 %collective-permute-start.8 = (f32[2,128,128]{2,1,0:T(8,128)S(1)}, f32[2,128,128]{2,1,0:T(8,128)S(1)}, u32[]{:S(2)}, u32[]{:S(2)}) collective-permute-start(f32[2,128,128]{2,1,0:T(8,128)S(1)} %sums_two.1.pk3), channel_id=1, source_target_pairs={{0,128},{128,0},{64,192},{192,64},{1,129},{129,1},{65,193},{193,65... | collective-permute-start | bytes 393224 | tf_op jit(solution)/shard_map/ppermute | solution.py:404
  41.8 0.0 collective-permute-done.9.hin
  41.8 0.8 %cot_one_base.1 = (f32[4,2,128,128]{3,2,1,0:T(8,128)S(1)}, f32[4,128,128]{2,1,0:T(8,128)S(1)}) custom-call(s32[1]{0:T(128)} %bitcast.core_ref, f32[16,128]{1,0:T(8,128)S(1)} %get-tuple-element.47.coef, f32[4,2,128,128]{3,2,1,0:T(8,128)S(1)} %get-tuple-element.62.l2, f32[4,128,128]{2,1,0:T(8,128)S(1)} %collective-permute-done.9.hin, ...), custom_call_target="tpu_custom_call" | custom-call | flops 10000000 | bytes 3022848 | tf_op jit(solution)/shard_map/cot_one_base/pallas_call | solution.py:380
  42.6 3.3 %collective-permute-done.10.hout = f32[4,128,128]{2,1,0:T(8,128)S(1)} collective-permute-done((f32[4,128,128]{2,1,0:T(8,128)S(1)}, f32[4,128,128]{2,1,0:T(8,128)S(1)}, u32[]{:S(2)}, u32[]{:S(2)}) %collective-permute-start.10) | collective-permute-done | bytes 262176 | tf_op jit(solution)/shard_map/ppermute | solution.py:405
  45.9 0.1 sums_three.1
  46.0 1.9 %collective-permute-start.12 = (f32[4,128,128]{2,1,0:T(8,128)S(1)}, f32[4,128,128]{2,1,0:T(8,128)S(1)}, u32[]{:S(2)}, u32[]{:S(2)}) collective-permute-start(f32[4,128,128]{2,1,0:T(8,128)S(1)} %get-tuple-element.77.pk4), channel_id=1, source_target_pairs={{0,128},{128,0},{64,192},{192,64},{1,129},{129,1},{65,193},{193,65... | collective-permute-start | bytes 786440 | tf_op jit(solution)/shard_map/ppermute | solution.py:404
  47.8 0.0 collective-permute-done.8.got
  47.8 0.2 cot_one.1
  48.0 8.0 %collective-permute-start.11 = (f32[4,128,128]{2,1,0:T(8,128)S(1)}, f32[4,128,128]{2,1,0:T(8,128)S(1)}, u32[]{:S(2)}, u32[]{:S(2)}) collective-permute-start(f32[4,128,128]{2,1,0:T(8,128)S(1)} %get-tuple-element.76), channel_id=1, source_target_pairs={{0,64},{64,0},{128,192},{192,128},{1,65},{65,1},{129,193},{193,129... | collective-permute-start | bytes 786440 | tf_op jit(solution)/shard_map/ppermute | solution.py:403
  56.0 1.9 %collective-permute-start.13 = (f32[4,128,128]{2,1,0:T(8,128)S(1)}, f32[4,128,128]{2,1,0:T(8,128)S(1)}, u32[]{:S(2)}, u32[]{:S(2)}) collective-permute-start(f32[4,128,128]{2,1,0:T(8,128)S(1)} %get-tuple-element.80), channel_id=1, source_target_pairs={{64,1},{1,64},{192,129},{129,192},{65,2},{2,65},{193,130},{130,193... | collective-permute-start | bytes 786440 | tf_op jit(solution)/shard_map/ppermute | solution.py:405
  57.9 0.3 collective-permute-done.12.got
  58.2 0.1 total_push.1
  58.3 1.9 %collective-permute-start.14 = (f32[2,128,128]{2,1,0:T(8,128)S(1)}, f32[2,128,128]{2,1,0:T(8,128)S(1)}, u32[]{:S(2)}, u32[]{:S(2)}) collective-permute-start(f32[2,128,128]{2,1,0:T(8,128)S(1)} %get-tuple-element.81.tsum), channel_id=1, source_target_pairs={{0,64},{64,0},{128,192},{192,128},{1,65},{65,1},{129,193},{193,129... | collective-permute-start | bytes 393224 | tf_op jit(solution)/shard_map/ppermute | solution.py:403
  60.2 0.0 collective-permute-done.11.hin
  60.2 0.6 finish_base.1.base
  60.7 3.3 %collective-permute-done.13.hout = f32[4,128,128]{2,1,0:T(8,128)S(1)} collective-permute-done((f32[4,128,128]{2,1,0:T(8,128)S(1)}, f32[4,128,128]{2,1,0:T(8,128)S(1)}, u32[]{:S(2)}, u32[]{:S(2)}) %collective-permute-start.13) | collective-permute-done | bytes 262176 | tf_op jit(solution)/shard_map/ppermute | solution.py:405
  64.0 0.0 collective-permute-done.14.after.got
  64.0 0.1 finish.1
  64.1 2.8 %collective-permute-start.15 = (f32[4,128,128]{2,1,0:T(8,128)S(1)}, f32[4,128,128]{2,1,0:T(8,128)S(1)}, u32[]{:S(2)}, u32[]{:S(2)}) collective-permute-start(f32[4,128,128]{2,1,0:T(8,128)S(1)} %get-tuple-element.83), channel_id=1, source_target_pairs={{0,64},{64,0},{128,192},{192,128},{1,65},{65,1},{129,193},{193,129... | collective-permute-start | bytes 786440 | tf_op jit(solution)/shard_map/ppermute | solution.py:403
  66.8 0.8 %write_dep.1 = f32[2,4,128,128]{3,2,1,0:T(8,128)} custom-call(s32[1]{0:T(128)} %bitcast.core_ref, f32[16,128]{1,0:T(8,128)S(1)} %get-tuple-element.47.coef, f32[2,128,128]{2,1,0:T(8,128)S(1)} %get-tuple-element.81.tsum, f32[2,128,128]{2,1,0:T(8,128)S(1)} %collective-permute-done.14.after.got, f32[2,4,128,128]{3,2,1,0:T(8,128)S(1)} %copy-done.1), custom_call_target="tpu_custom_call" | custom-call | flops 10000000 | bytes 794624 | tf_op jit(solution)/shard_map/write_dep/pallas_call | solution.py:380
  67.7 0.3 collective-permute-done.15.got
  68.0 0.8 %write_conc.1 = f32[2,4,128,128]{3,2,1,0:T(8,128)} custom-call(s32[1]{0:T(128)} %bitcast.core_ref, f32[4,128,128]{2,1,0:T(8,128)S(1)} %get-tuple-element.82.own, f32[4,128,128]{2,1,0:T(8,128)S(1)} %collective-permute-done.15.got), custom_call_target="tpu_custom_call" | custom-call | flops 10000000 | bytes 524288 | tf_op jit(solution)/shard_map/write_conc/pallas_call | solution.py:380
  (4 shorter events, 0.1 us)
Async XLA Ops:
  0.6 0.7 copy-start.6
  0.7 0.7 copy-start.7
  0.7 0.7 copy-start.8
  1.3 1.0 %copy-start.3 = (f32[2,4,128,128]{3,2,1,0:T(8,128)S(1)}, f32[2,4,128,128]{3,2,1,0:T(8,128)}, u32[]{:S(2)}) copy-start(f32[2,4,128,128]{3,2,1,0:T(8,128)} %dep.1) | copy-start | bytes 1572868
  2.4 1.0 %copy-start.4 = (f32[2,4,128,128]{3,2,1,0:T(8,128)S(1)}, f32[2,4,128,128]{3,2,1,0:T(8,128)}, u32[]{:S(2)}) copy-start(f32[2,4,128,128]{3,2,1,0:T(8,128)} %conc.1) | copy-start | bytes 1572868
  3.4 1.4 %copy-start.1 = (f32[2,4,128,128]{3,2,1,0:T(8,128)S(1)}, f32[2,4,128,128]{3,2,1,0:T(8,128)}, u32[]{:S(2)}) copy-start(f32[2,4,128,128]{3,2,1,0:T(8,128)} %q.5) | copy-start | bytes 1572868
  3.4 1.4 %copy-start.2 = (f32[2,4,128,128]{3,2,1,0:T(8,128)S(1)}, f32[2,4,128,128]{3,2,1,0:T(8,128)}, u32[]{:S(2)}) copy-start(f32[2,4,128,128]{3,2,1,0:T(8,128)} %p.3) | copy-start | bytes 1572868
  4.1 2.4 %collective-permute-start = (f32[9,128,128]{2,1,0:T(8,128)S(1)}, f32[9,128,128]{2,1,0:T(8,128)S(1)}, u32[]{:S(2)}, u32[]{:S(2)}) collective-permute-start(f32[9,128,128]{2,1,0:T(8,128)S(1)} %get-tuple-element.46), channel_id=1, source_target_pairs={{0,64},{64,0},{128,192},{192,128},{1,65},{65,1},{129,193},{193,129... | collective-permute-start | bytes 1769480 | tf_op jit(solution)/shard_map/ppermute | solution.py:403
  4.9 8.1 %collective-permute-start.1 = (f32[10,128,128]{2,1,0:T(8,128)S(1)}, f32[10,128,128]{2,1,0:T(8,128)S(1)}, u32[]{:S(2)}, u32[]{:S(2)}) collective-permute-start(f32[10,128,128]{2,1,0:T(8,128)S(1)} %send_cot.1), channel_id=1, source_target_pairs={{0,64},{64,0},{128,192},{192,128},{1,65},{65,1},{129,193},{193,129... | collective-permute-start | bytes 1966088 | tf_op jit(solution)/shard_map/ppermute | solution.py:403
  6.5 6.1 %copy-start = (f32[4,128,128]{2,1,0:T(8,128)S(1)}, f32[4,128,128]{2,1,0:T(8,128)}, u32[]{:S(2)}) copy-start(f32[4,128,128]{2,1,0:T(8,128)} %vel.15) | copy-start | bytes 786436
  6.6 10.1 %collective-permute-start.2 = (f32[4,128,128]{2,1,0:T(8,128)S(1)}, f32[4,128,128]{2,1,0:T(8,128)S(1)}, u32[]{:S(2)}, u32[]{:S(2)}) collective-permute-start(f32[4,128,128]{2,1,0:T(8,128)S(1)} %get-tuple-element.52), channel_id=1, source_target_pairs={{64,1},{1,64},{192,129},{129,192},{65,2},{2,65},{193,130},{130,193... | collective-permute-start | bytes 786440 | tf_op jit(solution)/shard_map/ppermute | solution.py:405
  10.0 14.4 %collective-permute-start.4 = (f32[4,128,128]{2,1,0:T(8,128)S(1)}, f32[4,128,128]{2,1,0:T(8,128)S(1)}, u32[]{:S(2)}, u32[]{:S(2)}) collective-permute-start(f32[4,128,128]{2,1,0:T(8,128)S(1)} %get-tuple-element.55.pk1), channel_id=1, source_target_pairs={{0,128},{128,0},{64,192},{192,64},{1,129},{129,1},{65,193},{193,65... | collective-permute-start | bytes 786440 | tf_op jit(solution)/shard_map/ppermute | solution.py:404
  13.5 15.8 %collective-permute-start.5 = (f32[4,128,128]{2,1,0:T(8,128)S(1)}, f32[4,128,128]{2,1,0:T(8,128)S(1)}, u32[]{:S(2)}, u32[]{:S(2)}) collective-permute-start(f32[4,128,128]{2,1,0:T(8,128)S(1)} %get-tuple-element.61), channel_id=1, source_target_pairs={{64,1},{1,64},{192,129},{129,192},{65,2},{2,65},{193,130},{130,193... | collective-permute-start | bytes 786440 | tf_op jit(solution)/shard_map/ppermute | solution.py:405
  16.7 7.7 %copy-start.5 = (s32[4,128,128]{2,1,0:T(8,128)S(1)}, s32[4,128,128]{2,1,0:T(8,128)}, u32[]{:S(2)}) copy-start(s32[4,128,128]{2,1,0:T(8,128)} %label.1) | copy-start | bytes 786436
  16.9 19.0 %collective-permute-start.3 = (f32[4,128,128]{2,1,0:T(8,128)S(1)}, f32[4,128,128]{2,1,0:T(8,128)S(1)}, u32[]{:S(2)}, u32[]{:S(2)}) collective-permute-start(f32[4,128,128]{2,1,0:T(8,128)S(1)} %get-tuple-element.54.pk2), channel_id=1, source_target_pairs={{0,128},{128,0},{64,192},{192,64},{1,129},{129,1},{65,193},{193,65... | collective-permute-start | bytes 786440 | tf_op jit(solution)/shard_map/ppermute | solution.py:404
  24.6 14.9 %collective-permute-start.6 = (f32[4,128,128]{2,1,0:T(8,128)S(1)}, f32[4,128,128]{2,1,0:T(8,128)S(1)}, u32[]{:S(2)}, u32[]{:S(2)}) collective-permute-start(f32[4,128,128]{2,1,0:T(8,128)S(1)} %get-tuple-element.64), channel_id=1, source_target_pairs={{0,64},{64,0},{128,192},{192,128},{1,65},{65,1},{129,193},{193,129... | collective-permute-start | bytes 786440 | tf_op jit(solution)/shard_map/ppermute | solution.py:403
  27.3 12.9 %collective-permute-start.7 = (f32[4,128,128]{2,1,0:T(8,128)S(1)}, f32[4,128,128]{2,1,0:T(8,128)S(1)}, u32[]{:S(2)}, u32[]{:S(2)}) collective-permute-start(f32[4,128,128]{2,1,0:T(8,128)S(1)} %get-tuple-element.67), channel_id=1, source_target_pairs={{64,1},{1,64},{192,129},{129,192},{65,2},{2,65},{193,130},{130,193... | collective-permute-start | bytes 786440 | tf_op jit(solution)/shard_map/ppermute | solution.py:405
  36.2 5.6 %collective-permute-start.9 = (f32[4,128,128]{2,1,0:T(8,128)S(1)}, f32[4,128,128]{2,1,0:T(8,128)S(1)}, u32[]{:S(2)}, u32[]{:S(2)}) collective-permute-start(f32[4,128,128]{2,1,0:T(8,128)S(1)} %get-tuple-element.70), channel_id=1, source_target_pairs={{0,64},{64,0},{128,192},{192,128},{1,65},{65,1},{129,193},{193,129... | collective-permute-start | bytes 786440 | tf_op jit(solution)/shard_map/ppermute | solution.py:403
  36.3 9.6 %collective-permute-start.10 = (f32[4,128,128]{2,1,0:T(8,128)S(1)}, f32[4,128,128]{2,1,0:T(8,128)S(1)}, u32[]{:S(2)}, u32[]{:S(2)}) collective-permute-start(f32[4,128,128]{2,1,0:T(8,128)S(1)} %get-tuple-element.73), channel_id=1, source_target_pairs={{64,1},{1,64},{192,129},{129,192},{65,2},{2,65},{193,130},{130,193... | collective-permute-start | bytes 786440 | tf_op jit(solution)/shard_map/ppermute | solution.py:405
  40.3 7.6 %collective-permute-start.8 = (f32[2,128,128]{2,1,0:T(8,128)S(1)}, f32[2,128,128]{2,1,0:T(8,128)S(1)}, u32[]{:S(2)}, u32[]{:S(2)}) collective-permute-start(f32[2,128,128]{2,1,0:T(8,128)S(1)} %sums_two.1.pk3), channel_id=1, source_target_pairs={{0,128},{128,0},{64,192},{192,64},{1,129},{129,1},{65,193},{193,65... | collective-permute-start | bytes 393224 | tf_op jit(solution)/shard_map/ppermute | solution.py:404
  46.0 12.2 %collective-permute-start.12 = (f32[4,128,128]{2,1,0:T(8,128)S(1)}, f32[4,128,128]{2,1,0:T(8,128)S(1)}, u32[]{:S(2)}, u32[]{:S(2)}) collective-permute-start(f32[4,128,128]{2,1,0:T(8,128)S(1)} %get-tuple-element.77.pk4), channel_id=1, source_target_pairs={{0,128},{128,0},{64,192},{192,64},{1,129},{129,1},{65,193},{193,65... | collective-permute-start | bytes 786440 | tf_op jit(solution)/shard_map/ppermute | solution.py:404
  48.0 12.1 %collective-permute-start.11 = (f32[4,128,128]{2,1,0:T(8,128)S(1)}, f32[4,128,128]{2,1,0:T(8,128)S(1)}, u32[]{:S(2)}, u32[]{:S(2)}) collective-permute-start(f32[4,128,128]{2,1,0:T(8,128)S(1)} %get-tuple-element.76), channel_id=1, source_target_pairs={{0,64},{64,0},{128,192},{192,128},{1,65},{65,1},{129,193},{193,129... | collective-permute-start | bytes 786440 | tf_op jit(solution)/shard_map/ppermute | solution.py:403
  56.0 8.0 %collective-permute-start.13 = (f32[4,128,128]{2,1,0:T(8,128)S(1)}, f32[4,128,128]{2,1,0:T(8,128)S(1)}, u32[]{:S(2)}, u32[]{:S(2)}) collective-permute-start(f32[4,128,128]{2,1,0:T(8,128)S(1)} %get-tuple-element.80), channel_id=1, source_target_pairs={{64,1},{1,64},{192,129},{129,192},{65,2},{2,65},{193,130},{130,193... | collective-permute-start | bytes 786440 | tf_op jit(solution)/shard_map/ppermute | solution.py:405
  58.3 5.7 %collective-permute-start.14 = (f32[2,128,128]{2,1,0:T(8,128)S(1)}, f32[2,128,128]{2,1,0:T(8,128)S(1)}, u32[]{:S(2)}, u32[]{:S(2)}) collective-permute-start(f32[2,128,128]{2,1,0:T(8,128)S(1)} %get-tuple-element.81.tsum), channel_id=1, source_target_pairs={{0,64},{64,0},{128,192},{192,128},{1,65},{65,1},{129,193},{193,129... | collective-permute-start | bytes 393224 | tf_op jit(solution)/shard_map/ppermute | solution.py:403
  64.1 3.9 %collective-permute-start.15 = (f32[4,128,128]{2,1,0:T(8,128)S(1)}, f32[4,128,128]{2,1,0:T(8,128)S(1)}, u32[]{:S(2)}, u32[]{:S(2)}) collective-permute-start(f32[4,128,128]{2,1,0:T(8,128)S(1)} %get-tuple-element.83), channel_id=1, source_target_pairs={{0,64},{64,0},{128,192},{192,128},{1,65},{65,1},{129,193},{193,129... | collective-permute-start | bytes 786440 | tf_op jit(solution)/shard_map/ppermute | solution.py:403

commit v3 on v2

--- a/solution.py
+++ b/solution.py
@@ -11,7 +11,7 @@
 SURFACE_EFF = (0.1, 0.6, 1.2, 2.0)
 N = 128
 WORK = {
-    "send_state": 0.0,
+    "send_state": 0.01,
     "send_cot": 0.01,
     "sums_zero": 0.01,
     "sums_one": 0.01,
@@ -29,6 +29,8 @@
     "write_dep": 0.01,
     "write_conc": 0.01,
     "total_push": 0.01,
+    "kappa_zero": 2.0,
+    "cot_start": 3.0,
 }
 F32 = jnp.float32
 
@@ -85,7 +87,7 @@
         msg[3 * c + 2] = p[c, 2 - other]
 
 
-def sums_zero(core_ref, rows, theta, mine, got, pk1, ho, c0, coef, u4, uin):
+def sums_zero(core_ref, rows, theta, mine, got, pk1, ho, sums, coef, u4, uin):
     core = core_ref[0]
     for k in range(3):
         coef[4 * k : 4 * k + 2, :] = rows[2 * k : 2 * k + 2, :]
@@ -101,8 +103,8 @@
             term = (co.vol[c] * co.rate[c]) * u
             total = total + term
             square = square + co.rate[c] * term
-        pk1[2 + l] = total
-        c0[l] = square
+        sums[l] = total
+        sums[2 + l] = square
     for c in range(4):
         uin[c] = mine[3 * c + 2] if c < 2 else got[4 + 3 * (c - 2)]
         ho[(c + 2) % 4] = u4[c, core]
@@ -160,57 +162,55 @@
         base[c, 1 - core] = base[c, 1 - core] + (co.dif[c] + above) * pin
 
 
-def sums_one(core_ref, coef, base, hout, vel, c0, a4, pk2):
-    core = core_ref[0]
-    co = Coef(coef)
-    fout, _ = facing(co, vel, core)
-    for l in range(2):
-        for c in range(4):
-            a4[c, l] = base[c, l]
-    for c in range(4):
-        a4[c, core] = a4[c, core] + H * (fout[c] * hout[c])
-    for l in range(2):
-        total = jnp.zeros((N, N), F32)
-        for c in range(4):
-            total = total + (co.vol[c] * co.rate[c]) * a4[c, l]
-        pk2[l] = total
-        pk2[2 + l] = c0[l]
-
-
-def state_one(core_ref, coef, pk1, got, label, a4, u4, u1, ho, hi, k01, th, a0s):
-    core = core_ref[0]
-    co = Coef(coef)
+def kappa_zero(core_ref, pk1, got, label, k0s, th):
+    core = core_ref[0]
     for l in range(2):
         coll = efficiency(label[2 * core + l])
         theta = pk1[l] + got[l]
-        a0 = pk1[2 + l] + got[2 + l]
-        k0 = coll * jnp.exp(-theta)
-        theta1 = theta + H * (k0 * a0)
-        k01[l] = k0
-        k01[2 + l] = coll * jnp.exp(-theta1)
-        k01[4 + l] = coll
+        k0s[l] = coll * jnp.exp(-theta)
+        k0s[2 + l] = coll
         th[l] = theta
-        th[2 + l] = theta1
-        a0s[l] = a0
-        for c in range(4):
-            u1[c, l] = a4[c, l] - (H * k0) * (co.rate[c] * u4[c, l])
-    for c in range(4):
-        ho[(c + 2) % 4] = u1[c, core]
+
+
+def state_one(core_ref, coef, base, hout, vel, sums, k0s, u4, after, u1, ho, hi, pk2):
+    core = core_ref[0]
+    co = Coef(coef)
+    fout, _ = facing(co, vel, core)
+    halo = [H * (fout[c] * hout[c]) for c in range(4)]
+    extra = jnp.zeros((N, N), F32)
+    for c in range(4):
+        extra = extra + (co.vol[c] * co.rate[c]) * halo[c]
+    for l in range(2):
+        total = jnp.zeros((N, N), F32)
+        for c in range(4):
+            a = base[c, l]
+            total = total + (co.vol[c] * co.rate[c]) * a
+            u1[c, l] = a - (H * k0s[l]) * (co.rate[c] * u4[c, l])
+        pk2[l] = total
+        pk2[2 + l] = sums[2 + l]
+        pk2[4 + l] = sums[l]
+    pk2[core] = pk2[core] + extra
+    for c in range(4):
+        edge = u1[c, core] + halo[c]
+        u1[c, core] = edge
+        ho[(c + 2) % 4] = edge
         hi[(c + 2) % 4] = u1[c, 1 - core]
 
 
-def state_two(core_ref, coef, u4, u1, hin, k01, vel, p4, q4, part, wout):
+def state_two(core_ref, coef, u4, u1, hin, vel, p4, q4, part, wout):
     core = core_ref[0]
     co = Coef(coef)
     fout, fin = facing(co, vel, core)
     for l in range(2):
         total = jnp.zeros((N, N), F32)
+        react = jnp.zeros((N, N), F32)
         for c in range(4):
             u = u1[c, l]
-            rate = advect(co, u1, vel, core, c, l) - (co.rate[c] * k01[2 + l]) * u
-            u2 = 0.75 * u4[c, l] + 0.25 * (u + H * rate)
-            total = total + (co.rate[c] * (q4[c, l] - p4[c, l])) * u2
+            w = co.rate[c] * (q4[c, l] - p4[c, l])
+            total = total + w * (0.75 * u4[c, l] + 0.25 * (u + H * advect(co, u1, vel, core, c, l)))
+            react = react + (0.25 * H) * (w * (co.rate[c] * u))
         part[l] = total
+        part[2 + l] = react
     edge = part[1 - core]
     for c in range(4):
         scaled = (0.25 * H) * co.rate[c]
@@ -219,35 +219,47 @@
     part[1 - core] = edge
 
 
-def sums_two(core_ref, part, wout, hout, pk3):
-    core = core_ref[0]
-    edge = part[core]
+def sums_two(core_ref, part, wout, hout, k01, pk3):
+    core = core_ref[0]
+    for l in range(2):
+        pk3[l] = part[l] - k01[2 + l] * part[2 + l]
+    edge = pk3[core]
     for c in range(4):
         edge = edge + wout[c] * hout[c]
-    pk3[1 - core] = part[1 - core]
     pk3[core] = edge
 
 
-def cot_two(core_ref, coef, pk2, got, k01, th, a0, p4, q4, base, hout, vel, l2, ho, hi, k2s, sums):
+def cot_start(core_ref, p4, base, hout, start):
+    core = core_ref[0]
+    for c in range(4):
+        for l in range(2):
+            start[c, l] = (2.0 / 3.0) * p4[c, l] + (2.0 / 3.0 * H) * base[c, l]
+        start[c, core] = start[c, core] + (2.0 / 3.0 * H) * hout[c]
+
+
+def cot_two(core_ref, coef, pk2, got, k0s, th, p4, q4, base, vel, l2, ho, hi, k01, k2s, sums):
     core = core_ref[0]
     co = Coef(coef)
     fout, fin = facing(co, vel, core)
     for l in range(2):
+        k0 = k0s[l]
+        a0 = pk2[4 + l] + got[4 + l]
         c0 = pk2[2 + l] + got[2 + l]
-        a1 = (pk2[l] + got[l]) - (H * k01[l]) * c0
-        theta2 = 0.75 * th[l] + 0.25 * (th[2 + l] + H * (k01[2 + l] * a1))
-        k2 = k01[4 + l] * jnp.exp(-theta2)
+        theta1 = th[l] + H * (k0 * a0)
+        k1 = k0s[2 + l] * jnp.exp(-theta1)
+        k01[l] = k0
+        k01[2 + l] = k1
+        a1 = (pk2[l] + got[l]) - (H * k0) * c0
+        theta2 = 0.75 * th[l] + 0.25 * (theta1 + H * (k1 * a1))
+        k2 = k0s[2 + l] * jnp.exp(-theta2)
         k2s[l] = k2
-        sums[l] = a0[l]
+        sums[l] = a0
         sums[2 + l] = a1
         sums[4 + l] = c0
         for c in range(4):
             p = p4[c, l]
-            l2[c, l] = (2.0 / 3.0) * p + (2.0 / 3.0 * H) * (
-                base[c, l] + (co.rate[c] * k2) * (q4[c, l] - p)
-            )
-    for c in range(4):
-        l2[c, core] = l2[c, core] + (2.0 / 3.0 * H) * hout[c]
+            l2[c, l] = base[c, l] + (2.0 / 3.0 * H) * ((co.rate[c] * k2) * (q4[c, l] - p))
+    for c in range(4):
         ho[(c + 2) % 4] = fout[c] * l2[c, core]
         hi[(c + 2) % 4] = fin[c] * l2[c, 1 - core]
 
@@ -416,9 +428,9 @@
     got0 = inner(msg0)
     (msg1,) = call(send_cot, [layers(10)], (core,), (p, q))
     got1 = inner(msg1)
-    pk1, ho0, c0, coef, u4, uin = call(
+    pk1, ho0, csums, coef, u4, uin = call(
         sums_zero,
-        [layers(4), layers(4), layers(2), (16, N), eight, layers(4)],
+        [layers(2), layers(4), layers(4), (16, N), eight, layers(4)],
         (core,),
         (rows, theta, mine, got0),
     )
@@ -429,28 +441,29 @@
         cot_base, [eight, eight, eight, layers(4)], (core,), (coef, p, q, got1, velocity)
     )
     hp = outer(hop)
-    a4, pk2 = call(sums_one, [eight, layers(4)], (core,), (coef, abase, hu0, velocity, c0))
+    k0s, th = call(kappa_zero, [layers(4), layers(2)], (core,), (pk1, gpk1, label))
+    u1, ho1, hi1, pk2 = call(
+        state_one,
+        [eight, layers(4), layers(4), layers(6)],
+        (core,),
+        (coef, abase, hu0, velocity, csums, k0s, u4, pbase),
+    )
     gpk2 = across(pk2)
-    u1, ho1, hi1, k01, th, a0 = call(
-        state_one,
-        [eight, layers(4), layers(4), layers(6), layers(4), layers(2)],
-        (core,),
-        (coef, pk1, gpk1, label, a4, u4),
-    )
     iu1 = inner(hi1)
     hu1 = outer(ho1)
     part2, wout = call(
-        state_two, [layers(2), layers(4)], (core,), (coef, u4, u1, iu1, k01, velocity, p4, q4)
-    )
-    l2, ho2, hi2, k2s, sums = call(
+        state_two, [layers(4), layers(4)], (core,), (coef, u4, u1, iu1, velocity, p4, q4)
+    )
+    (l2start,) = call(cot_start, [eight], (core,), (p4, pbase, hp))
+    l2, ho2, hi2, k01, k2s, sums = call(
         cot_two,
-        [eight, layers(4), layers(4), layers(2), layers(6)],
+        [eight, layers(4), layers(4), layers(4), layers(2), layers(6)],
         (core,),
-        (coef, pk2, gpk2, k01, th, a0, p4, q4, pbase, hp, velocity),
+        (coef, pk2, gpk2, k0s, th, p4, q4, l2start, velocity),
     )
     il2 = inner(hi2)
     hl2 = outer(ho2)
-    (pk3,) = call(sums_two, [layers(2)], (core,), (part2, wout, hu1))
+    (pk3,) = call(sums_two, [layers(2)], (core,), (part2, wout, hu1, k01))
     gpk3 = across(pk3)
     l1base, part1 = call(
         cot_one_base, [eight, layers(4)], (core,), (coef, l2, il2, k01, velocity, q4, u1, u4)

time: 69.2 us -> 67.4 us (0.974)
  the two profiles are of different devices: /device:TPU:97 before, /device:TPU:129 now
where the time goes in v3:
time: 67.4 us; the launch traced here: 67.1 us
  starting transfers between devices  32.7 us (49%)
  waiting for transfers between devices  24 us (36%)
  Pallas kernels  6.71 us (10%)
  local copies, waits for them, and re-layouts  2.76 us (4%)
  between operations  0.87 us (1%)
    ppermute x7, starting transfers between devices, shards(): inner = lambda x: lax.ppermute(x, 'size', swap)  15.3 us
    ppermute x4, waiting for transfers between devices, shards(): across = lambda x: lax.ppermute(x, 'size', far)  12 us
    ppermute x5, starting transfers between devices, shards(): outer = lambda x: lax.ppermute(x, ('size', 'gz'), face)  11.3 us
    ppermute x5, waiting for transfers between devices, shards(): outer = lambda x: lax.ppermute(x, ('size', 'gz'), face)  10.7 us
    pallas_call x19, Pallas kernels, call(): pl.pallas_call(body, out_shape=[jax.ShapeDtypeStruct(s, F32) for s in out...  6.71 us
    ppermute x4, starting transfers between devices, shards(): across = lambda x: lax.ppermute(x, 'size', far)  6.19 us
    unnamed x18, local copies, waits for them, and re-layouts  2.76 us
    ppermute x7, waiting for transfers between devices, shards(): inner = lambda x: lax.ppermute(x, 'size', swap)  1.36 us
  transfers between devices with their start and end apart: 16, of which 8 were waited for; matrix products, arithmetic and copies ran while one was open for 0% of the time, Pallas kernels for 8%

profile of v3, /device:TPU:129, one launch (start us, length us, event | category | flops | bytes accessed | tf_op | source)
XLA Modules:
  0.0 67.1 jit_solution(6139623171923048277)
XLA Ops:
  0.6 0.0 copy-start.5
  0.7 0.0 copy-start.6
  0.7 0.0 copy-start.7
  0.7 0.6 copy-done.5
  1.3 0.0 copy-done.6
  1.3 0.0 copy-done.7
  1.3 0.0 copy-start.3
  1.3 1.0 %copy-done.3 = f32[2,4,128,128]{3,2,1,0:T(8,128)S(1)} copy-done((f32[2,4,128,128]{3,2,1,0:T(8,128)S(1)}, f32[2,4,128,128]{3,2,1,0:T(8,128)}, u32[]{:S(2)}) %copy-start.3) | copy-done | bytes 524312
  2.4 1.0 %copy-done.4 = f32[2,4,128,128]{3,2,1,0:T(8,128)S(1)} copy-done((f32[2,4,128,128]{3,2,1,0:T(8,128)S(1)}, f32[2,4,128,128]{3,2,1,0:T(8,128)}, u32[]{:S(2)}) %copy-start.4) | copy-done | bytes 524312
  3.4 0.6 send_state.1
  4.1 0.8 %collective-permute-start = (f32[9,128,128]{2,1,0:T(8,128)S(1)}, f32[9,128,128]{2,1,0:T(8,128)S(1)}, u32[]{:S(2)}, u32[]{:S(2)}) collective-permute-start(f32[9,128,128]{2,1,0:T(8,128)S(1)} %get-tuple-element.45), channel_id=1, source_target_pairs={{0,64},{64,0},{128,192},{192,128},{1,65},{65,1},{129,193},{193,129... | collective-permute-start | bytes 1769480 | tf_op jit(solution)/shard_map/ppermute | solution.py:415
  4.8 0.0 copy-done.1
  4.8 0.0 copy-done.2
  4.9 0.5 collective-permute-start.1
  5.4 1.0 %collective-permute-done.got = f32[9,128,128]{2,1,0:T(8,128)S(1)} collective-permute-done((f32[9,128,128]{2,1,0:T(8,128)S(1)}, f32[9,128,128]{2,1,0:T(8,128)S(1)}, u32[]{:S(2)}, u32[]{:S(2)}) %collective-permute-start) | collective-permute-done | bytes 589856 | tf_op jit(solution)/shard_map/ppermute | solution.py:415
  6.5 0.1 sums_zero.1
  6.6 2.8 %collective-permute-start.3 = (f32[2,128,128]{2,1,0:T(8,128)S(1)}, f32[2,128,128]{2,1,0:T(8,128)S(1)}, u32[]{:S(2)}, u32[]{:S(2)}) collective-permute-start(f32[2,128,128]{2,1,0:T(8,128)S(1)} %get-tuple-element.53.pk1), channel_id=1, source_target_pairs={{0,128},{128,0},{64,192},{192,64},{1,129},{129,1},{65,193},{193,65... | collective-permute-start | bytes 393224 | tf_op jit(solution)/shard_map/ppermute | solution.py:416
  9.4 2.7 %collective-permute-start.2 = (f32[4,128,128]{2,1,0:T(8,128)S(1)}, f32[4,128,128]{2,1,0:T(8,128)S(1)}, u32[]{:S(2)}, u32[]{:S(2)}) collective-permute-start(f32[4,128,128]{2,1,0:T(8,128)S(1)} %get-tuple-element.51), channel_id=1, source_target_pairs={{64,1},{1,64},{192,129},{129,192},{65,2},{2,65},{193,130},{130,193... | collective-permute-start | bytes 786440 | tf_op jit(solution)/shard_map/ppermute | solution.py:417
  12.2 0.0 copy-done
  12.2 0.4 step_base.1.base
  12.6 0.0 copy-start.8
  12.6 0.0 collective-permute-done.1.got
  12.7 0.5 cot_base.1
  13.2 2.8 %collective-permute-start.5 = (f32[4,128,128]{2,1,0:T(8,128)S(1)}, f32[4,128,128]{2,1,0:T(8,128)S(1)}, u32[]{:S(2)}, u32[]{:S(2)}) collective-permute-start(f32[4,128,128]{2,1,0:T(8,128)S(1)} %get-tuple-element.58), channel_id=1, source_target_pairs={{64,1},{1,64},{192,129},{129,192},{65,2},{2,65},{193,130},{130,193... | collective-permute-start | bytes 786440 | tf_op jit(solution)/shard_map/ppermute | solution.py:417
  16.0 0.0 collective-permute-done.3.got
  16.0 0.0 copy-done.8
  16.0 0.1 kappa_zero.1
  16.1 3.2 %collective-permute-done.2.hout = f32[4,128,128]{2,1,0:T(8,128)S(1)} collective-permute-done((f32[4,128,128]{2,1,0:T(8,128)S(1)}, f32[4,128,128]{2,1,0:T(8,128)S(1)}, u32[]{:S(2)}, u32[]{:S(2)}) %collective-permute-start.2) | collective-permute-done | bytes 262176 | tf_op jit(solution)/shard_map/ppermute | solution.py:417
  19.2 0.3 state_one.1
  19.5 1.6 %collective-permute-start.4 = (f32[6,128,128]{2,1,0:T(8,128)S(1)}, f32[6,128,128]{2,1,0:T(8,128)S(1)}, u32[]{:S(2)}, u32[]{:S(2)}) collective-permute-start(f32[6,128,128]{2,1,0:T(8,128)S(1)} %get-tuple-element.56.pk2), channel_id=1, source_target_pairs={{0,128},{128,0},{64,192},{192,64},{1,129},{129,1},{65,193},{193,65... | collective-permute-start | bytes 1179656 | tf_op jit(solution)/shard_map/ppermute | solution.py:416
  21.2 1.8 %collective-permute-start.6 = (f32[4,128,128]{2,1,0:T(8,128)S(1)}, f32[4,128,128]{2,1,0:T(8,128)S(1)}, u32[]{:S(2)}, u32[]{:S(2)}) collective-permute-start(f32[4,128,128]{2,1,0:T(8,128)S(1)} %get-tuple-element.61), channel_id=1, source_target_pairs={{0,64},{64,0},{128,192},{192,128},{1,65},{65,1},{129,193},{193,129... | collective-permute-start | bytes 786440 | tf_op jit(solution)/shard_map/ppermute | solution.py:415
  23.0 1.9 %collective-permute-start.7 = (f32[4,128,128]{2,1,0:T(8,128)S(1)}, f32[4,128,128]{2,1,0:T(8,128)S(1)}, u32[]{:S(2)}, u32[]{:S(2)}) collective-permute-start(f32[4,128,128]{2,1,0:T(8,128)S(1)} %get-tuple-element.64), channel_id=1, source_target_pairs={{64,1},{1,64},{192,129},{129,192},{65,2},{2,65},{193,130},{130,193... | collective-permute-start | bytes 786440 | tf_op jit(solution)/shard_map/ppermute | solution.py:417
  24.9 0.4 collective-permute-done.5.hout
  25.2 0.1 cot_start.1.base
  25.4 11.6 %collective-permute-done.4.got = f32[6,128,128]{2,1,0:T(8,128)S(1)} collective-permute-done((f32[6,128,128]{2,1,0:T(8,128)S(1)}, f32[6,128,128]{2,1,0:T(8,128)S(1)}, u32[]{:S(2)}, u32[]{:S(2)}) %collective-permute-start.4) | collective-permute-done | bytes 393248 | tf_op jit(solution)/shard_map/ppermute | solution.py:416
  37.0 0.3 cot_two.1
  37.3 1.9 %collective-permute-start.9 = (f32[4,128,128]{2,1,0:T(8,128)S(1)}, f32[4,128,128]{2,1,0:T(8,128)S(1)}, u32[]{:S(2)}, u32[]{:S(2)}) collective-permute-start(f32[4,128,128]{2,1,0:T(8,128)S(1)} %get-tuple-element.68), channel_id=1, source_target_pairs={{0,64},{64,0},{128,192},{192,128},{1,65},{65,1},{129,193},{193,129... | collective-permute-start | bytes 786440 | tf_op jit(solution)/shard_map/ppermute | solution.py:415
  39.3 1.9 %collective-permute-start.10 = (f32[4,128,128]{2,1,0:T(8,128)S(1)}, f32[4,128,128]{2,1,0:T(8,128)S(1)}, u32[]{:S(2)}, u32[]{:S(2)}) collective-permute-start(f32[4,128,128]{2,1,0:T(8,128)S(1)} %get-tuple-element.71), channel_id=1, source_target_pairs={{64,1},{1,64},{192,129},{129,192},{65,2},{2,65},{193,130},{130,193... | collective-permute-start | bytes 786440 | tf_op jit(solution)/shard_map/ppermute | solution.py:417
  41.2 0.0 collective-permute-done.6.hin
  41.2 0.7 %state_two.1 = (f32[4,128,128]{2,1,0:T(8,128)S(1)}, f32[4,128,128]{2,1,0:T(8,128)S(1)}) custom-call(s32[1]{0:T(128)} %bitcast.core_ref, f32[16,128]{1,0:T(8,128)S(1)} %get-tuple-element.46.coef, f32[4,2,128,128]{3,2,1,0:T(8,128)S(1)} %get-tuple-element.49.u4, f32[4,2,128,128]{3,2,1,0:T(8,128)S(1)} %get-tuple-element.60.u1, ...), custom_call_target="tpu_custom_call" | custom-call | flops 10000000 | bytes 2629632 | tf_op jit(solution)/shard_map/state_two/pallas_call | solution.py:392
  41.9 0.0 collective-permute-done.7.hout
  41.9 0.1 sums_two.1.pk3
  42.0 0.4 collective-permute-start.8
  42.4 0.0 collective-permute-done.9.hin
  42.4 0.8 %cot_one_base.1 = (f32[4,2,128,128]{3,2,1,0:T(8,128)S(1)}, f32[4,128,128]{2,1,0:T(8,128)S(1)}) custom-call(s32[1]{0:T(128)} %bitcast.core_ref, f32[16,128]{1,0:T(8,128)S(1)} %get-tuple-element.46.coef, f32[4,2,128,128]{3,2,1,0:T(8,128)S(1)} %get-tuple-element.59.l2, f32[4,128,128]{2,1,0:T(8,128)S(1)} %collective-permute-done.9.hin, ...), custom_call_target="tpu_custom_call" | custom-call | flops 10000000 | bytes 2891776 | tf_op jit(solution)/shard_map/cot_one_base/pallas_call | solution.py:392
  43.2 5.2 %collective-permute-done.10.hout = f32[4,128,128]{2,1,0:T(8,128)S(1)} collective-permute-done((f32[4,128,128]{2,1,0:T(8,128)S(1)}, f32[4,128,128]{2,1,0:T(8,128)S(1)}, u32[]{:S(2)}, u32[]{:S(2)}) %collective-permute-start.10) | collective-permute-done | bytes 262176 | tf_op jit(solution)/shard_map/ppermute | solution.py:417
  48.4 0.1 sums_three.1
  48.5 1.3 %collective-permute-start.12 = (f32[4,128,128]{2,1,0:T(8,128)S(1)}, f32[4,128,128]{2,1,0:T(8,128)S(1)}, u32[]{:S(2)}, u32[]{:S(2)}) collective-permute-start(f32[4,128,128]{2,1,0:T(8,128)S(1)} %get-tuple-element.75.pk4), channel_id=1, source_target_pairs={{0,128},{128,0},{64,192},{192,64},{1,129},{129,1},{65,193},{193,65... | collective-permute-start | bytes 786440 | tf_op jit(solution)/shard_map/ppermute | solution.py:416
  49.7 0.0 collective-permute-done.8.got
  49.7 0.2 cot_one.1
  49.9 3.0 %collective-permute-start.11 = (f32[4,128,128]{2,1,0:T(8,128)S(1)}, f32[4,128,128]{2,1,0:T(8,128)S(1)}, u32[]{:S(2)}, u32[]{:S(2)}) collective-permute-start(f32[4,128,128]{2,1,0:T(8,128)S(1)} %get-tuple-element.74), channel_id=1, source_target_pairs={{0,64},{64,0},{128,192},{192,128},{1,65},{65,1},{129,193},{193,129... | collective-permute-start | bytes 786440 | tf_op jit(solution)/shard_map/ppermute | solution.py:415
  52.9 1.9 %collective-permute-start.13 = (f32[4,128,128]{2,1,0:T(8,128)S(1)}, f32[4,128,128]{2,1,0:T(8,128)S(1)}, u32[]{:S(2)}, u32[]{:S(2)}) collective-permute-start(f32[4,128,128]{2,1,0:T(8,128)S(1)} %get-tuple-element.78), channel_id=1, source_target_pairs={{64,1},{1,64},{192,129},{129,192},{65,2},{2,65},{193,130},{130,193... | collective-permute-start | bytes 786440 | tf_op jit(solution)/shard_map/ppermute | solution.py:417
  54.9 0.4 collective-permute-done.12.got
  55.3 0.1 total_push.1
  55.4 4.9 %collective-permute-start.14 = (f32[2,128,128]{2,1,0:T(8,128)S(1)}, f32[2,128,128]{2,1,0:T(8,128)S(1)}, u32[]{:S(2)}, u32[]{:S(2)}) collective-permute-start(f32[2,128,128]{2,1,0:T(8,128)S(1)} %get-tuple-element.79.tsum), channel_id=1, source_target_pairs={{0,64},{64,0},{128,192},{192,128},{1,65},{65,1},{129,193},{193,129... | collective-permute-start | bytes 393224 | tf_op jit(solution)/shard_map/ppermute | solution.py:415
  60.3 0.0 collective-permute-done.11.hin
  60.3 0.6 finish_base.1.base
  60.9 1.9 %collective-permute-done.13.hout = f32[4,128,128]{2,1,0:T(8,128)S(1)} collective-permute-done((f32[4,128,128]{2,1,0:T(8,128)S(1)}, f32[4,128,128]{2,1,0:T(8,128)S(1)}, u32[]{:S(2)}, u32[]{:S(2)}) %collective-permute-start.13) | collective-permute-done | bytes 262176 | tf_op jit(solution)/shard_map/ppermute | solution.py:417
  62.8 0.0 collective-permute-done.14.after.got
  62.8 0.1 finish.1
  62.8 2.3 %collective-permute-start.15 = (f32[4,128,128]{2,1,0:T(8,128)S(1)}, f32[4,128,128]{2,1,0:T(8,128)S(1)}, u32[]{:S(2)}, u32[]{:S(2)}) collective-permute-start(f32[4,128,128]{2,1,0:T(8,128)S(1)} %get-tuple-element.81), channel_id=1, source_target_pairs={{0,64},{64,0},{128,192},{192,128},{1,65},{65,1},{129,193},{193,129... | collective-permute-start | bytes 786440 | tf_op jit(solution)/shard_map/ppermute | solution.py:415
  65.1 0.8 %write_dep.1 = f32[2,4,128,128]{3,2,1,0:T(8,128)} custom-call(s32[1]{0:T(128)} %bitcast.core_ref, f32[16,128]{1,0:T(8,128)S(1)} %get-tuple-element.46.coef, f32[2,128,128]{2,1,0:T(8,128)S(1)} %get-tuple-element.79.tsum, f32[2,128,128]{2,1,0:T(8,128)S(1)} %collective-permute-done.14.after.got, f32[2,4,128,128]{3,2,1,0:T(8,128)S(1)} %copy-done.1), custom_call_target="tpu_custom_call" | custom-call | flops 10000000 | bytes 794624 | tf_op jit(solution)/shard_map/write_dep/pallas_call | solution.py:392
  66.0 0.3 collective-permute-done.15.got
  66.3 0.8 %write_conc.1 = f32[2,4,128,128]{3,2,1,0:T(8,128)} custom-call(s32[1]{0:T(128)} %bitcast.core_ref, f32[4,128,128]{2,1,0:T(8,128)S(1)} %get-tuple-element.80.own, f32[4,128,128]{2,1,0:T(8,128)S(1)} %collective-permute-done.15.got), custom_call_target="tpu_custom_call" | custom-call | flops 10000000 | bytes 524288 | tf_op jit(solution)/shard_map/write_conc/pallas_call | solution.py:392
  (5 shorter events, 0.0 us)
Async XLA Ops:
  0.6 0.7 copy-start.5
  0.7 0.7 copy-start.6
  0.7 0.7 copy-start.7
  1.3 1.0 %copy-start.3 = (f32[2,4,128,128]{3,2,1,0:T(8,128)S(1)}, f32[2,4,128,128]{3,2,1,0:T(8,128)}, u32[]{:S(2)}) copy-start(f32[2,4,128,128]{3,2,1,0:T(8,128)} %dep.1) | copy-start | bytes 1572868
  2.4 1.0 %copy-start.4 = (f32[2,4,128,128]{3,2,1,0:T(8,128)S(1)}, f32[2,4,128,128]{3,2,1,0:T(8,128)}, u32[]{:S(2)}) copy-start(f32[2,4,128,128]{3,2,1,0:T(8,128)} %conc.1) | copy-start | bytes 1572868
  3.4 1.4 %copy-start.1 = (f32[2,4,128,128]{3,2,1,0:T(8,128)S(1)}, f32[2,4,128,128]{3,2,1,0:T(8,128)}, u32[]{:S(2)}) copy-start(f32[2,4,128,128]{3,2,1,0:T(8,128)} %q.5) | copy-start | bytes 1572868
  3.4 1.4 %copy-start.2 = (f32[2,4,128,128]{3,2,1,0:T(8,128)S(1)}, f32[2,4,128,128]{3,2,1,0:T(8,128)}, u32[]{:S(2)}) copy-start(f32[2,4,128,128]{3,2,1,0:T(8,128)} %p.3) | copy-start | bytes 1572868
  4.1 2.4 %collective-permute-start = (f32[9,128,128]{2,1,0:T(8,128)S(1)}, f32[9,128,128]{2,1,0:T(8,128)S(1)}, u32[]{:S(2)}, u32[]{:S(2)}) collective-permute-start(f32[9,128,128]{2,1,0:T(8,128)S(1)} %get-tuple-element.45), channel_id=1, source_target_pairs={{0,64},{64,0},{128,192},{192,128},{1,65},{65,1},{129,193},{193,129... | collective-permute-start | bytes 1769480 | tf_op jit(solution)/shard_map/ppermute | solution.py:415
  4.9 7.8 %collective-permute-start.1 = (f32[10,128,128]{2,1,0:T(8,128)S(1)}, f32[10,128,128]{2,1,0:T(8,128)S(1)}, u32[]{:S(2)}, u32[]{:S(2)}) collective-permute-start(f32[10,128,128]{2,1,0:T(8,128)S(1)} %send_cot.1), channel_id=1, source_target_pairs={{0,64},{64,0},{128,192},{192,128},{1,65},{65,1},{129,193},{193,129... | collective-permute-start | bytes 1966088 | tf_op jit(solution)/shard_map/ppermute | solution.py:415
  6.5 5.7 %copy-start = (f32[4,128,128]{2,1,0:T(8,128)S(1)}, f32[4,128,128]{2,1,0:T(8,128)}, u32[]{:S(2)}) copy-start(f32[4,128,128]{2,1,0:T(8,128)} %vel.15) | copy-start | bytes 786436
  6.6 9.4 %collective-permute-start.3 = (f32[2,128,128]{2,1,0:T(8,128)S(1)}, f32[2,128,128]{2,1,0:T(8,128)S(1)}, u32[]{:S(2)}, u32[]{:S(2)}) collective-permute-start(f32[2,128,128]{2,1,0:T(8,128)S(1)} %get-tuple-element.53.pk1), channel_id=1, source_target_pairs={{0,128},{128,0},{64,192},{192,64},{1,129},{129,1},{65,193},{193,65... | collective-permute-start | bytes 393224 | tf_op jit(solution)/shard_map/ppermute | solution.py:416
  9.4 9.8 %collective-permute-start.2 = (f32[4,128,128]{2,1,0:T(8,128)S(1)}, f32[4,128,128]{2,1,0:T(8,128)S(1)}, u32[]{:S(2)}, u32[]{:S(2)}) collective-permute-start(f32[4,128,128]{2,1,0:T(8,128)S(1)} %get-tuple-element.51), channel_id=1, source_target_pairs={{64,1},{1,64},{192,129},{129,192},{65,2},{2,65},{193,130},{130,193... | collective-permute-start | bytes 786440 | tf_op jit(solution)/shard_map/ppermute | solution.py:417
  12.6 3.4 %copy-start.8 = (s32[4,128,128]{2,1,0:T(8,128)S(1)}, s32[4,128,128]{2,1,0:T(8,128)}, u32[]{:S(2)}) copy-start(s32[4,128,128]{2,1,0:T(8,128)} %label.1) | copy-start | bytes 786436
  13.2 12.1 %collective-permute-start.5 = (f32[4,128,128]{2,1,0:T(8,128)S(1)}, f32[4,128,128]{2,1,0:T(8,128)S(1)}, u32[]{:S(2)}, u32[]{:S(2)}) collective-permute-start(f32[4,128,128]{2,1,0:T(8,128)S(1)} %get-tuple-element.58), channel_id=1, source_target_pairs={{64,1},{1,64},{192,129},{129,192},{65,2},{2,65},{193,130},{130,193... | collective-permute-start | bytes 786440 | tf_op jit(solution)/shard_map/ppermute | solution.py:417
  19.5 17.5 %collective-permute-start.4 = (f32[6,128,128]{2,1,0:T(8,128)S(1)}, f32[6,128,128]{2,1,0:T(8,128)S(1)}, u32[]{:S(2)}, u32[]{:S(2)}) collective-permute-start(f32[6,128,128]{2,1,0:T(8,128)S(1)} %get-tuple-element.56.pk2), channel_id=1, source_target_pairs={{0,128},{128,0},{64,192},{192,64},{1,129},{129,1},{65,193},{193,65... | collective-permute-start | bytes 1179656 | tf_op jit(solution)/shard_map/ppermute | solution.py:416
  21.2 20.0 %collective-permute-start.6 = (f32[4,128,128]{2,1,0:T(8,128)S(1)}, f32[4,128,128]{2,1,0:T(8,128)S(1)}, u32[]{:S(2)}, u32[]{:S(2)}) collective-permute-start(f32[4,128,128]{2,1,0:T(8,128)S(1)} %get-tuple-element.61), channel_id=1, source_target_pairs={{0,64},{64,0},{128,192},{192,128},{1,65},{65,1},{129,193},{193,129... | collective-permute-start | bytes 786440 | tf_op jit(solution)/shard_map/ppermute | solution.py:415
  23.0 18.9 %collective-permute-start.7 = (f32[4,128,128]{2,1,0:T(8,128)S(1)}, f32[4,128,128]{2,1,0:T(8,128)S(1)}, u32[]{:S(2)}, u32[]{:S(2)}) collective-permute-start(f32[4,128,128]{2,1,0:T(8,128)S(1)} %get-tuple-element.64), channel_id=1, source_target_pairs={{64,1},{1,64},{192,129},{129,192},{65,2},{2,65},{193,130},{130,193... | collective-permute-start | bytes 786440 | tf_op jit(solution)/shard_map/ppermute | solution.py:417
  37.3 5.1 %collective-permute-start.9 = (f32[4,128,128]{2,1,0:T(8,128)S(1)}, f32[4,128,128]{2,1,0:T(8,128)S(1)}, u32[]{:S(2)}, u32[]{:S(2)}) collective-permute-start(f32[4,128,128]{2,1,0:T(8,128)S(1)} %get-tuple-element.68), channel_id=1, source_target_pairs={{0,64},{64,0},{128,192},{192,128},{1,65},{65,1},{129,193},{193,129... | collective-permute-start | bytes 786440 | tf_op jit(solution)/shard_map/ppermute | solution.py:415
  39.3 9.1 %collective-permute-start.10 = (f32[4,128,128]{2,1,0:T(8,128)S(1)}, f32[4,128,128]{2,1,0:T(8,128)S(1)}, u32[]{:S(2)}, u32[]{:S(2)}) collective-permute-start(f32[4,128,128]{2,1,0:T(8,128)S(1)} %get-tuple-element.71), channel_id=1, source_target_pairs={{64,1},{1,64},{192,129},{129,192},{65,2},{2,65},{193,130},{130,193... | collective-permute-start | bytes 786440 | tf_op jit(solution)/shard_map/ppermute | solution.py:417
  42.0 7.8 %collective-permute-start.8 = (f32[2,128,128]{2,1,0:T(8,128)S(1)}, f32[2,128,128]{2,1,0:T(8,128)S(1)}, u32[]{:S(2)}, u32[]{:S(2)}) collective-permute-start(f32[2,128,128]{2,1,0:T(8,128)S(1)} %sums_two.1.pk3), channel_id=1, source_target_pairs={{0,128},{128,0},{64,192},{192,64},{1,129},{129,1},{65,193},{193,65... | collective-permute-start | bytes 393224 | tf_op jit(solution)/shard_map/ppermute | solution.py:416
  48.5 6.8 %collective-permute-start.12 = (f32[4,128,128]{2,1,0:T(8,128)S(1)}, f32[4,128,128]{2,1,0:T(8,128)S(1)}, u32[]{:S(2)}, u32[]{:S(2)}) collective-permute-start(f32[4,128,128]{2,1,0:T(8,128)S(1)} %get-tuple-element.75.pk4), channel_id=1, source_target_pairs={{0,128},{128,0},{64,192},{192,64},{1,129},{129,1},{65,193},{193,65... | collective-permute-start | bytes 786440 | tf_op jit(solution)/shard_map/ppermute | solution.py:416
  49.9 10.3 %collective-permute-start.11 = (f32[4,128,128]{2,1,0:T(8,128)S(1)}, f32[4,128,128]{2,1,0:T(8,128)S(1)}, u32[]{:S(2)}, u32[]{:S(2)}) collective-permute-start(f32[4,128,128]{2,1,0:T(8,128)S(1)} %get-tuple-element.74), channel_id=1, source_target_pairs={{0,64},{64,0},{128,192},{192,128},{1,65},{65,1},{129,193},{193,129... | collective-permute-start | bytes 786440 | tf_op jit(solution)/shard_map/ppermute | solution.py:415
  52.9 9.8 %collective-permute-start.13 = (f32[4,128,128]{2,1,0:T(8,128)S(1)}, f32[4,128,128]{2,1,0:T(8,128)S(1)}, u32[]{:S(2)}, u32[]{:S(2)}) collective-permute-start(f32[4,128,128]{2,1,0:T(8,128)S(1)} %get-tuple-element.78), channel_id=1, source_target_pairs={{64,1},{1,64},{192,129},{129,192},{65,2},{2,65},{193,130},{130,193... | collective-permute-start | bytes 786440 | tf_op jit(solution)/shard_map/ppermute | solution.py:417
  55.4 7.4 %collective-permute-start.14 = (f32[2,128,128]{2,1,0:T(8,128)S(1)}, f32[2,128,128]{2,1,0:T(8,128)S(1)}, u32[]{:S(2)}, u32[]{:S(2)}) collective-permute-start(f32[2,128,128]{2,1,0:T(8,128)S(1)} %get-tuple-element.79.tsum), channel_id=1, source_target_pairs={{0,64},{64,0},{128,192},{192,128},{1,65},{65,1},{129,193},{193,129... | collective-permute-start | bytes 393224 | tf_op jit(solution)/shard_map/ppermute | solution.py:415
  62.8 3.5 %collective-permute-start.15 = (f32[4,128,128]{2,1,0:T(8,128)S(1)}, f32[4,128,128]{2,1,0:T(8,128)S(1)}, u32[]{:S(2)}, u32[]{:S(2)}) collective-permute-start(f32[4,128,128]{2,1,0:T(8,128)S(1)} %get-tuple-element.81), channel_id=1, source_target_pairs={{0,64},{64,0},{128,192},{192,128},{1,65},{65,1},{129,193},{193,129... | collective-permute-start | bytes 786440 | tf_op jit(solution)/shard_map/ppermute | solution.py:415

commit v4 on v3

--- a/solution.py
+++ b/solution.py
@@ -22,7 +22,7 @@
     "sums_two": 0.01,
     "cot_two": 0.01,
     "cot_one_base": 0.01,
-    "cot_one": 0.01,
+    "cot_one": 2.0,
     "sums_three": 0.01,
     "finish_base": 0.01,
     "finish": 0.01,
@@ -183,12 +183,11 @@
     for l in range(2):
         total = jnp.zeros((N, N), F32)
         for c in range(4):
-            a = base[c, l]
-            total = total + (co.vol[c] * co.rate[c]) * a
-            u1[c, l] = a - (H * k0s[l]) * (co.rate[c] * u4[c, l])
+            u = base[c, l] - (H * k0s[l]) * (co.rate[c] * u4[c, l])
+            total = total + (co.vol[c] * co.rate[c]) * u
+            u1[c, l] = u
         pk2[l] = total
-        pk2[2 + l] = sums[2 + l]
-        pk2[4 + l] = sums[l]
+        pk2[2 + l] = sums[l]
     pk2[core] = pk2[core] + extra
     for c in range(4):
         edge = u1[c, core] + halo[c]
@@ -243,19 +242,17 @@
     fout, fin = facing(co, vel, core)
     for l in range(2):
         k0 = k0s[l]
-        a0 = pk2[4 + l] + got[4 + l]
-        c0 = pk2[2 + l] + got[2 + l]
+        a0 = pk2[2 + l] + got[2 + l]
         theta1 = th[l] + H * (k0 * a0)
         k1 = k0s[2 + l] * jnp.exp(-theta1)
         k01[l] = k0
         k01[2 + l] = k1
-        a1 = (pk2[l] + got[l]) - (H * k0) * c0
+        a1 = pk2[l] + got[l]
         theta2 = 0.75 * th[l] + 0.25 * (theta1 + H * (k1 * a1))
         k2 = k0s[2 + l] * jnp.exp(-theta2)
         k2s[l] = k2
         sums[l] = a0
         sums[2 + l] = a1
-        sums[4 + l] = c0
         for c in range(4):
             p = p4[c, l]
             l2[c, l] = base[c, l] + (2.0 / 3.0 * H) * ((co.rate[c] * k2) * (q4[c, l] - p))
@@ -264,7 +261,7 @@
         hi[(c + 2) % 4] = fin[c] * l2[c, 1 - core]
 
 
-def cot_one_base(core_ref, coef, l2, hin, k01, vel, q4, u1, u4, l1, part):
+def cot_one_base(core_ref, coef, l2, hin, k01, vel, q4, u1, u4, after, l1, part):
     core = core_ref[0]
     co = Coef(coef)
     for c in range(4):
@@ -295,7 +292,7 @@
         t2s[l] = t2
         t2s[2 + l] = sums[l]
         t2s[4 + l] = sums[2 + l]
-        t2s[6 + l] = push * sums[4 + l]
+        t2s[6 + l] = push
         for c in range(4):
             l1[c, l] = l1k[c, l] + (co.rate[c] * co.vol[c]) * push
     for c in range(4):
@@ -303,7 +300,7 @@
         hi[(c + 2) % 4] = fin[c] * l1[c, 1 - core]
 
 
-def sums_three(core_ref, coef, base, part, hout, u4, l1, pk4):
+def sums_three(core_ref, coef, base, part, sums, hout, u4, l1, pk4):
     core = core_ref[0]
     co = Coef(coef)
     edge = part[2 + core]
@@ -314,6 +311,7 @@
         edge = edge - (co.rate[c] * more) * u4[c, core]
     for l in range(2):
         pk4[l] = part[l]
+        pk4[4 + l] = sums[2 + l]
     pk4[3 - core] = part[3 - core]
     pk4[2 + core] = edge
 
@@ -323,7 +321,8 @@
         t2 = t2s[l]
         t1 = (-0.25 * H) * k01[2 + l] * ((pk4[l] + got[l]) + t2 * t2s[4 + l])
         both = 0.25 * t2 + t1
-        zero = (pk4[2 + l] + got[2 + l]) + both * t2s[2 + l] - t2s[6 + l]
+        square = pk4[4 + l] + got[4 + l]
+        zero = (pk4[2 + l] + got[2 + l]) + both * t2s[2 + l] - t2s[6 + l] * square
         tsum[l] = t2 + t1 - H * (k01[l] * zero)
         mixed[l] = both
 
@@ -444,7 +443,7 @@
     k0s, th = call(kappa_zero, [layers(4), layers(2)], (core,), (pk1, gpk1, label))
     u1, ho1, hi1, pk2 = call(
         state_one,
-        [eight, layers(4), layers(4), layers(6)],
+        [eight, layers(4), layers(4), layers(4)],
         (core,),
         (coef, abase, hu0, velocity, csums, k0s, u4, pbase),
     )
@@ -457,7 +456,7 @@
     (l2start,) = call(cot_start, [eight], (core,), (p4, pbase, hp))
     l2, ho2, hi2, k01, k2s, sums = call(
         cot_two,
-        [eight, layers(4), layers(4), layers(4), layers(2), layers(6)],
+        [eight, layers(4), layers(4), layers(4), layers(2), layers(4)],
         (core,),
         (coef, pk2, gpk2, k0s, th, p4, q4, l2start, velocity),
     )
@@ -466,9 +465,11 @@
     (pk3,) = call(sums_two, [layers(2)], (core,), (part2, wout, hu1, k01))
     gpk3 = across(pk3)
     l1base, part1 = call(
-        cot_one_base, [eight, layers(4)], (core,), (coef, l2, il2, k01, velocity, q4, u1, u4)
-    )
-    l1k, pk4 = call(sums_three, [eight, layers(4)], (core,), (coef, l1base, part1, hl2, u4))
+        cot_one_base, [eight, layers(4)], (core,), (coef, l2, il2, k01, velocity, q4, u1, u4, pk3)
+    )
+    l1k, pk4 = call(
+        sums_three, [eight, layers(6)], (core,), (coef, l1base, part1, csums, hl2, u4)
+    )
     gpk4 = across(pk4)
     l1, ho3, hi3, t2s = call(
         cot_one,

time: 67.4 us -> 68.9 us (1.022)
  starting transfers between devices: 32.7 us -> 37.4 us
  waiting for transfers between devices: 24 us -> 20.6 us
    ppermute x7, starting transfers between devices: 15.3 us -> 19.7 us  [shards(): inner = lambda x: lax.ppermute(x, 'size', swap)]
    ppermute x5, waiting for transfers between devices: 10.7 us -> 7.96 us  [shards(): outer = lambda x: lax.ppermute(x, ('size', 'gz'), face)]
    ppermute x4, waiting for transfers between devices: 12 us -> 10.3 us  [shards(): across = lambda x: lax.ppermute(x, 'size', far)]
    ppermute x7, waiting for transfers between devices: 1.36 us -> 2.37 us  [shards(): inner = lambda x: lax.ppermute(x, 'size', swap)]
    unnamed x18 -> x22, local copies, waits for them, and re-layouts: 2.76 us -> 2.96 us
where the time goes in v4:
time: 68.9 us; the launch traced here: 68.6 us
  starting transfers between devices  37.4 us (54%)
  waiting for transfers between devices  20.6 us (30%)
  Pallas kernels  6.66 us (10%)
  local copies, waits for them, and re-layouts  2.96 us (4%)
  between operations  0.89 us (1%)
    ppermute x7, starting transfers between devices, shards(): inner = lambda x: lax.ppermute(x, 'size', swap)  19.7 us
    ppermute x5, starting transfers between devices, shards(): outer = lambda x: lax.ppermute(x, ('size', 'gz'), face)  11.3 us
    ppermute x4, waiting for transfers between devices, shards(): across = lambda x: lax.ppermute(x, 'size', far)  10.3 us
    ppermute x5, waiting for transfers between devices, shards(): outer = lambda x: lax.ppermute(x, ('size', 'gz'), face)  7.96 us
    pallas_call x19, Pallas kernels, call(): pl.pallas_call(body, out_shape=[jax.ShapeDtypeStruct(s, F32) for s in out...  6.66 us
    ppermute x4, starting transfers between devices, shards(): across = lambda x: lax.ppermute(x, 'size', far)  6.5 us
    unnamed x22, local copies, waits for them, and re-layouts  2.96 us
    ppermute x7, waiting for transfers between devices, shards(): inner = lambda x: lax.ppermute(x, 'size', swap)  2.37 us
  transfers between devices with their start and end apart: 16, of which 8 were waited for; matrix products, arithmetic and copies ran while one was open for 0% of the time, Pallas kernels for 8%

profile of v4, /device:TPU:129, one launch (start us, length us, event | category | flops | bytes accessed | tf_op | source)
XLA Modules:
  0.0 68.6 jit_solution(308833290172292)
XLA Ops:
  0.6 0.0 copy-start.1
  0.7 1.0 %copy-done.1 = f32[2,4,128,128]{3,2,1,0:T(8,128)S(1)} copy-done((f32[2,4,128,128]{3,2,1,0:T(8,128)S(1)}, f32[2,4,128,128]{3,2,1,0:T(8,128)}, u32[]{:S(2)}) %copy-start.1) | copy-done | bytes 524312
  1.7 0.0 copy-start.3
  1.7 1.0 %copy-done.3 = f32[2,4,128,128]{3,2,1,0:T(8,128)S(1)} copy-done((f32[2,4,128,128]{3,2,1,0:T(8,128)S(1)}, f32[2,4,128,128]{3,2,1,0:T(8,128)}, u32[]{:S(2)}) %copy-start.3) | copy-done | bytes 524312
  2.7 0.0 copy-start.9
  2.8 0.8 %collective-permute-start.1 = (f32[10,128,128]{2,1,0:T(8,128)S(1)}, f32[10,128,128]{2,1,0:T(8,128)S(1)}, u32[]{:S(2)}, u32[]{:S(2)}) collective-permute-start(f32[10,128,128]{2,1,0:T(8,128)S(1)} %send_cot.1), channel_id=1, source_target_pairs={{0,64},{64,0},{128,192},{192,128},{1,65},{65,1},{129,193},{193,129... | collective-permute-start | bytes 1966088 | tf_op jit(solution)/shard_map/ppermute | solution.py:414
  3.6 0.2 copy-done.5
  3.8 0.2 copy-done.6
  3.9 0.0 copy-done.7
  3.9 0.0 copy-done.8
  3.9 0.0 copy-done.9
  3.9 0.6 send_state.1
  4.6 0.8 %collective-permute-start = (f32[9,128,128]{2,1,0:T(8,128)S(1)}, f32[9,128,128]{2,1,0:T(8,128)S(1)}, u32[]{:S(2)}, u32[]{:S(2)}) collective-permute-start(f32[9,128,128]{2,1,0:T(8,128)S(1)} %get-tuple-element.45), channel_id=1, source_target_pairs={{0,64},{64,0},{128,192},{192,128},{1,65},{65,1},{129,193},{193,129... | collective-permute-start | bytes 1769480 | tf_op jit(solution)/shard_map/ppermute | solution.py:414
  5.4 1.6 %collective-permute-done.got = f32[9,128,128]{2,1,0:T(8,128)S(1)} collective-permute-done((f32[9,128,128]{2,1,0:T(8,128)S(1)}, f32[9,128,128]{2,1,0:T(8,128)S(1)}, u32[]{:S(2)}, u32[]{:S(2)}) %collective-permute-start) | collective-permute-done | bytes 589856 | tf_op jit(solution)/shard_map/ppermute | solution.py:414
  7.0 0.1 sums_zero.1
  7.1 2.8 %collective-permute-start.3 = (f32[2,128,128]{2,1,0:T(8,128)S(1)}, f32[2,128,128]{2,1,0:T(8,128)S(1)}, u32[]{:S(2)}, u32[]{:S(2)}) collective-permute-start(f32[2,128,128]{2,1,0:T(8,128)S(1)} %get-tuple-element.53.pk1), channel_id=1, source_target_pairs={{0,128},{128,0},{64,192},{192,64},{1,129},{129,1},{65,193},{193,65... | collective-permute-start | bytes 393224 | tf_op jit(solution)/shard_map/ppermute | solution.py:415
  10.0 2.7 %collective-permute-start.2 = (f32[4,128,128]{2,1,0:T(8,128)S(1)}, f32[4,128,128]{2,1,0:T(8,128)S(1)}, u32[]{:S(2)}, u32[]{:S(2)}) collective-permute-start(f32[4,128,128]{2,1,0:T(8,128)S(1)} %get-tuple-element.51), channel_id=1, source_target_pairs={{64,1},{1,64},{192,129},{129,192},{65,2},{2,65},{193,130},{130,193... | collective-permute-start | bytes 786440 | tf_op jit(solution)/shard_map/ppermute | solution.py:416
  12.7 0.0 collective-permute-done.1.got
  12.7 0.0 copy-done.4
  12.7 0.0 copy-done
  12.8 0.0 copy-done.2
  12.8 0.5 cot_base.1
  13.3 2.8 %collective-permute-start.5 = (f32[4,128,128]{2,1,0:T(8,128)S(1)}, f32[4,128,128]{2,1,0:T(8,128)S(1)}, u32[]{:S(2)}, u32[]{:S(2)}) collective-permute-start(f32[4,128,128]{2,1,0:T(8,128)S(1)} %get-tuple-element.58), channel_id=1, source_target_pairs={{64,1},{1,64},{192,129},{129,192},{65,2},{2,65},{193,130},{130,193... | collective-permute-start | bytes 786440 | tf_op jit(solution)/shard_map/ppermute | solution.py:416
  16.1 0.0 copy-start.10
  16.1 0.4 step_base.1.base
  16.5 0.0 collective-permute-done.3.got
  16.5 0.5 copy-done.10
  17.0 0.1 kappa_zero.1
  17.1 2.7 %collective-permute-done.2.hout = f32[4,128,128]{2,1,0:T(8,128)S(1)} collective-permute-done((f32[4,128,128]{2,1,0:T(8,128)S(1)}, f32[4,128,128]{2,1,0:T(8,128)S(1)}, u32[]{:S(2)}, u32[]{:S(2)}) %collective-permute-start.2) | collective-permute-done | bytes 262176 | tf_op jit(solution)/shard_map/ppermute | solution.py:416
  19.8 0.2 state_one.1
  20.0 1.6 %collective-permute-start.4 = (f32[4,128,128]{2,1,0:T(8,128)S(1)}, f32[4,128,128]{2,1,0:T(8,128)S(1)}, u32[]{:S(2)}, u32[]{:S(2)}) collective-permute-start(f32[4,128,128]{2,1,0:T(8,128)S(1)} %get-tuple-element.56.pk2), channel_id=1, source_target_pairs={{0,128},{128,0},{64,192},{192,64},{1,129},{129,1},{65,193},{193,65... | collective-permute-start | bytes 786440 | tf_op jit(solution)/shard_map/ppermute | solution.py:415
  21.7 1.8 %collective-permute-start.6 = (f32[4,128,128]{2,1,0:T(8,128)S(1)}, f32[4,128,128]{2,1,0:T(8,128)S(1)}, u32[]{:S(2)}, u32[]{:S(2)}) collective-permute-start(f32[4,128,128]{2,1,0:T(8,128)S(1)} %get-tuple-element.61), channel_id=1, source_target_pairs={{0,64},{64,0},{128,192},{192,128},{1,65},{65,1},{129,193},{193,129... | collective-permute-start | bytes 786440 | tf_op jit(solution)/shard_map/ppermute | solution.py:414
  23.5 1.9 %collective-permute-start.7 = (f32[4,128,128]{2,1,0:T(8,128)S(1)}, f32[4,128,128]{2,1,0:T(8,128)S(1)}, u32[]{:S(2)}, u32[]{:S(2)}) collective-permute-start(f32[4,128,128]{2,1,0:T(8,128)S(1)} %get-tuple-element.64), channel_id=1, source_target_pairs={{64,1},{1,64},{192,129},{129,192},{65,2},{2,65},{193,130},{130,193... | collective-permute-start | bytes 786440 | tf_op jit(solution)/shard_map/ppermute | solution.py:416
  25.4 0.4 collective-permute-done.5.hout
  25.8 0.1 cot_start.1.base
  25.9 7.5 %collective-permute-done.4.got = f32[4,128,128]{2,1,0:T(8,128)S(1)} collective-permute-done((f32[4,128,128]{2,1,0:T(8,128)S(1)}, f32[4,128,128]{2,1,0:T(8,128)S(1)}, u32[]{:S(2)}, u32[]{:S(2)}) %collective-permute-start.4) | collective-permute-done | bytes 262176 | tf_op jit(solution)/shard_map/ppermute | solution.py:415
  33.4 0.3 cot_two.1
  33.7 3.2 %collective-permute-start.9 = (f32[4,128,128]{2,1,0:T(8,128)S(1)}, f32[4,128,128]{2,1,0:T(8,128)S(1)}, u32[]{:S(2)}, u32[]{:S(2)}) collective-permute-start(f32[4,128,128]{2,1,0:T(8,128)S(1)} %get-tuple-element.68), channel_id=1, source_target_pairs={{0,64},{64,0},{128,192},{192,128},{1,65},{65,1},{129,193},{193,129... | collective-permute-start | bytes 786440 | tf_op jit(solution)/shard_map/ppermute | solution.py:414
  36.9 1.9 %collective-permute-start.10 = (f32[4,128,128]{2,1,0:T(8,128)S(1)}, f32[4,128,128]{2,1,0:T(8,128)S(1)}, u32[]{:S(2)}, u32[]{:S(2)}) collective-permute-start(f32[4,128,128]{2,1,0:T(8,128)S(1)} %get-tuple-element.71), channel_id=1, source_target_pairs={{64,1},{1,64},{192,129},{129,192},{65,2},{2,65},{193,130},{130,193... | collective-permute-start | bytes 786440 | tf_op jit(solution)/shard_map/ppermute | solution.py:416
  38.8 0.0 collective-permute-done.6.hin
  38.8 0.7 %state_two.1 = (f32[4,128,128]{2,1,0:T(8,128)S(1)}, f32[4,128,128]{2,1,0:T(8,128)S(1)}) custom-call(s32[1]{0:T(128)} %bitcast.core_ref, f32[16,128]{1,0:T(8,128)S(1)} %get-tuple-element.46.coef, f32[4,2,128,128]{3,2,1,0:T(8,128)S(1)} %get-tuple-element.49.u4, f32[4,2,128,128]{3,2,1,0:T(8,128)S(1)} %get-tuple-element.60.u1, ...), custom_call_target="tpu_custom_call" | custom-call | flops 10000000 | bytes 2629632 | tf_op jit(solution)/shard_map/state_two/pallas_call | solution.py:391
  39.5 0.0 collective-permute-done.7.hout
  39.6 0.1 sums_two.1.after.pk3
  39.6 0.7 %collective-permute-start.8 = (f32[2,128,128]{2,1,0:T(8,128)S(1)}, f32[2,128,128]{2,1,0:T(8,128)S(1)}, u32[]{:S(2)}, u32[]{:S(2)}) collective-permute-start(f32[2,128,128]{2,1,0:T(8,128)S(1)} %sums_two.1.after.pk3), channel_id=1, source_target_pairs={{0,128},{128,0},{64,192},{192,64},{1,129},{129,1},{65,193},{193,65... | collective-permute-start | bytes 393224 | tf_op jit(solution)/shard_map/ppermute | solution.py:415
  40.3 0.0 collective-permute-done.9.hin
  40.3 0.8 %cot_one_base.1 = (f32[4,2,128,128]{3,2,1,0:T(8,128)S(1)}, f32[4,128,128]{2,1,0:T(8,128)S(1)}) custom-call(s32[1]{0:T(128)} %bitcast.core_ref, f32[16,128]{1,0:T(8,128)S(1)} %get-tuple-element.46.coef, f32[4,2,128,128]{3,2,1,0:T(8,128)S(1)} %get-tuple-element.59.l2, f32[4,128,128]{2,1,0:T(8,128)S(1)} %collective-permute-done.9.hin, ...), custom_call_target="tpu_custom_call" | custom-call | flops 10000000 | bytes 3022848 | tf_op jit(solution)/shard_map/cot_one_base/pallas_call | solution.py:391
  41.1 4.9 %collective-permute-done.10.hout = f32[4,128,128]{2,1,0:T(8,128)S(1)} collective-permute-done((f32[4,128,128]{2,1,0:T(8,128)S(1)}, f32[4,128,128]{2,1,0:T(8,128)S(1)}, u32[]{:S(2)}, u32[]{:S(2)}) %collective-permute-start.10) | collective-permute-done | bytes 262176 | tf_op jit(solution)/shard_map/ppermute | solution.py:416
  46.0 0.1 sums_three.1
  46.1 1.3 %collective-permute-start.12 = (f32[6,128,128]{2,1,0:T(8,128)S(1)}, f32[6,128,128]{2,1,0:T(8,128)S(1)}, u32[]{:S(2)}, u32[]{:S(2)}) collective-permute-start(f32[6,128,128]{2,1,0:T(8,128)S(1)} %get-tuple-element.75.pk4), channel_id=1, source_target_pairs={{0,128},{128,0},{64,192},{192,64},{1,129},{129,1},{65,193},{193,65... | collective-permute-start | bytes 1179656 | tf_op jit(solution)/shard_map/ppermute | solution.py:415
  47.5 0.0 collective-permute-done.8.got
  47.5 0.2 cot_one.1
  47.6 3.1 %collective-permute-start.11 = (f32[4,128,128]{2,1,0:T(8,128)S(1)}, f32[4,128,128]{2,1,0:T(8,128)S(1)}, u32[]{:S(2)}, u32[]{:S(2)}) collective-permute-start(f32[4,128,128]{2,1,0:T(8,128)S(1)} %get-tuple-element.74), channel_id=1, source_target_pairs={{0,64},{64,0},{128,192},{192,128},{1,65},{65,1},{129,193},{193,129... | collective-permute-start | bytes 786440 | tf_op jit(solution)/shard_map/ppermute | solution.py:414
  50.8 1.9 %collective-permute-start.13 = (f32[4,128,128]{2,1,0:T(8,128)S(1)}, f32[4,128,128]{2,1,0:T(8,128)S(1)}, u32[]{:S(2)}, u32[]{:S(2)}) collective-permute-start(f32[4,128,128]{2,1,0:T(8,128)S(1)} %get-tuple-element.78), channel_id=1, source_target_pairs={{64,1},{1,64},{192,129},{129,192},{65,2},{2,65},{193,130},{130,193... | collective-permute-start | bytes 786440 | tf_op jit(solution)/shard_map/ppermute | solution.py:416
  52.7 2.7 %collective-permute-done.12.got = f32[6,128,128]{2,1,0:T(8,128)S(1)} collective-permute-done((f32[6,128,128]{2,1,0:T(8,128)S(1)}, f32[6,128,128]{2,1,0:T(8,128)S(1)}, u32[]{:S(2)}, u32[]{:S(2)}) %collective-permute-start.12) | collective-permute-done | bytes 393248 | tf_op jit(solution)/shard_map/ppermute | solution.py:415
  55.4 0.1 total_push.1
  55.5 9.6 %collective-permute-start.14 = (f32[2,128,128]{2,1,0:T(8,128)S(1)}, f32[2,128,128]{2,1,0:T(8,128)S(1)}, u32[]{:S(2)}, u32[]{:S(2)}) collective-permute-start(f32[2,128,128]{2,1,0:T(8,128)S(1)} %get-tuple-element.79.tsum), channel_id=1, source_target_pairs={{0,64},{64,0},{128,192},{192,128},{1,65},{65,1},{129,193},{193,129... | collective-permute-start | bytes 393224 | tf_op jit(solution)/shard_map/ppermute | solution.py:414
  65.1 0.0 collective-permute-done.11.hin
  65.1 0.6 finish_base.1.base
  65.7 0.0 collective-permute-done.13.hout
  65.7 0.4 collective-permute-done.14.after.got
  66.1 0.4 collective-permute-start.15
  66.6 0.8 %write_dep.1 = f32[2,4,128,128]{3,2,1,0:T(8,128)} custom-call(s32[1]{0:T(128)} %bitcast.core_ref, f32[16,128]{1,0:T(8,128)S(1)} %get-tuple-element.46.coef, f32[2,128,128]{2,1,0:T(8,128)S(1)} %get-tuple-element.79.tsum, f32[2,128,128]{2,1,0:T(8,128)S(1)} %collective-permute-done.14.after.got, f32[2,4,128,128]{3,2,1,0:T(8,128)S(1)} %copy-done.2), custom_call_target="tpu_custom_call" | custom-call | flops 10000000 | bytes 794624 | tf_op jit(solution)/shard_map/write_dep/pallas_call | solution.py:391
  67.4 0.3 collective-permute-done.15.got
  67.7 0.8 %write_conc.1 = f32[2,4,128,128]{3,2,1,0:T(8,128)} custom-call(s32[1]{0:T(128)} %bitcast.core_ref, f32[4,128,128]{2,1,0:T(8,128)S(1)} %get-tuple-element.80.own, f32[4,128,128]{2,1,0:T(8,128)S(1)} %collective-permute-done.15.got), custom_call_target="tpu_custom_call" | custom-call | flops 10000000 | bytes 524288 | tf_op jit(solution)/shard_map/write_conc/pallas_call | solution.py:391
  (9 shorter events, 0.1 us)
Async XLA Ops:
  0.6 1.0 %copy-start.1 = (f32[2,4,128,128]{3,2,1,0:T(8,128)S(1)}, f32[2,4,128,128]{3,2,1,0:T(8,128)}, u32[]{:S(2)}) copy-start(f32[2,4,128,128]{3,2,1,0:T(8,128)} %q.5) | copy-start | bytes 1572868
  1.7 1.0 %copy-start.3 = (f32[2,4,128,128]{3,2,1,0:T(8,128)S(1)}, f32[2,4,128,128]{3,2,1,0:T(8,128)}, u32[]{:S(2)}) copy-start(f32[2,4,128,128]{3,2,1,0:T(8,128)} %p.3) | copy-start | bytes 1572868
  2.7 1.0 %copy-start.5 = (f32[2,4,128,128]{3,2,1,0:T(8,128)S(1)}, f32[2,4,128,128]{3,2,1,0:T(8,128)}, u32[]{:S(2)}) copy-start(f32[2,4,128,128]{3,2,1,0:T(8,128)} %dep.1) | copy-start | bytes 1572868
  2.7 1.2 %copy-start.6 = (f32[2,4,128,128]{3,2,1,0:T(8,128)S(1)}, f32[2,4,128,128]{3,2,1,0:T(8,128)}, u32[]{:S(2)}) copy-start(f32[2,4,128,128]{3,2,1,0:T(8,128)} %conc.1) | copy-start | bytes 1572868
  2.7 1.2 %copy-start.7 = (f32[2]{0:T(128)S(1)}, f32[2]{0:T(128)}, u32[]{:S(2)}) copy-start(f32[2]{0:T(128)} %dif.1) | copy-start | bytes 28
  2.7 1.2 %copy-start.8 = (f32[2]{0:T(128)S(1)}, f32[2]{0:T(128)}, u32[]{:S(2)}) copy-start(f32[2]{0:T(128)} %rate.1) | copy-start | bytes 28
  2.7 1.2 %copy-start.9 = (f32[2]{0:T(128)S(1)}, f32[2]{0:T(128)}, u32[]{:S(2)}) copy-start(f32[2]{0:T(128)} %vol.1) | copy-start | bytes 28
  2.8 9.9 %collective-permute-start.1 = (f32[10,128,128]{2,1,0:T(8,128)S(1)}, f32[10,128,128]{2,1,0:T(8,128)S(1)}, u32[]{:S(2)}, u32[]{:S(2)}) collective-permute-start(f32[10,128,128]{2,1,0:T(8,128)S(1)} %send_cot.1), channel_id=1, source_target_pairs={{0,64},{64,0},{128,192},{192,128},{1,65},{65,1},{129,193},{193,129... | collective-permute-start | bytes 1966088 | tf_op jit(solution)/shard_map/ppermute | solution.py:414
  3.9 8.8 %copy-start.4 = (f32[2,4,128,128]{3,2,1,0:T(8,128)S(1)}, f32[2,4,128,128]{3,2,1,0:T(8,128)}, u32[]{:S(2)}) copy-start(f32[2,4,128,128]{3,2,1,0:T(8,128)} %p.3) | copy-start | bytes 1572868
  4.6 2.4 %collective-permute-start = (f32[9,128,128]{2,1,0:T(8,128)S(1)}, f32[9,128,128]{2,1,0:T(8,128)S(1)}, u32[]{:S(2)}, u32[]{:S(2)}) collective-permute-start(f32[9,128,128]{2,1,0:T(8,128)S(1)} %get-tuple-element.45), channel_id=1, source_target_pairs={{0,64},{64,0},{128,192},{192,128},{1,65},{65,1},{129,193},{193,129... | collective-permute-start | bytes 1769480 | tf_op jit(solution)/shard_map/ppermute | solution.py:414
  7.0 5.8 %copy-start = (f32[4,128,128]{2,1,0:T(8,128)S(1)}, f32[4,128,128]{2,1,0:T(8,128)}, u32[]{:S(2)}) copy-start(f32[4,128,128]{2,1,0:T(8,128)} %vel.15) | copy-start | bytes 786436
  7.0 5.8 %copy-start.2 = (f32[2,4,128,128]{3,2,1,0:T(8,128)S(1)}, f32[2,4,128,128]{3,2,1,0:T(8,128)}, u32[]{:S(2)}) copy-start(f32[2,4,128,128]{3,2,1,0:T(8,128)} %q.5) | copy-start | bytes 1572868
  7.1 9.4 %collective-permute-start.3 = (f32[2,128,128]{2,1,0:T(8,128)S(1)}, f32[2,128,128]{2,1,0:T(8,128)S(1)}, u32[]{:S(2)}, u32[]{:S(2)}) collective-permute-start(f32[2,128,128]{2,1,0:T(8,128)S(1)} %get-tuple-element.53.pk1), channel_id=1, source_target_pairs={{0,128},{128,0},{64,192},{192,64},{1,129},{129,1},{65,193},{193,65... | collective-permute-start | bytes 393224 | tf_op jit(solution)/shard_map/ppermute | solution.py:415
  10.0 9.8 %collective-permute-start.2 = (f32[4,128,128]{2,1,0:T(8,128)S(1)}, f32[4,128,128]{2,1,0:T(8,128)S(1)}, u32[]{:S(2)}, u32[]{:S(2)}) collective-permute-start(f32[4,128,128]{2,1,0:T(8,128)S(1)} %get-tuple-element.51), channel_id=1, source_target_pairs={{64,1},{1,64},{192,129},{129,192},{65,2},{2,65},{193,130},{130,193... | collective-permute-start | bytes 786440 | tf_op jit(solution)/shard_map/ppermute | solution.py:416
  13.3 12.5 %collective-permute-start.5 = (f32[4,128,128]{2,1,0:T(8,128)S(1)}, f32[4,128,128]{2,1,0:T(8,128)S(1)}, u32[]{:S(2)}, u32[]{:S(2)}) collective-permute-start(f32[4,128,128]{2,1,0:T(8,128)S(1)} %get-tuple-element.58), channel_id=1, source_target_pairs={{64,1},{1,64},{192,129},{129,192},{65,2},{2,65},{193,130},{130,193... | collective-permute-start | bytes 786440 | tf_op jit(solution)/shard_map/ppermute | solution.py:416
  16.1 1.0 %copy-start.10 = (s32[4,128,128]{2,1,0:T(8,128)S(1)}, s32[4,128,128]{2,1,0:T(8,128)}, u32[]{:S(2)}) copy-start(s32[4,128,128]{2,1,0:T(8,128)} %label.1) | copy-start | bytes 786436
  20.0 13.4 %collective-permute-start.4 = (f32[4,128,128]{2,1,0:T(8,128)S(1)}, f32[4,128,128]{2,1,0:T(8,128)S(1)}, u32[]{:S(2)}, u32[]{:S(2)}) collective-permute-start(f32[4,128,128]{2,1,0:T(8,128)S(1)} %get-tuple-element.56.pk2), channel_id=1, source_target_pairs={{0,128},{128,0},{64,192},{192,64},{1,129},{129,1},{65,193},{193,65... | collective-permute-start | bytes 786440 | tf_op jit(solution)/shard_map/ppermute | solution.py:415
  21.7 17.2 %collective-permute-start.6 = (f32[4,128,128]{2,1,0:T(8,128)S(1)}, f32[4,128,128]{2,1,0:T(8,128)S(1)}, u32[]{:S(2)}, u32[]{:S(2)}) collective-permute-start(f32[4,128,128]{2,1,0:T(8,128)S(1)} %get-tuple-element.61), channel_id=1, source_target_pairs={{0,64},{64,0},{128,192},{192,128},{1,65},{65,1},{129,193},{193,129... | collective-permute-start | bytes 786440 | tf_op jit(solution)/shard_map/ppermute | solution.py:414
  23.5 16.1 %collective-permute-start.7 = (f32[4,128,128]{2,1,0:T(8,128)S(1)}, f32[4,128,128]{2,1,0:T(8,128)S(1)}, u32[]{:S(2)}, u32[]{:S(2)}) collective-permute-start(f32[4,128,128]{2,1,0:T(8,128)S(1)} %get-tuple-element.64), channel_id=1, source_target_pairs={{64,1},{1,64},{192,129},{129,192},{65,2},{2,65},{193,130},{130,193... | collective-permute-start | bytes 786440 | tf_op jit(solution)/shard_map/ppermute | solution.py:416
  33.7 6.6 %collective-permute-start.9 = (f32[4,128,128]{2,1,0:T(8,128)S(1)}, f32[4,128,128]{2,1,0:T(8,128)S(1)}, u32[]{:S(2)}, u32[]{:S(2)}) collective-permute-start(f32[4,128,128]{2,1,0:T(8,128)S(1)} %get-tuple-element.68), channel_id=1, source_target_pairs={{0,64},{64,0},{128,192},{192,128},{1,65},{65,1},{129,193},{193,129... | collective-permute-start | bytes 786440 | tf_op jit(solution)/shard_map/ppermute | solution.py:414
  36.9 9.1 %collective-permute-start.10 = (f32[4,128,128]{2,1,0:T(8,128)S(1)}, f32[4,128,128]{2,1,0:T(8,128)S(1)}, u32[]{:S(2)}, u32[]{:S(2)}) collective-permute-start(f32[4,128,128]{2,1,0:T(8,128)S(1)} %get-tuple-element.71), channel_id=1, source_target_pairs={{64,1},{1,64},{192,129},{129,192},{65,2},{2,65},{193,130},{130,193... | collective-permute-start | bytes 786440 | tf_op jit(solution)/shard_map/ppermute | solution.py:416
  39.6 7.8 %collective-permute-start.8 = (f32[2,128,128]{2,1,0:T(8,128)S(1)}, f32[2,128,128]{2,1,0:T(8,128)S(1)}, u32[]{:S(2)}, u32[]{:S(2)}) collective-permute-start(f32[2,128,128]{2,1,0:T(8,128)S(1)} %sums_two.1.after.pk3), channel_id=1, source_target_pairs={{0,128},{128,0},{64,192},{192,64},{1,129},{129,1},{65,193},{193,65... | collective-permute-start | bytes 393224 | tf_op jit(solution)/shard_map/ppermute | solution.py:415
  46.1 9.3 %collective-permute-start.12 = (f32[6,128,128]{2,1,0:T(8,128)S(1)}, f32[6,128,128]{2,1,0:T(8,128)S(1)}, u32[]{:S(2)}, u32[]{:S(2)}) collective-permute-start(f32[6,128,128]{2,1,0:T(8,128)S(1)} %get-tuple-element.75.pk4), channel_id=1, source_target_pairs={{0,128},{128,0},{64,192},{192,64},{1,129},{129,1},{65,193},{193,65... | collective-permute-start | bytes 1179656 | tf_op jit(solution)/shard_map/ppermute | solution.py:415
  47.6 17.4 %collective-permute-start.11 = (f32[4,128,128]{2,1,0:T(8,128)S(1)}, f32[4,128,128]{2,1,0:T(8,128)S(1)}, u32[]{:S(2)}, u32[]{:S(2)}) collective-permute-start(f32[4,128,128]{2,1,0:T(8,128)S(1)} %get-tuple-element.74), channel_id=1, source_target_pairs={{0,64},{64,0},{128,192},{192,128},{1,65},{65,1},{129,193},{193,129... | collective-permute-start | bytes 786440 | tf_op jit(solution)/shard_map/ppermute | solution.py:414
  50.8 14.9 %collective-permute-start.13 = (f32[4,128,128]{2,1,0:T(8,128)S(1)}, f32[4,128,128]{2,1,0:T(8,128)S(1)}, u32[]{:S(2)}, u32[]{:S(2)}) collective-permute-start(f32[4,128,128]{2,1,0:T(8,128)S(1)} %get-tuple-element.78), channel_id=1, source_target_pairs={{64,1},{1,64},{192,129},{129,192},{65,2},{2,65},{193,130},{130,193... | collective-permute-start | bytes 786440 | tf_op jit(solution)/shard_map/ppermute | solution.py:416
  55.5 10.5 %collective-permute-start.14 = (f32[2,128,128]{2,1,0:T(8,128)S(1)}, f32[2,128,128]{2,1,0:T(8,128)S(1)}, u32[]{:S(2)}, u32[]{:S(2)}) collective-permute-start(f32[2,128,128]{2,1,0:T(8,128)S(1)} %get-tuple-element.79.tsum), channel_id=1, source_target_pairs={{0,64},{64,0},{128,192},{192,128},{1,65},{65,1},{129,193},{193,129... | collective-permute-start | bytes 393224 | tf_op jit(solution)/shard_map/ppermute | solution.py:414
  66.1 1.6 %collective-permute-start.15 = (f32[4,128,128]{2,1,0:T(8,128)S(1)}, f32[4,128,128]{2,1,0:T(8,128)S(1)}, u32[]{:S(2)}, u32[]{:S(2)}) collective-permute-start(f32[4,128,128]{2,1,0:T(8,128)S(1)} %get-tuple-element.81), channel_id=1, source_target_pairs={{0,64},{64,0},{128,192},{192,128},{1,65},{65,1},{129,193},{193,129... | collective-permute-start | bytes 786440 | tf_op jit(solution)/shard_map/ppermute | solution.py:414

commit v5 on v3

--- a/solution.py
+++ b/solution.py
@@ -136,7 +136,7 @@
     )
 
 
-def step_base(core_ref, coef, u4, uin, vel, a4):
+def step_base(core_ref, coef, u4, uin, vel, after, a4):
     core = core_ref[0]
     co = Coef(coef)
     _, fin = facing(co, vel, core)
@@ -328,7 +328,7 @@
         mixed[l] = both
 
 
-def finish_base(core_ref, coef, p4, q4, l2, l1, hin, k01, mixed, vel, out):
+def finish_base(core_ref, coef, p4, q4, l2, l1, hin, k01, mixed, vel, out, early):
     core = core_ref[0]
     co = Coef(coef)
     for l in range(2):
@@ -339,15 +339,16 @@
             out[c, l] = (1.0 / 3.0) * p4[c, l] + 0.75 * l2[c, l] + x + H * rest
     for c in range(4):
         out[c, 1 - core] = out[c, 1 - core] + H * hin[c]
-
-
-def finish(core_ref, base, hout, after, own, msg):
-    core = core_ref[0]
-    for c in range(4):
-        dst = own if c < 2 else msg
-        k = 2 * (c % 2)
-        dst[k + 1 - core] = base[c, 1 - core]
-        dst[k + core] = base[c, core] + H * hout[c]
+    for c in range(2):
+        early[c] = out[2 + c, 1 - core]
+
+
+def finish(core_ref, base, hout, after, first, own, late):
+    core = core_ref[0]
+    for c in range(2):
+        own[2 * c + 1 - core] = base[c, 1 - core]
+        own[2 * c + core] = base[c, core] + H * hout[c]
+        late[c] = base[2 + c, core] + H * hout[2 + c]
 
 
 def write_dep(core_ref, coef, tsum, got, q, dep, buf, sem):
@@ -365,16 +366,18 @@
         copy.wait()
 
 
-def write_conc(core_ref, own, got, conc, sem):
-    core = core_ref[0]
+def write_conc(core_ref, own, early, late, conc, sem):
+    core = core_ref[0]
+    there = 2 * (1 - core)
     copies = []
     for c in range(2):
-        for k, (src, half) in enumerate(((own, core), (got, 1 - core))):
-            copies.append(
-                pltpu.make_async_copy(
-                    src.at[pl.ds(2 * c, 2)], conc.at[c, pl.ds(2 * half, 2)], sem.at[2 * c + k]
-                )
-            )
+        pairs = (
+            (own.at[pl.ds(2 * c, 2)], conc.at[c, pl.ds(2 * core, 2)]),
+            (early.at[c], conc.at[c, there + core]),
+            (late.at[c], conc.at[c, there + 1 - core]),
+        )
+        for k, (src, dst) in enumerate(pairs):
+            copies.append(pltpu.make_async_copy(src, dst, sem.at[3 * c + k]))
             copies[-1].start()
     for copy in copies:
         copy.wait()
@@ -436,11 +439,11 @@
     )
     gpk1 = across(pk1)
     hu0 = outer(ho0)
-    (abase,) = call(step_base, [eight], (core,), (coef, u4, uin, velocity))
     p4, q4, pbase, hop = call(
         cot_base, [eight, eight, eight, layers(4)], (core,), (coef, p, q, got1, velocity)
     )
     hp = outer(hop)
+    (abase,) = call(step_base, [eight], (core,), (coef, u4, uin, velocity, pbase))
     k0s, th = call(kappa_zero, [layers(4), layers(2)], (core,), (pk1, gpk1, label))
     u1, ho1, hi1, pk2 = call(
         state_one,
@@ -482,16 +485,19 @@
         total_push, [layers(2), layers(2)], (core,), (pk4, gpk4, k01, t2s)
     )
     tother = inner(tsum)
-    (base,) = call(
-        finish_base, [eight], (core,), (coef, p4, q4, l2, l1, il1, k01, mixed, velocity)
-    )
-    own, msg = call(finish, [layers(4), layers(4)], (core,), (base, hl1, tother))
-    theirs = inner(msg)
+    base, early = call(
+        finish_base, [eight, layers(2)], (core,), (coef, p4, q4, l2, l1, il1, k01, mixed, velocity)
+    )
+    gearly = inner(early)
+    own, late = call(finish, [layers(4), layers(2)], (core,), (base, hl1, tother, gearly))
+    glate = inner(late)
     state = (2, 4, N, N)
     (dep_out,) = call(
         write_dep, [state], (core,), (coef, tsum, tother, q), [state], 4, hbm_out=True
     )
-    (conc_out,) = call(write_conc, [state], (core,), (own, theirs), (), 4, hbm_out=True)
+    (conc_out,) = call(
+        write_conc, [state], (core,), (own, gearly, glate), (), 6, hbm_out=True
+    )
     return conc_out, dep_out
 
 

time: 67.4 us -> 67.5 us (level)
  waiting for transfers between devices: 24 us -> 23 us
    ppermute x7 -> x8, starting transfers between devices: 15.3 us -> 15.9 us  [shards(): inner = lambda x: lax.ppermute(x, 'size', swap)]
    ppermute x7 -> x8, waiting for transfers between devices: 1.36 us -> 1.19 us  [shards(): inner = lambda x: lax.ppermute(x, 'size', swap)]
  transfers between devices with their start and end apart: 16 -> 17, of which waited for: 8 -> 8; matrix products, arithmetic and copies ran while one was open for 0% -> 0% of each run, Pallas kernels for 8% -> 8%
where the time goes in v5:
time: 67.5 us; the launch traced here: 67.1 us
  starting transfers between devices  33.3 us (49%)
  waiting for transfers between devices  23 us (34%)
  Pallas kernels  6.71 us (10%)
  local copies, waits for them, and re-layouts  3.25 us (5%)
  between operations  0.86 us (1%)
    ppermute x8, starting transfers between devices, shards(): inner = lambda x: lax.ppermute(x, 'size', swap)  15.9 us
    ppermute x4, waiting for transfers between devices, shards(): across = lambda x: lax.ppermute(x, 'size', far)  11.8 us
    ppermute x5, starting transfers between devices, shards(): outer = lambda x: lax.ppermute(x, ('size', 'gz'), face)  11.3 us
    ppermute x5, waiting for transfers between devices, shards(): outer = lambda x: lax.ppermute(x, ('size', 'gz'), face)  10 us
    pallas_call x19, Pallas kernels, call(): pl.pallas_call(body, out_shape=[jax.ShapeDtypeStruct(s, F32) for s in out...  6.71 us
    ppermute x4, starting transfers between devices, shards(): across = lambda x: lax.ppermute(x, 'size', far)  6.15 us
    unnamed x18, local copies, waits for them, and re-layouts  3.25 us
  transfers between devices with their start and end apart: 17, of which 8 were waited for; matrix products, arithmetic and copies ran while one was open for 0% of the time, Pallas kernels for 8%

profile of v5, /device:TPU:129, one launch (start us, length us, event | category | flops | bytes accessed | tf_op | source)
XLA Modules:
  0.0 67.1 jit_solution(10089850575455058376)
XLA Ops:
  0.6 0.0 copy-start.5
  0.7 0.0 copy-start.6
  0.7 0.0 copy-start.7
  0.7 0.6 copy-done.5
  1.3 0.0 copy-done.6
  1.3 0.0 copy-done.7
  1.3 1.0 %copy-done.3 = f32[2,4,128,128]{3,2,1,0:T(8,128)S(1)} copy-done((f32[2,4,128,128]{3,2,1,0:T(8,128)S(1)}, f32[2,4,128,128]{3,2,1,0:T(8,128)}, u32[]{:S(2)}) %copy-start.3) | copy-done | bytes 524312
  2.4 1.0 %copy-done.4 = f32[2,4,128,128]{3,2,1,0:T(8,128)S(1)} copy-done((f32[2,4,128,128]{3,2,1,0:T(8,128)S(1)}, f32[2,4,128,128]{3,2,1,0:T(8,128)}, u32[]{:S(2)}) %copy-start.4) | copy-done | bytes 524312
  3.4 0.6 send_state.1
  4.1 0.8 %collective-permute-start = (f32[9,128,128]{2,1,0:T(8,128)S(1)}, f32[9,128,128]{2,1,0:T(8,128)S(1)}, u32[]{:S(2)}, u32[]{:S(2)}) collective-permute-start(f32[9,128,128]{2,1,0:T(8,128)S(1)} %get-tuple-element.47), channel_id=1, source_target_pairs={{0,64},{64,0},{128,192},{192,128},{1,65},{65,1},{129,193},{193,129... | collective-permute-start | bytes 1769480 | tf_op jit(solution)/shard_map/ppermute | solution.py:418
  4.8 0.0 copy-done.1
  4.8 0.0 copy-done.2
  4.9 0.5 collective-permute-start.1
  5.4 1.0 %collective-permute-done.got = f32[9,128,128]{2,1,0:T(8,128)S(1)} collective-permute-done((f32[9,128,128]{2,1,0:T(8,128)S(1)}, f32[9,128,128]{2,1,0:T(8,128)S(1)}, u32[]{:S(2)}, u32[]{:S(2)}) %collective-permute-start) | collective-permute-done | bytes 589856 | tf_op jit(solution)/shard_map/ppermute | solution.py:418
  6.5 0.1 sums_zero.1
  6.6 2.8 %collective-permute-start.3 = (f32[2,128,128]{2,1,0:T(8,128)S(1)}, f32[2,128,128]{2,1,0:T(8,128)S(1)}, u32[]{:S(2)}, u32[]{:S(2)}) collective-permute-start(f32[2,128,128]{2,1,0:T(8,128)S(1)} %get-tuple-element.56.pk1), channel_id=1, source_target_pairs={{0,128},{128,0},{64,192},{192,64},{1,129},{129,1},{65,193},{193,65... | collective-permute-start | bytes 393224 | tf_op jit(solution)/shard_map/ppermute | solution.py:419
  9.4 2.7 %collective-permute-start.2 = (f32[4,128,128]{2,1,0:T(8,128)S(1)}, f32[4,128,128]{2,1,0:T(8,128)S(1)}, u32[]{:S(2)}, u32[]{:S(2)}) collective-permute-start(f32[4,128,128]{2,1,0:T(8,128)S(1)} %get-tuple-element.54), channel_id=1, source_target_pairs={{64,1},{1,64},{192,129},{129,192},{65,2},{2,65},{193,130},{130,193... | collective-permute-start | bytes 786440 | tf_op jit(solution)/shard_map/ppermute | solution.py:420
  12.2 0.0 collective-permute-done.1.got
  12.2 0.0 copy-done
  12.2 0.5 cot_base.1
  12.7 2.8 %collective-permute-start.5 = (f32[4,128,128]{2,1,0:T(8,128)S(1)}, f32[4,128,128]{2,1,0:T(8,128)S(1)}, u32[]{:S(2)}, u32[]{:S(2)}) collective-permute-start(f32[4,128,128]{2,1,0:T(8,128)S(1)} %get-tuple-element.60), channel_id=1, source_target_pairs={{64,1},{1,64},{192,129},{129,192},{65,2},{2,65},{193,130},{130,193... | collective-permute-start | bytes 786440 | tf_op jit(solution)/shard_map/ppermute | solution.py:420
  15.5 0.0 copy-start.8
  15.5 0.4 step_base.1.base
  16.0 0.0 collective-permute-done.3.got
  16.0 0.5 copy-done.8
  16.5 0.1 kappa_zero.1
  16.5 2.7 %collective-permute-done.2.hout = f32[4,128,128]{2,1,0:T(8,128)S(1)} collective-permute-done((f32[4,128,128]{2,1,0:T(8,128)S(1)}, f32[4,128,128]{2,1,0:T(8,128)S(1)}, u32[]{:S(2)}, u32[]{:S(2)}) %collective-permute-start.2) | collective-permute-done | bytes 262176 | tf_op jit(solution)/shard_map/ppermute | solution.py:420
  19.2 0.3 state_one.1
  19.5 1.6 %collective-permute-start.4 = (f32[6,128,128]{2,1,0:T(8,128)S(1)}, f32[6,128,128]{2,1,0:T(8,128)S(1)}, u32[]{:S(2)}, u32[]{:S(2)}) collective-permute-start(f32[6,128,128]{2,1,0:T(8,128)S(1)} %get-tuple-element.58.pk2), channel_id=1, source_target_pairs={{0,128},{128,0},{64,192},{192,64},{1,129},{129,1},{65,193},{193,65... | collective-permute-start | bytes 1179656 | tf_op jit(solution)/shard_map/ppermute | solution.py:419
  21.2 1.8 %collective-permute-start.6 = (f32[4,128,128]{2,1,0:T(8,128)S(1)}, f32[4,128,128]{2,1,0:T(8,128)S(1)}, u32[]{:S(2)}, u32[]{:S(2)}) collective-permute-start(f32[4,128,128]{2,1,0:T(8,128)S(1)} %get-tuple-element.63), channel_id=1, source_target_pairs={{0,64},{64,0},{128,192},{192,128},{1,65},{65,1},{129,193},{193,129... | collective-permute-start | bytes 786440 | tf_op jit(solution)/shard_map/ppermute | solution.py:418
  23.0 1.9 %collective-permute-start.7 = (f32[4,128,128]{2,1,0:T(8,128)S(1)}, f32[4,128,128]{2,1,0:T(8,128)S(1)}, u32[]{:S(2)}, u32[]{:S(2)}) collective-permute-start(f32[4,128,128]{2,1,0:T(8,128)S(1)} %get-tuple-element.66), channel_id=1, source_target_pairs={{64,1},{1,64},{192,129},{129,192},{65,2},{2,65},{193,130},{130,193... | collective-permute-start | bytes 786440 | tf_op jit(solution)/shard_map/ppermute | solution.py:420
  24.9 0.3 collective-permute-done.5.hout
  25.2 0.1 cot_start.1.base
  25.3 11.5 %collective-permute-done.4.got = f32[6,128,128]{2,1,0:T(8,128)S(1)} collective-permute-done((f32[6,128,128]{2,1,0:T(8,128)S(1)}, f32[6,128,128]{2,1,0:T(8,128)S(1)}, u32[]{:S(2)}, u32[]{:S(2)}) %collective-permute-start.4) | collective-permute-done | bytes 393248 | tf_op jit(solution)/shard_map/ppermute | solution.py:419
  36.8 0.3 cot_two.1
  37.1 2.1 %collective-permute-start.9 = (f32[4,128,128]{2,1,0:T(8,128)S(1)}, f32[4,128,128]{2,1,0:T(8,128)S(1)}, u32[]{:S(2)}, u32[]{:S(2)}) collective-permute-start(f32[4,128,128]{2,1,0:T(8,128)S(1)} %get-tuple-element.70), channel_id=1, source_target_pairs={{0,64},{64,0},{128,192},{192,128},{1,65},{65,1},{129,193},{193,129... | collective-permute-start | bytes 786440 | tf_op jit(solution)/shard_map/ppermute | solution.py:418
  39.2 1.9 %collective-permute-start.10 = (f32[4,128,128]{2,1,0:T(8,128)S(1)}, f32[4,128,128]{2,1,0:T(8,128)S(1)}, u32[]{:S(2)}, u32[]{:S(2)}) collective-permute-start(f32[4,128,128]{2,1,0:T(8,128)S(1)} %get-tuple-element.73), channel_id=1, source_target_pairs={{64,1},{1,64},{192,129},{129,192},{65,2},{2,65},{193,130},{130,193... | collective-permute-start | bytes 786440 | tf_op jit(solution)/shard_map/ppermute | solution.py:420
  41.2 0.0 collective-permute-done.6.hin
  41.2 0.7 %state_two.1 = (f32[4,128,128]{2,1,0:T(8,128)S(1)}, f32[4,128,128]{2,1,0:T(8,128)S(1)}) custom-call(s32[1]{0:T(128)} %bitcast.core_ref, f32[16,128]{1,0:T(8,128)S(1)} %get-tuple-element.48.coef, f32[4,2,128,128]{3,2,1,0:T(8,128)S(1)} %get-tuple-element.51.u4, f32[4,2,128,128]{3,2,1,0:T(8,128)S(1)} %get-tuple-element.62.u1, ...), custom_call_target="tpu_custom_call" | custom-call | flops 10000000 | bytes 2629632 | tf_op jit(solution)/shard_map/state_two/pallas_call | solution.py:395
  41.9 0.0 collective-permute-done.7.hout
  41.9 0.1 sums_two.1.pk3
  42.0 0.4 collective-permute-start.8
  42.3 0.0 collective-permute-done.9.hin
  42.3 0.8 %cot_one_base.1 = (f32[4,2,128,128]{3,2,1,0:T(8,128)S(1)}, f32[4,128,128]{2,1,0:T(8,128)S(1)}) custom-call(s32[1]{0:T(128)} %bitcast.core_ref, f32[16,128]{1,0:T(8,128)S(1)} %get-tuple-element.48.coef, f32[4,2,128,128]{3,2,1,0:T(8,128)S(1)} %get-tuple-element.61.l2, f32[4,128,128]{2,1,0:T(8,128)S(1)} %collective-permute-done.9.hin, ...), custom_call_target="tpu_custom_call" | custom-call | flops 10000000 | bytes 2891776 | tf_op jit(solution)/shard_map/cot_one_base/pallas_call | solution.py:395
  43.1 5.3 %collective-permute-done.10.hout = f32[4,128,128]{2,1,0:T(8,128)S(1)} collective-permute-done((f32[4,128,128]{2,1,0:T(8,128)S(1)}, f32[4,128,128]{2,1,0:T(8,128)S(1)}, u32[]{:S(2)}, u32[]{:S(2)}) %collective-permute-start.10) | collective-permute-done | bytes 262176 | tf_op jit(solution)/shard_map/ppermute | solution.py:420
  48.4 0.1 sums_three.1
  48.5 1.3 %collective-permute-start.12 = (f32[4,128,128]{2,1,0:T(8,128)S(1)}, f32[4,128,128]{2,1,0:T(8,128)S(1)}, u32[]{:S(2)}, u32[]{:S(2)}) collective-permute-start(f32[4,128,128]{2,1,0:T(8,128)S(1)} %get-tuple-element.77.pk4), channel_id=1, source_target_pairs={{0,128},{128,0},{64,192},{192,64},{1,129},{129,1},{65,193},{193,65... | collective-permute-start | bytes 786440 | tf_op jit(solution)/shard_map/ppermute | solution.py:419
  49.7 0.0 collective-permute-done.8.got
  49.7 0.2 cot_one.1
  49.9 3.2 %collective-permute-start.11 = (f32[4,128,128]{2,1,0:T(8,128)S(1)}, f32[4,128,128]{2,1,0:T(8,128)S(1)}, u32[]{:S(2)}, u32[]{:S(2)}) collective-permute-start(f32[4,128,128]{2,1,0:T(8,128)S(1)} %get-tuple-element.76), channel_id=1, source_target_pairs={{0,64},{64,0},{128,192},{192,128},{1,65},{65,1},{129,193},{193,129... | collective-permute-start | bytes 786440 | tf_op jit(solution)/shard_map/ppermute | solution.py:418
  53.1 1.9 %collective-permute-start.13 = (f32[4,128,128]{2,1,0:T(8,128)S(1)}, f32[4,128,128]{2,1,0:T(8,128)S(1)}, u32[]{:S(2)}, u32[]{:S(2)}) collective-permute-start(f32[4,128,128]{2,1,0:T(8,128)S(1)} %get-tuple-element.81), channel_id=1, source_target_pairs={{64,1},{1,64},{192,129},{129,192},{65,2},{2,65},{193,130},{130,193... | collective-permute-start | bytes 786440 | tf_op jit(solution)/shard_map/ppermute | solution.py:420
  55.0 0.3 collective-permute-done.12.got
  55.3 0.1 total_push.1
  55.4 4.9 %collective-permute-start.14 = (f32[2,128,128]{2,1,0:T(8,128)S(1)}, f32[2,128,128]{2,1,0:T(8,128)S(1)}, u32[]{:S(2)}, u32[]{:S(2)}) collective-permute-start(f32[2,128,128]{2,1,0:T(8,128)S(1)} %get-tuple-element.82.tsum), channel_id=1, source_target_pairs={{0,64},{64,0},{128,192},{192,128},{1,65},{65,1},{129,193},{193,129... | collective-permute-start | bytes 393224 | tf_op jit(solution)/shard_map/ppermute | solution.py:418
  60.3 0.0 collective-permute-done.11.hin
  60.3 0.6 finish_base.1
  60.9 0.1 collective-permute-start.15
  61.0 1.8 %collective-permute-done.13.hout = f32[4,128,128]{2,1,0:T(8,128)S(1)} collective-permute-done((f32[4,128,128]{2,1,0:T(8,128)S(1)}, f32[4,128,128]{2,1,0:T(8,128)S(1)}, u32[]{:S(2)}, u32[]{:S(2)}) %collective-permute-start.13) | collective-permute-done | bytes 262176 | tf_op jit(solution)/shard_map/ppermute | solution.py:420
  62.8 0.0 collective-permute-done.14.after.got
  62.8 0.0 collective-permute-done.15.first.early
  62.8 2.4 %collective-permute-start.16 = (f32[2,128,128]{2,1,0:T(8,128)S(1)}, f32[2,128,128]{2,1,0:T(8,128)S(1)}, u32[]{:S(2)}, u32[]{:S(2)}) collective-permute-start(f32[2,128,128]{2,1,0:T(8,128)S(1)} %get-tuple-element.85), channel_id=1, source_target_pairs={{0,64},{64,0},{128,192},{192,128},{1,65},{65,1},{129,193},{193,129... | collective-permute-start | bytes 393224 | tf_op jit(solution)/shard_map/ppermute | solution.py:418
  65.3 0.8 %write_dep.1 = f32[2,4,128,128]{3,2,1,0:T(8,128)} custom-call(s32[1]{0:T(128)} %bitcast.core_ref, f32[16,128]{1,0:T(8,128)S(1)} %get-tuple-element.48.coef, f32[2,128,128]{2,1,0:T(8,128)S(1)} %get-tuple-element.82.tsum, f32[2,128,128]{2,1,0:T(8,128)S(1)} %collective-permute-done.14.after.got, f32[2,4,128,128]{3,2,1,0:T(8,128)S(1)} %copy-done.1), custom_call_target="tpu_custom_call" | custom-call | flops 10000000 | bytes 794624 | tf_op jit(solution)/shard_map/write_dep/pallas_call | solution.py:395
  66.1 0.1 collective-permute-done.16.late
  66.3 0.8 %write_conc.1 = f32[2,4,128,128]{3,2,1,0:T(8,128)} custom-call(s32[1]{0:T(128)} %bitcast.core_ref, f32[4,128,128]{2,1,0:T(8,128)S(1)} %get-tuple-element.84.own, f32[2,128,128]{2,1,0:T(8,128)S(1)} %collective-permute-done.15.first.early, f32[2,128,128]{2,1,0:T(8,128)S(1)} %collective-permute-done.16.late), custom_call_target="tpu_custom_call" | custom-call | flops 10000000 | bytes 524288 | tf_op jit(solution)/shard_map/write_conc/pallas_call | solution.py:395
  (7 shorter events, 0.1 us)
Async XLA Ops:
  0.6 0.7 copy-start.5
  0.7 0.7 copy-start.6
  0.7 0.7 copy-start.7
  1.3 1.0 %copy-start.3 = (f32[2,4,128,128]{3,2,1,0:T(8,128)S(1)}, f32[2,4,128,128]{3,2,1,0:T(8,128)}, u32[]{:S(2)}) copy-start(f32[2,4,128,128]{3,2,1,0:T(8,128)} %dep.1) | copy-start | bytes 1572868
  2.4 1.0 %copy-start.4 = (f32[2,4,128,128]{3,2,1,0:T(8,128)S(1)}, f32[2,4,128,128]{3,2,1,0:T(8,128)}, u32[]{:S(2)}) copy-start(f32[2,4,128,128]{3,2,1,0:T(8,128)} %conc.1) | copy-start | bytes 1572868
  3.4 1.4 %copy-start.1 = (f32[2,4,128,128]{3,2,1,0:T(8,128)S(1)}, f32[2,4,128,128]{3,2,1,0:T(8,128)}, u32[]{:S(2)}) copy-start(f32[2,4,128,128]{3,2,1,0:T(8,128)} %q.5) | copy-start | bytes 1572868
  3.4 1.4 %copy-start.2 = (f32[2,4,128,128]{3,2,1,0:T(8,128)S(1)}, f32[2,4,128,128]{3,2,1,0:T(8,128)}, u32[]{:S(2)}) copy-start(f32[2,4,128,128]{3,2,1,0:T(8,128)} %p.3) | copy-start | bytes 1572868
  4.1 2.4 %collective-permute-start = (f32[9,128,128]{2,1,0:T(8,128)S(1)}, f32[9,128,128]{2,1,0:T(8,128)S(1)}, u32[]{:S(2)}, u32[]{:S(2)}) collective-permute-start(f32[9,128,128]{2,1,0:T(8,128)S(1)} %get-tuple-element.47), channel_id=1, source_target_pairs={{0,64},{64,0},{128,192},{192,128},{1,65},{65,1},{129,193},{193,129... | collective-permute-start | bytes 1769480 | tf_op jit(solution)/shard_map/ppermute | solution.py:418
  4.9 7.3 %collective-permute-start.1 = (f32[10,128,128]{2,1,0:T(8,128)S(1)}, f32[10,128,128]{2,1,0:T(8,128)S(1)}, u32[]{:S(2)}, u32[]{:S(2)}) collective-permute-start(f32[10,128,128]{2,1,0:T(8,128)S(1)} %send_cot.1), channel_id=1, source_target_pairs={{0,64},{64,0},{128,192},{192,128},{1,65},{65,1},{129,193},{193,129... | collective-permute-start | bytes 1966088 | tf_op jit(solution)/shard_map/ppermute | solution.py:418
  6.5 5.7 %copy-start = (f32[4,128,128]{2,1,0:T(8,128)S(1)}, f32[4,128,128]{2,1,0:T(8,128)}, u32[]{:S(2)}) copy-start(f32[4,128,128]{2,1,0:T(8,128)} %vel.15) | copy-start | bytes 786436
  6.6 9.4 %collective-permute-start.3 = (f32[2,128,128]{2,1,0:T(8,128)S(1)}, f32[2,128,128]{2,1,0:T(8,128)S(1)}, u32[]{:S(2)}, u32[]{:S(2)}) collective-permute-start(f32[2,128,128]{2,1,0:T(8,128)S(1)} %get-tuple-element.56.pk1), channel_id=1, source_target_pairs={{0,128},{128,0},{64,192},{192,64},{1,129},{129,1},{65,193},{193,65... | collective-permute-start | bytes 393224 | tf_op jit(solution)/shard_map/ppermute | solution.py:419
  9.4 9.8 %collective-permute-start.2 = (f32[4,128,128]{2,1,0:T(8,128)S(1)}, f32[4,128,128]{2,1,0:T(8,128)S(1)}, u32[]{:S(2)}, u32[]{:S(2)}) collective-permute-start(f32[4,128,128]{2,1,0:T(8,128)S(1)} %get-tuple-element.54), channel_id=1, source_target_pairs={{64,1},{1,64},{192,129},{129,192},{65,2},{2,65},{193,130},{130,193... | collective-permute-start | bytes 786440 | tf_op jit(solution)/shard_map/ppermute | solution.py:420
  12.7 12.4 %collective-permute-start.5 = (f32[4,128,128]{2,1,0:T(8,128)S(1)}, f32[4,128,128]{2,1,0:T(8,128)S(1)}, u32[]{:S(2)}, u32[]{:S(2)}) collective-permute-start(f32[4,128,128]{2,1,0:T(8,128)S(1)} %get-tuple-element.60), channel_id=1, source_target_pairs={{64,1},{1,64},{192,129},{129,192},{65,2},{2,65},{193,130},{130,193... | collective-permute-start | bytes 786440 | tf_op jit(solution)/shard_map/ppermute | solution.py:420
  15.5 1.0 %copy-start.8 = (s32[4,128,128]{2,1,0:T(8,128)S(1)}, s32[4,128,128]{2,1,0:T(8,128)}, u32[]{:S(2)}) copy-start(s32[4,128,128]{2,1,0:T(8,128)} %label.1) | copy-start | bytes 786436
  19.5 17.3 %collective-permute-start.4 = (f32[6,128,128]{2,1,0:T(8,128)S(1)}, f32[6,128,128]{2,1,0:T(8,128)S(1)}, u32[]{:S(2)}, u32[]{:S(2)}) collective-permute-start(f32[6,128,128]{2,1,0:T(8,128)S(1)} %get-tuple-element.58.pk2), channel_id=1, source_target_pairs={{0,128},{128,0},{64,192},{192,64},{1,129},{129,1},{65,193},{193,65... | collective-permute-start | bytes 1179656 | tf_op jit(solution)/shard_map/ppermute | solution.py:419
  21.2 20.0 %collective-permute-start.6 = (f32[4,128,128]{2,1,0:T(8,128)S(1)}, f32[4,128,128]{2,1,0:T(8,128)S(1)}, u32[]{:S(2)}, u32[]{:S(2)}) collective-permute-start(f32[4,128,128]{2,1,0:T(8,128)S(1)} %get-tuple-element.63), channel_id=1, source_target_pairs={{0,64},{64,0},{128,192},{192,128},{1,65},{65,1},{129,193},{193,129... | collective-permute-start | bytes 786440 | tf_op jit(solution)/shard_map/ppermute | solution.py:418
  23.0 18.9 %collective-permute-start.7 = (f32[4,128,128]{2,1,0:T(8,128)S(1)}, f32[4,128,128]{2,1,0:T(8,128)S(1)}, u32[]{:S(2)}, u32[]{:S(2)}) collective-permute-start(f32[4,128,128]{2,1,0:T(8,128)S(1)} %get-tuple-element.66), channel_id=1, source_target_pairs={{64,1},{1,64},{192,129},{129,192},{65,2},{2,65},{193,130},{130,193... | collective-permute-start | bytes 786440 | tf_op jit(solution)/shard_map/ppermute | solution.py:420
  37.1 5.2 %collective-permute-start.9 = (f32[4,128,128]{2,1,0:T(8,128)S(1)}, f32[4,128,128]{2,1,0:T(8,128)S(1)}, u32[]{:S(2)}, u32[]{:S(2)}) collective-permute-start(f32[4,128,128]{2,1,0:T(8,128)S(1)} %get-tuple-element.70), channel_id=1, source_target_pairs={{0,64},{64,0},{128,192},{192,128},{1,65},{65,1},{129,193},{193,129... | collective-permute-start | bytes 786440 | tf_op jit(solution)/shard_map/ppermute | solution.py:418
  39.2 9.1 %collective-permute-start.10 = (f32[4,128,128]{2,1,0:T(8,128)S(1)}, f32[4,128,128]{2,1,0:T(8,128)S(1)}, u32[]{:S(2)}, u32[]{:S(2)}) collective-permute-start(f32[4,128,128]{2,1,0:T(8,128)S(1)} %get-tuple-element.73), channel_id=1, source_target_pairs={{64,1},{1,64},{192,129},{129,192},{65,2},{2,65},{193,130},{130,193... | collective-permute-start | bytes 786440 | tf_op jit(solution)/shard_map/ppermute | solution.py:420
  42.0 7.8 %collective-permute-start.8 = (f32[2,128,128]{2,1,0:T(8,128)S(1)}, f32[2,128,128]{2,1,0:T(8,128)S(1)}, u32[]{:S(2)}, u32[]{:S(2)}) collective-permute-start(f32[2,128,128]{2,1,0:T(8,128)S(1)} %sums_two.1.pk3), channel_id=1, source_target_pairs={{0,128},{128,0},{64,192},{192,64},{1,129},{129,1},{65,193},{193,65... | collective-permute-start | bytes 393224 | tf_op jit(solution)/shard_map/ppermute | solution.py:419
  48.5 6.8 %collective-permute-start.12 = (f32[4,128,128]{2,1,0:T(8,128)S(1)}, f32[4,128,128]{2,1,0:T(8,128)S(1)}, u32[]{:S(2)}, u32[]{:S(2)}) collective-permute-start(f32[4,128,128]{2,1,0:T(8,128)S(1)} %get-tuple-element.77.pk4), channel_id=1, source_target_pairs={{0,128},{128,0},{64,192},{192,64},{1,129},{129,1},{65,193},{193,65... | collective-permute-start | bytes 786440 | tf_op jit(solution)/shard_map/ppermute | solution.py:419
  49.9 10.4 %collective-permute-start.11 = (f32[4,128,128]{2,1,0:T(8,128)S(1)}, f32[4,128,128]{2,1,0:T(8,128)S(1)}, u32[]{:S(2)}, u32[]{:S(2)}) collective-permute-start(f32[4,128,128]{2,1,0:T(8,128)S(1)} %get-tuple-element.76), channel_id=1, source_target_pairs={{0,64},{64,0},{128,192},{192,128},{1,65},{65,1},{129,193},{193,129... | collective-permute-start | bytes 786440 | tf_op jit(solution)/shard_map/ppermute | solution.py:418
  53.1 9.7 %collective-permute-start.13 = (f32[4,128,128]{2,1,0:T(8,128)S(1)}, f32[4,128,128]{2,1,0:T(8,128)S(1)}, u32[]{:S(2)}, u32[]{:S(2)}) collective-permute-start(f32[4,128,128]{2,1,0:T(8,128)S(1)} %get-tuple-element.81), channel_id=1, source_target_pairs={{64,1},{1,64},{192,129},{129,192},{65,2},{2,65},{193,130},{130,193... | collective-permute-start | bytes 786440 | tf_op jit(solution)/shard_map/ppermute | solution.py:420
  55.4 7.4 %collective-permute-start.14 = (f32[2,128,128]{2,1,0:T(8,128)S(1)}, f32[2,128,128]{2,1,0:T(8,128)S(1)}, u32[]{:S(2)}, u32[]{:S(2)}) collective-permute-start(f32[2,128,128]{2,1,0:T(8,128)S(1)} %get-tuple-element.82.tsum), channel_id=1, source_target_pairs={{0,64},{64,0},{128,192},{192,128},{1,65},{65,1},{129,193},{193,129... | collective-permute-start | bytes 393224 | tf_op jit(solution)/shard_map/ppermute | solution.py:418
  60.9 1.9 %collective-permute-start.15 = (f32[2,128,128]{2,1,0:T(8,128)S(1)}, f32[2,128,128]{2,1,0:T(8,128)S(1)}, u32[]{:S(2)}, u32[]{:S(2)}) collective-permute-start(f32[2,128,128]{2,1,0:T(8,128)S(1)} %get-tuple-element.83), channel_id=1, source_target_pairs={{0,64},{64,0},{128,192},{192,128},{1,65},{65,1},{129,193},{193,129... | collective-permute-start | bytes 393224 | tf_op jit(solution)/shard_map/ppermute | solution.py:418
  62.8 3.4 %collective-permute-start.16 = (f32[2,128,128]{2,1,0:T(8,128)S(1)}, f32[2,128,128]{2,1,0:T(8,128)S(1)}, u32[]{:S(2)}, u32[]{:S(2)}) collective-permute-start(f32[2,128,128]{2,1,0:T(8,128)S(1)} %get-tuple-element.85), channel_id=1, source_target_pairs={{0,64},{64,0},{128,192},{192,128},{1,65},{65,1},{129,193},{193,129... | collective-permute-start | bytes 393224 | tf_op jit(solution)/shard_map/ppermute | solution.py:418
